TPU v7x, 512 devices: a whole 4x8x8 slice. The times are simulated.
512 devices in a mesh: ctx: 32 (over y, x), head: 16 (over z, core).
Axes of the slice: x: 4, y: 8, z: 8, core: 2. Of those that a mesh axis runs over, the one named last changes fastest.
Arguments:
- latent: bfloat16 [40960, 576], P('ctx'), may hold values from -7 to 7
- query: bfloat16 [4096, 36864], P('ctx', 'head'), may hold values from -200 to 200
- grad_out: bfloat16 [4096, 32768], P('ctx', 'head'), may hold values from -6 to 6
- picks: int32 [4096, 32], P('ctx'), may hold values from 0 to 639, as said below
Outputs:
- grad_query: bfloat16 [4096, 36864], P('ctx', 'head')
- grad_latent: float32 [40960, 576], P(('ctx', 'head'))
Inputs may be any that keep to these rules, and one draw needn't show every extreme that they name: `picks`: the 32 blocks of a query are distinct, none past the block of the last query held by the same index of ctx; blocks past a query's own position are padding. The queries of one index of ctx pick exactly 36 distinct blocks together, always including the blocks that hold those queries, and at most 2 of them lie on one index of ctx; every device's pool reaches that bound on some index.
All inputs are finite; a program needn't handle non-finite values.
Results may differ from a plain program's by a relative error of at most 0.0049.
Values may be sent and summed in bfloat16 or wider, within the bound.
No kernel may reach another device: no remote copies, remote signals or barrier semaphores. Data moves between devices by JAX's collectives and lax.ppermute only.
A program may use at most 128 MiB of HBM per device.

v0:
```python
import jax
import jax.numpy as jnp
from jax import lax
from jax.sharding import PartitionSpec as P

LAT = 512
BLOCK = 64
POOL = 36


score_scale = 192.0 ** (-0.5)


def owner_total(returned, asked_ids, per_owner, columns):
    blocks = returned.reshape(-1, BLOCK, columns)
    summed = (
        jnp.zeros((per_owner, BLOCK, columns), jnp.float32).at[asked_ids.reshape(-1)].add(blocks)
    )
    return summed.reshape(per_owner * BLOCK, columns)


def local(latent, query, grad_out, picks):
    n_ctx = lax.axis_size("ctx")
    ctx_index = lax.axis_index("ctx")
    ctx_rows, key_width = latent.shape
    per_owner = ctx_rows // BLOCK
    all_blocks = per_owner * n_ctx
    query_count = query.shape[0]
    local_heads = grad_out.shape[1] // LAT
    capacity = min(per_owner, max(2, 2 * POOL // n_ctx))
    slot_rows = capacity * BLOCK
    chosen = jnp.zeros((all_blocks,), jnp.int32).at[picks.reshape(-1)].max(1) > 0
    present = chosen.reshape(n_ctx, per_owner)
    slot_rank = jnp.cumsum(present.astype(jnp.int32), axis=1) - 1
    slot_hit = present[:, :, None] & (
        slot_rank[:, :, None] == jnp.arange(capacity, dtype=jnp.int32)[None, None, :]
    )
    local_ids = jnp.arange(per_owner, dtype=jnp.int32)
    wanted = jnp.sum(slot_hit.astype(jnp.int32) * local_ids[None, :, None], axis=1)
    filled = jnp.any(slot_hit, axis=1)
    asked_ids = lax.all_to_all(wanted, "ctx", split_axis=0, concat_axis=0, tiled=True)
    own_blocks = latent.reshape(per_owner, BLOCK, key_width)
    outgoing = jnp.take(own_blocks, asked_ids, axis=0).reshape(n_ctx, slot_rows, key_width)
    arrived = lax.all_to_all(outgoing, "ctx", split_axis=0, concat_axis=0, tiled=True)
    flat_filled = filled.reshape(-1)
    slot_order = jnp.cumsum(flat_filled.astype(jnp.int32)) - 1
    union_place = (
        flat_filled[None, :] & (slot_order[None, :] == jnp.arange(POOL, dtype=jnp.int32)[:, None])
    ).astype(jnp.int32)
    source_slot = jnp.sum(
        union_place * jnp.arange(n_ctx * capacity, dtype=jnp.int32)[None, :], axis=1
    )
    global_ids = (jnp.arange(n_ctx, dtype=jnp.int32)[:, None] * per_owner + wanted).reshape(-1)
    union_ids = jnp.sum(union_place * global_ids[None, :], axis=1)
    union_keys = jnp.take(
        arrived.reshape(n_ctx * capacity, BLOCK, key_width), source_slot, axis=0
    ).reshape(POOL * BLOCK, key_width)
    picked = jnp.any(picks[:, :, None] == union_ids[None, None, :], axis=1)
    key_pos = (union_ids[:, None] * BLOCK + jnp.arange(BLOCK, dtype=jnp.int32)[None, :]).reshape(-1)
    first_pos = (ctx_rows - query_count) * n_ctx + ctx_index * query_count
    query_pos = first_pos + jnp.arange(query_count, dtype=jnp.int32)
    allowed = jnp.repeat(picked, BLOCK, axis=1) & (key_pos[None, :] <= query_pos[:, None])
    query_heads = query.reshape(query_count, local_heads, key_width)
    grad_heads = grad_out.reshape(query_count, local_heads, LAT)
    contract = (((2,), (1,)), ((), ()))
    scores = (
        lax.dot_general(query_heads, union_keys, contract, preferred_element_type=jnp.float32)
        * score_scale
    )
    masked = jnp.where(allowed[:, None, :], scores, -jnp.inf)
    row_max = jnp.max(masked, axis=2, keepdims=True)
    exponent = jnp.exp(masked - row_max)
    attn_probs = exponent / jnp.sum(exponent, axis=2, keepdims=True)
    probs_low = attn_probs.astype(jnp.bfloat16)
    prob_grad = lax.dot_general(
        grad_heads, union_keys[:, :LAT], contract, preferred_element_type=jnp.float32
    )
    row_delta = jnp.sum(attn_probs * prob_grad, axis=2, keepdims=True)
    dscore = (attn_probs * (prob_grad - row_delta)).astype(jnp.bfloat16)
    leading = (((0, 1), (0, 1)), ((), ()))
    key_grad = (
        lax.dot_general(dscore, query_heads, leading, preferred_element_type=jnp.float32)
        * score_scale
    )
    value_grad = lax.dot_general(probs_low, grad_heads, leading, preferred_element_type=jnp.float32)
    key_grad = jnp.concatenate([key_grad[:, :LAT] + value_grad, key_grad[:, LAT:]], axis=1)
    slot_grad = jnp.take(
        key_grad.reshape(POOL, BLOCK, key_width), jnp.clip(slot_order, 0, POOL - 1), axis=0
    )
    slot_grad = jnp.where(flat_filled[:, None, None], slot_grad, 0.0).reshape(
        n_ctx, capacity, BLOCK, key_width
    )
    row_contract = (((2,), (0,)), ((), ()))
    query_grad = (
        lax.dot_general(dscore, union_keys, row_contract, preferred_element_type=jnp.float32)
        * score_scale
    ).astype(jnp.bfloat16)
    query_grad = query_grad.reshape(query_count, local_heads * key_width)
    returned = lax.all_to_all(slot_grad, "ctx", split_axis=0, concat_axis=0, tiled=True)
    owner_grad = owner_total(returned, asked_ids, per_owner, key_width)
    grad_latent = lax.psum_scatter(owner_grad, "head", scatter_dimension=0, tiled=True)
    return (query_grad, grad_latent)


def solution(mesh):
    return jax.shard_map(
        local,
        mesh=mesh,
        in_specs=(P("ctx", None), P("ctx", "head"), P("ctx", "head"), P("ctx", None)),
        out_specs=(P("ctx", "head"), P(("ctx", "head"), None)),
        check_vma=False,
    )
```

profile of v0, /device:TPU:1, one launch (start us, length us, event | category | flops | bytes accessed | tf_op | source)
XLA Modules:
  0.0 590.7 jit_solution(11091277297900550533)
XLA Ops:
  8.1 28.8 %scatter_custom_fusion = s32[640]{0:T(1024)S(1)} fusion(s32[4096]{0:T(1024)S(1)} %bitcast.76, s32[4096]{0:T(1024)S(1)} %broadcast.254, s32[]{:T(128)} %constant.30.clone.1), kind=kCustom, calls=%fused_computation.56 | custom fusion | flops 4096 | bytes 2564 | tf_op jit(solution)/shard_map/scatter-max | solution.py:32
  38.2 10.5 %all-to-all-start = ((s32[32,1,2]{2,1,0:T(1,128)}), s32[32,1,2]{2,1,0:T(1,128)S(1)}, u32[]{:S(2)}, u32[]{:S(2)}) async-start(s32[32,1,2]{2,1,0:T(1,128)} %copy.92), calls=%async_computation | async-start | bytes 32768 | tf_op jit(solution)/shard_map/all_to_all | solution.py:41
  48.7 1.9 copy.95
  50.6 6.6 %all-to-all-done = s32[32,1,2]{2,1,0:T(1,128)S(1)} async-done(((s32[32,1,2]{2,1,0:T(1,128)}), s32[32,1,2]{2,1,0:T(1,128)S(1)}, u32[]{:S(2)}, u32[]{:S(2)}) %all-to-all-start) | async-done | bytes 288 | tf_op jit(solution)/shard_map/all_to_all | solution.py:41
  57.8 3.5 gather_fusion
  61.3 6.1 %bitcast_select_fusion = bf16[32,128,576]{2,1,0:T(8,128)(2,1)} fusion(pred[32,128]{1,0:T(8,128)(4,1)S(1)} %broadcast_in_dim.98, bf16[32,128,576]{2,1,0:T(8,128)(2,1)} %bitcast.68), kind=kLoop, calls=%fused_computation.10 | loop fusion | flops 2359296 | bytes 9441280 | tf_op jit(solution)/shard_map/jit(_take)/select_n | solution.py:43
  67.4 7.6 %copy.98 = bf16[32,128,576]{1,2,0:T(8,128)(2,1)} copy(bf16[32,128,576]{2,1,0:T(8,128)(2,1)} %bitcast_select_fusion) | data formatting | bytes 9437184 | tf_op jit(solution)/shard_map/jit(_take)/select_n | solution.py:43
  75.0 5.2 all-to-all-start.1
  83.6 1.0 copy.126
  85.1 1.1 bitcast_and_fusion
  87.4 96.1 %all-to-all-done.1 = bf16[32,128,576]{1,2,0:T(8,128)(2,1)} async-done(((bf16[32,128,576]{1,2,0:T(8,128)(2,1)}), bf16[32,128,576]{1,2,0:T(8,128)(2,1)}, u32[]{:S(2)}, u32[]{:S(2)}) %all-to-all-start.1) | async-done | bytes 4718624 | tf_op jit(solution)/shard_map/all_to_all | solution.py:44
  183.5 7.6 %copy.99 = bf16[32,128,576]{2,1,0:T(8,128)(2,1)} copy(bf16[32,128,576]{1,2,0:T(8,128)(2,1)} %all-to-all-done.1) | data formatting | bytes 9437184 | tf_op jit(solution)/shard_map/all_to_all | solution.py:44
  191.1 3.8 gather_fusion.1
  194.9 1.1 broadcast_select_fusion
  196.0 1.3 bitcast_select_fusion.1
  197.3 2.0 fusion.4
  199.3 2.5 fusion.22
  201.9 1.5 multiply_reduce_fusion
  204.1 1.5 copy-done.1
  205.5 3.9 bitcast_multiply_fusion
  209.4 9.2 %fusion.5 = f32[2304,512]{0,1:T(8,128)} fusion(bf16[128,4,512]{0,2,1:T(8,128)(2,1)S(1)} %bitcast.75, f32[2304,576]{0,1:T(8,128)} %bitcast_multiply_fusion, f32[128,4]{0,1:T(4,128)S(1)} %get-tuple-element.15, f32[128,4,2304]{0,2,1:T(8,128)} %copy-done.2), kind=kOutput, calls=%fused_computation.17 | convolution fusion | flops 1212680960 | bytes 19400704 | tf_op jit(solution)/shard_map/dot_general | solution.py:85
  218.6 5.0 pad_maximum_fusion
  223.6 6.3 %copy.116 = f32[2304,576]{1,0:T(8,128)} copy(f32[2304,576]{0,1:T(8,128)} %pad_maximum_fusion) | data formatting | bytes 10616832 | tf_op jit(solution)/shard_map/concatenate | solution.py:86
  229.9 8.0 %gather_fusion.2 = f32[64,64,576]{2,1,0:T(8,128)} fusion(f32[36,64,576]{2,1,0:T(8,128)} %bitcast.65, s32[1024]{0:T(1024)} %pad_clamp_fusion), kind=kCustom, calls=%fused_computation.2 | custom fusion | bytes 18874624 | tf_op jit(solution)/shard_map/jit(_take)/gather | solution.py:87
  237.9 10.2 %select_select_fusion = f32[32,2,64,576]{3,2,1,0:T(8,128)} fusion(f32[32,2,64,576]{3,2,1,0:T(8,128)} %bitcast.66, pred[32,2]{1,0:T(8,128)(4,1)S(1)} %copy-done.11, pred[32,2]{1,0:T(8,128)(4,1)S(1)} %copy-done.10), kind=kLoop, calls=%fused_computation.6 | loop fusion | flops 4718592 | bytes 18874496 | tf_op jit(solution)/shard_map/jit(_where)/select_n | solution.py:90
  248.2 8.4 %all-to-all-start.2 = ((f32[32,2,64,576]{3,2,1,0:T(8,128)}), f32[32,2,64,576]{3,2,1,0:T(8,128)}, u32[]{:S(2)}, u32[]{:S(2)}) async-start(f32[32,2,64,576]{3,2,1,0:T(8,128)} %select_select_fusion), calls=%async_computation.2 | async-start | bytes 20971520 | tf_op jit(solution)/shard_map/all_to_all | solution.py:99
  258.0 231.0 %all-to-all-done.2 = f32[32,2,64,576]{3,2,1,0:T(8,128)} async-done(((f32[32,2,64,576]{3,2,1,0:T(8,128)}), f32[32,2,64,576]{3,2,1,0:T(8,128)}, u32[]{:S(2)}, u32[]{:S(2)}) %all-to-all-start.2) | async-done | bytes 9437216 | tf_op jit(solution)/shard_map/all_to_all | solution.py:99
  489.3 13.9 %scatter_fusion = f32[20,64,576]{2,1,0:T(8,128)S(1)} fusion(f32[20,64,576]{2,1,0:T(8,128)S(1)} %broadcast_in_dim.107, s32[64]{0:T(128)S(1)} %fusion.15, f32[64,64,576]{2,1,0:T(8,128)} %bitcast.23), kind=kCustom, calls=%fused_computation.4 | custom fusion | flops 2359296 | bytes 28311808 | tf_op jit(solution)/shard_map/scatter-add | solution.py:17
  503.3 1.7 copy-done
  505.0 4.1 fusion.12
  509.1 1.1 copy.117
  510.2 73.6 %reduce-scatter.2.cloned.1.call-done = f32[80,576]{1,0:T(8,128)} async-done(((f32[1280,576]{1,0:T(8,128)}), f32[80,576]{1,0:T(8,128)}) %reduce-scatter.2.cloned.1.call-update) | async-done | bytes 184336 | tf_op jit(solution)/shard_map/reduce_scatter | solution.py:101
  (87 shorter events, 10.2 us)
Async XLA Ops:
  38.2 19.0 %all-to-all-start = ((s32[32,1,2]{2,1,0:T(1,128)}), s32[32,1,2]{2,1,0:T(1,128)S(1)}, u32[]{:S(2)}, u32[]{:S(2)}) async-start(s32[32,1,2]{2,1,0:T(1,128)} %copy.92), calls=%async_computation | async-start | bytes 32768 | tf_op jit(solution)/shard_map/all_to_all | solution.py:41
  75.0 8.6 %copy-start.5 = (bf16[128,2048]{1,0:T(8,128)(2,1)S(1)}, bf16[128,2048]{1,0:T(8,128)(2,1)}, u32[]{:S(2)}) copy-start(bf16[128,2048]{1,0:T(8,128)(2,1)} %param.6) | copy-start | bytes 1572868
  75.0 9.6 %copy-start.4 = (bf16[128,2304]{1,0:T(8,128)(2,1)S(1)}, bf16[128,2304]{1,0:T(8,128)(2,1)}, u32[]{:S(2)}) copy-start(bf16[128,2304]{1,0:T(8,128)(2,1)} %param.5) | copy-start | bytes 1769476
  75.0 10.0 %copy-start.8 = (s32[128,32]{0,1:T(8,128)S(1)}, s32[128,32]{0,1:T(8,128)}, u32[]{:S(2)}) copy-start(s32[128,32]{0,1:T(8,128)} %param.7) | copy-start | bytes 49156
  75.0 108.5 %all-to-all-start.1 = ((bf16[32,128,576]{1,2,0:T(8,128)(2,1)}), bf16[32,128,576]{1,2,0:T(8,128)(2,1)}, u32[]{:S(2)}, u32[]{:S(2)}) async-start(bf16[32,128,576]{1,2,0:T(8,128)(2,1)} %copy.98), calls=%async_computation.1 | async-start | bytes 9437184 | tf_op jit(solution)/shard_map/all_to_all | solution.py:44
  80.3 0.6 copy-start.9
  81.8 3.1 copy-start.13
  194.9 1.1 copy-start.12
  194.9 2.4 copy-start.7
  197.3 4.6 copy-start.3
  199.3 2.6 copy-start.2
  199.3 2.6 copy-start.6
  204.1 1.5 copy-start.1
  209.4 9.2 %slice-start = ((f32[2304,576]{0,1:T(8,128)}), f32[2304,64]{0,1:T(8,128)S(1)}, s32[]{:S(2)}) async-start(f32[2304,576]{0,1:T(8,128)} %bitcast_multiply_fusion), calls=%async_computation.5 | async-start | bytes 1179648 | tf_op jit(solution)/shard_map/slice | solution.py:86
  229.9 8.0 %copy-start.10 = (pred[32,2]{1,0:T(8,128)(4,1)S(1)}, pred[32,2]{1,0:T(8,128)(4,1)}, u32[]{:S(2)}) copy-start(pred[32,2]{1,0:T(8,128)(4,1)} %copy-done.9) | copy-start | bytes 196
  229.9 8.0 %copy-start.11 = (pred[32,2]{1,0:T(8,128)(4,1)S(1)}, pred[32,2]{1,0:T(8,128)(4,1)}, u32[]{:S(2)}) copy-start(pred[32,2]{1,0:T(8,128)(4,1)} %copy.112) | copy-start | bytes 196
  248.2 240.8 %all-to-all-start.2 = ((f32[32,2,64,576]{3,2,1,0:T(8,128)}), f32[32,2,64,576]{3,2,1,0:T(8,128)}, u32[]{:S(2)}, u32[]{:S(2)}) async-start(f32[32,2,64,576]{3,2,1,0:T(8,128)} %select_select_fusion), calls=%async_computation.2 | async-start | bytes 20971520 | tf_op jit(solution)/shard_map/all_to_all | solution.py:99
  256.6 327.2 %reduce-scatter.2.cloned.1.call-start = ((), (), s32[]{:S(2)}) async-start(), calls=%async_computation.4 | async-start | bytes 3481600 | tf_op jit(solution)/shard_map/reduce_scatter | solution.py:101
  503.3 1.7 copy-start
Sparse Core Ops, SparseCore 0:
  505.1 78.6 reduce-scatter.1
where the time goes:
time: 594 us; the launch traced here: 591 us
  waiting for transfers between devices  407 us (69%)
  other arithmetic  73.5 us (12%)
  local copies, waits for them, and re-layouts  50.6 us (9%)
  starting transfers between devices  24.1 us (4%)
  matrix products  20.7 us (3%)
  between operations  14.4 us (2%)
    all_to_all x1, waiting for transfers between devices, local(): lax.all_to_all(slot_grad, 'ctx', split_axis=0, concat_axis=0, tiled=True)  231 us
    all_to_all x1, waiting for transfers between devices, local(): lax.all_to_all(outgoing, 'ctx', split_axis=0, concat_axis=0, tiled=True)  96.1 us
    reduce_scatter x1, waiting for transfers between devices, local(): lax.psum_scatter(owner_grad, 'head', scatter_dimension=0, tiled=True)  73.6 us
    another operation x1, other arithmetic, local(): jnp.zeros((all_blocks,), jnp.int32).at[picks.reshape(-1)].max(1) > 0  28.8 us
    scatter-add x1, other arithmetic, owner_total(): jnp.zeros((per_owner, BLOCK, columns), jnp.float32)  13.9 us
  transfers between devices with their start and end apart: 4, of which 4 were waited for; matrix products, arithmetic and copies ran while one was open for 3% of the time, Pallas kernels for 0%

commit v1 on v0

v1 whole, which is shorter than its diff:
```python
import functools

import jax
import jax.numpy as jnp
from jax import lax
from jax.experimental import pallas as pl
from jax.experimental.pallas import tpu as pltpu
from jax.sharding import PartitionSpec as P

LAT = 512
BLOCK = 64
POOL = 36
CAP = 2
NEG = -1e30

score_scale = 192.0 ** (-0.5)
bf16 = jnp.bfloat16
f32 = jnp.float32


def iota(shape, dim):
    return lax.broadcasted_iota(jnp.int32, shape, dim)


def by20(x):
    return (x * 3277) >> 16


def dot(a, b, ca, cb):
    return lax.dot_general(a, b, (((ca,), (cb,)), ((), ())), preferred_element_type=f32)


def call(body, out_shape, *args, scratch=(), flops=0, traffic=0):
    vmem = pl.BlockSpec(memory_space=pltpu.VMEM)
    smem = pl.BlockSpec(memory_space=pltpu.SMEM)
    specs = [smem if a.dtype == jnp.int32 and a.ndim == 1 else vmem for a in args]
    return pl.pallas_call(
        body,
        out_shape=out_shape,
        in_specs=specs,
        out_specs=jax.tree.map(lambda _: vmem, out_shape),
        scratch_shapes=list(scratch),
        compiler_params=pltpu.CompilerParams(vmem_limit_bytes=48 * 1024 * 1024),
        cost_estimate=pl.CostEstimate(flops=flops, bytes_accessed=traffic, transcendentals=0),
    )(*args)


def own_rows(pos_ref, lat_ref, out_ref, *, part):
    rows, tokens = out_ref.shape[0], lat_ref.shape[0]
    row, col = iota((rows, tokens), 0), iota((rows, tokens), 1)
    want = (row >> 2) * BLOCK + pos_ref[1] * part + (row & 3)
    pick = (col == want).astype(f32).astype(bf16)
    out_ref[...] = dot(pick, lat_ref[...], 1, 0).astype(bf16)


def plan(pos_ref, picks_ref, sel_ref, bias_ref, send_ref, local_ref, *, part, per_owner, first):
    queries, picks = picks_ref.shape
    rows, wide = sel_ref.shape
    blocks = wide // part
    parts = BLOCK // part
    lane = iota((queries, blocks), 1)
    hit = jnp.zeros((queries, blocks), jnp.bool_)
    for k in range(picks):
        hit = jnp.logical_or(hit, picks_ref[:, k : k + 1] == lane)
    hit = hit.astype(f32)
    chosen = jnp.max(hit, axis=0, keepdims=True)
    hit = hit.astype(bf16)
    chosen8 = jnp.broadcast_to(chosen, (8, blocks)).astype(bf16)
    lo, hi = iota((blocks, blocks), 0), iota((blocks, blocks), 1)
    before = jnp.where(lo < hi, 1.0, 0.0)
    order = dot(chosen8, before.astype(bf16), 1, 0)[:1]
    same = jnp.where(by20(lo) == by20(hi), before, 0.0)
    rank = dot(chosen8, same.astype(bf16), 1, 0)[:1]
    row = iota((rows, blocks), 0)
    slot = ((row >> 2)).astype(f32)
    here = jnp.where(jnp.logical_and(order == slot, chosen > 0.5), 1.0, 0.0)
    block_id = jnp.sum(here * iota((rows, blocks), 1).astype(f32), axis=1, keepdims=True)
    block_rank = jnp.sum(here * rank, axis=1, keepdims=True)
    block_id = block_id.astype(jnp.int32)
    block_rank = block_rank.astype(jnp.int32)
    row = iota((rows, wide), 0)
    col = iota((rows, wide), 1)
    sel = col == block_id * part + (row & 3)
    sel_ref[...] = jnp.where(sel, 1.0, 0.0).astype(bf16)
    picked = dot(here.astype(bf16), hit, 1, 1)
    query_pos = first + pos_ref[0] * queries + iota((rows, queries), 1)
    for p in range(parts):
        key_pos = block_id * BLOCK + p * part + (iota((rows, queries), 0) & 3)
        allowed = jnp.logical_and(picked > 0.5, key_pos <= query_pos)
        bias_ref[p * rows : (p + 1) * rows, :] = jnp.where(allowed, 0.0, NEG)
    owner = by20(block_id)
    local_id = block_id - owner * per_owner
    row = iota(send_ref.shape, 0)
    col = iota(send_ref.shape, 1)
    target = (owner * CAP + block_rank) * part + (row & 3)
    send_ref[...] = jnp.where(col == target, 1.0, 0.0).astype(bf16)
    lane = iota(local_ref.shape, 1)
    local_ref[...] = jnp.where(lane == 0, local_id.astype(f32), jnp.where(lane == 1, 1.0, 0.0))


def compact(sel_ref, all_ref, out_ref):
    out_ref[...] = dot(sel_ref[...], all_ref[...], 1, 0).astype(bf16)


def attend(k_ref, q_ref, g_ref, bias_ref, dq_ref, dk_ref, s_ref, d_ref, qs_ref, gs_ref, dqs_ref):
    tokens, width = k_ref.shape
    queries = q_ref.shape[0]
    heads = g_ref.shape[1] // LAT
    cols = heads * queries
    step = 256
    steps = tokens // step
    for h in range(heads):
        qs_ref[h * queries : (h + 1) * queries, :] = q_ref[:, h * width : (h + 1) * width]
        gs_ref[h * queries : (h + 1) * queries, :] = g_ref[:, h * LAT : (h + 1) * LAT]

    def one(i, top):
        at = pl.ds(pl.multiple_of(i * step, step), step)
        keys = k_ref[at, :]
        bias = bias_ref[at, :]
        s = dot(keys, qs_ref[...], 1, 1) * score_scale + jnp.concatenate([bias] * heads, axis=1)
        s_ref[at, :] = s
        d_ref[at, :] = dot(keys[:, :LAT], gs_ref[...], 1, 1)
        return jnp.maximum(top, jnp.max(s.reshape(step // 8, 8, cols), axis=0))

    top = lax.fori_loop(0, steps, one, jnp.full((8, cols), -jnp.inf, f32))
    top = jnp.max(top, axis=0, keepdims=True)

    def two(i, carry):
        total, mixed = carry
        at = pl.ds(pl.multiple_of(i * step, step), step)
        e = jnp.exp(s_ref[at, :] - top)
        s_ref[at, :] = e
        ed = e * d_ref[at, :]
        total = total + jnp.sum(e.reshape(step // 8, 8, cols), axis=0)
        mixed = mixed + jnp.sum(ed.reshape(step // 8, 8, cols), axis=0)
        return total, mixed

    zero = jnp.zeros((8, cols), f32)
    total, mixed = lax.fori_loop(0, steps, two, (zero, zero))
    inv = 1.0 / jnp.sum(total, axis=0, keepdims=True)
    delta = jnp.sum(mixed, axis=0, keepdims=True) * inv
    dqs_ref[...] = jnp.zeros_like(dqs_ref)

    def three(i, carry):
        at = pl.ds(pl.multiple_of(i * step, step), step)
        p = s_ref[at, :] * inv
        ds = (p * (d_ref[at, :] - delta)).astype(bf16)
        dk = dot(ds, qs_ref[...], 1, 0) * score_scale
        dv = dot(p.astype(bf16), gs_ref[...], 1, 0)
        dk_ref[at, :LAT] = (dk[:, :LAT] + dv).astype(dk_ref.dtype)
        dk_ref[at, LAT:] = dk[:, LAT:].astype(dk_ref.dtype)
        dqs_ref[...] += dot(ds, k_ref[at, :], 0, 0)
        return carry

    lax.fori_loop(0, steps, three, 0)
    for h in range(heads):
        part = dqs_ref[h * queries : (h + 1) * queries, :] * score_scale
        dq_ref[:, h * width : (h + 1) * width] = part.astype(bf16)


def outgoing(send_ref, grad_ref, local_ref, out_ref):
    width = grad_ref.shape[1]
    send = send_ref[...]
    out_ref[:, :LAT] = dot(send, grad_ref[:, :LAT].astype(bf16), 0, 0).astype(bf16)
    tail = jnp.concatenate(
        [grad_ref[:, LAT:].astype(f32), local_ref[:, : 128 - (width - LAT)]], axis=1
    ).astype(bf16)
    out_ref[:, LAT:] = dot(send, tail, 0, 0).astype(bf16)


def gather_back(pos_ref, in_ref, out_ref, *, part, width):
    rows = in_ref.shape[0]
    outs = out_ref.shape[0]
    parts = BLOCK // part
    mine = pos_ref[1]
    ids = in_ref[:, LAT:].astype(f32)
    lane = iota(ids.shape, 1)
    block = jnp.sum(jnp.where(lane == width - LAT, ids, 0.0), axis=1, keepdims=True)
    valid = jnp.sum(jnp.where(lane == width - LAT + 1, ids, 0.0), axis=1, keepdims=True)
    block = block.astype(jnp.int32)
    row = iota((rows, outs), 0)
    col = iota((rows, outs), 1)
    chunks = outs // part
    per_dest = 20
    dest = col >> 3
    which = (col >> 2) & 1
    start = ((per_dest * dest - mine + parts - 1) >> 4) + which
    inside = parts * start + mine < per_dest * (dest + 1)
    match = jnp.logical_and(block == start, (row & 3) == (col & 3))
    match = jnp.logical_and(match, jnp.logical_and(inside, valid > 0.5))
    out_ref[...] = dot(jnp.where(match, 1.0, 0.0).astype(bf16), in_ref[:, :width], 0, 0)


def place(pos_ref, in_ref, out_ref, *, part):
    outs = out_ref.shape[0]
    rows = in_ref.shape[0]
    parts = BLOCK // part
    per_dest = outs // part
    mine = pos_ref[1]
    row = iota((outs, rows), 0)
    col = iota((outs, rows), 1)
    chunk = per_dest * mine + (row >> 2)
    source = col >> 3
    which = (col >> 2) & 1
    start = ((per_dest * mine - source + parts - 1) >> 4) + which
    match = jnp.logical_and(parts * start + source == chunk, (row & 3) == (col & 3))
    out_ref[...] = lax.dot_general(
        jnp.where(match, 1.0, 0.0),
        in_ref[...].astype(f32),
        (((1,), (0,)), ((), ())),
        precision=lax.Precision.HIGHEST,
        preferred_element_type=f32,
    )


def local(latent, query, grad_out, picks):
    n_ctx = lax.axis_size("ctx")
    n_head = lax.axis_size("head")
    ctx_rows, width = latent.shape
    queries = query.shape[0]
    per_owner = ctx_rows // BLOCK
    blocks = per_owner * n_ctx
    part = BLOCK // n_head
    pool_rows = POOL * part
    pos = jnp.stack([lax.axis_index("ctx"), lax.axis_index("head")]).astype(jnp.int32)
    first = (ctx_rows - queries) * n_ctx
    shape = jax.ShapeDtypeStruct

    own = call(
        functools.partial(own_rows, part=part),
        shape((per_owner * part, width), bf16),
        pos,
        latent,
    )
    everyone = lax.all_gather(own, "ctx", axis=0, tiled=True)
    sel, bias, send, local_id = call(
        functools.partial(plan, part=part, per_owner=per_owner, first=first),
        (
            shape((pool_rows, blocks * part), bf16),
            shape((POOL * BLOCK, queries), f32),
            shape((pool_rows, n_ctx * CAP * part), bf16),
            shape((pool_rows, 128), f32),
        ),
        pos,
        picks,
        flops=4 * 10**9,
        traffic=4 * 10**6,
    )
    mine = call(compact, shape((pool_rows, width), bf16), sel, everyone)
    keys = lax.all_gather(mine, "head", axis=0, tiled=True)
    tokens = POOL * BLOCK
    rows = queries * (grad_out.shape[1] // LAT)
    query_grad, key_grad = call(
        attend,
        (shape(query.shape, bf16), shape((tokens, width), f32)),
        keys,
        query,
        grad_out,
        bias,
        scratch=(
            pltpu.VMEM((tokens, rows), f32),
            pltpu.VMEM((tokens, rows), f32),
            pltpu.VMEM((rows, width), bf16),
            pltpu.VMEM((rows, LAT), bf16),
            pltpu.VMEM((rows, width), f32),
        ),
        flops=7 * 10**9,
        traffic=10**7,
    )
    reduced = lax.psum_scatter(key_grad, "head", scatter_dimension=0, tiled=True)
    slots = n_ctx * CAP * part
    outbox = call(outgoing, shape((slots, 640), bf16), send, reduced, local_id)
    inbox = lax.all_to_all(outbox, "ctx", split_axis=0, concat_axis=0, tiled=True)
    totals = call(
        functools.partial(gather_back, part=part, width=width),
        shape((n_head * CAP * part, width), f32),
        pos,
        inbox,
    )
    spread = lax.all_to_all(totals, "head", split_axis=0, concat_axis=0, tiled=True)
    grad_latent = call(
        functools.partial(place, part=part),
        shape((ctx_rows // n_head, width), f32),
        pos,
        spread,
    )
    return (query_grad, grad_latent)


def solution(mesh):
    return jax.shard_map(
        local,
        mesh=mesh,
        in_specs=(P("ctx", None), P("ctx", "head"), P("ctx", "head"), P("ctx", None)),
        out_specs=(P("ctx", "head"), P(("ctx", "head"), None)),
        check_vma=False,
    )
```

time: 594 us -> 283 us (0.48)
  waiting for transfers between devices: 407 us -> 194 us
  other arithmetic: 73.5 us -> 0.08 us
  local copies, waits for them, and re-layouts: 50.6 us -> 6.75 us
  blocking collectives: 0 us -> 43.3 us
  Pallas kernels: 0 us -> 24.6 us
  starting transfers between devices: 24.1 us -> 0.12 us
  matrix products: 20.7 us -> 0 us
    all_to_all x3 -> x0, waiting for transfers between devices: 334 us -> none  [the longest x1 231 us: local(): lax.all_to_all(slot_grad, 'ctx', split_axis=0, concat_axis=0, tiled=True)]
    all_gather x0 -> x2, waiting for transfers between devices: none -> 130 us  [the longest x1 84.9 us: local(): everyone = lax.all_gather(own, 'ctx', axis=0, tiled=True)]
    all_to_all x0 -> x2, blocking collectives: none -> 43.3 us  [the longest x1 23.8 us: local(): lax.all_to_all(totals, 'head', split_axis=0, concat_axis=0, tiled=True)]
    another operation x3 -> x1, other arithmetic: 29.1 us -> 0.08 us  [local(): jnp.stack([lax.axis_index('ctx'), lax.axis_index('head')]).astype(jnp.int32)]
    pallas_call x0 -> x7, Pallas kernels: none -> 24.6 us  [call(): pl.pallas_call(body, out_shape=out_shape, in_specs=specs, out_specs=jax.t...]
    all_to_all x3 -> x0, starting transfers between devices: 24.1 us -> none  [the longest x1 10.5 us: local(): lax.all_to_all(wanted, 'ctx', split_axis=0, concat_axis=0, tiled=True)]
    dot_general x5 -> x0, matrix products: 20.7 us -> none  [the longest x1 9.17 us: local(): lax.dot_general(probs_low, grad_heads, leading, preferred_element_type=jn...]
    select_n x8 -> x0, other arithmetic: 18.8 us -> none  [the longest x1 10.2 us: local(): jnp.where(flat_filled[:, None, None], slot_grad, 0.0)]
  transfers between devices with their start and end apart: 4 -> 3, of which waited for: 4 -> 3; matrix products, arithmetic and copies ran while one was open for 3% -> 0% of each run, Pallas kernels for 0% -> 1%
where the time goes in v1:
time: 283 us
  waiting for transfers between devices  194 us (69%)
  blocking collectives  43.3 us (15%)
  Pallas kernels  24.6 us (9%)
  between operations  13.8 us (5%)
  local copies, waits for them, and re-layouts  6.75 us (2%)
    all_gather x1, waiting for transfers between devices, local(): everyone = lax.all_gather(own, 'ctx', axis=0, tiled=True)  84.9 us
    reduce_scatter x1, waiting for transfers between devices, local(): lax.psum_scatter(key_grad, 'head', scatter_dimension=0, tiled=True)  64.1 us
    all_gather x1, waiting for transfers between devices, local(): keys = lax.all_gather(mine, 'head', axis=0, tiled=True)  45.3 us
    pallas_call x7, Pallas kernels, call(): pl.pallas_call(body, out_shape=out_shape, in_specs=specs, out_specs=jax.t...  24.6 us
    all_to_all x1, blocking collectives, local(): lax.all_to_all(totals, 'head', split_axis=0, concat_axis=0, tiled=True)  23.8 us
    all_to_all x1, blocking collectives, local(): lax.all_to_all(outbox, 'ctx', split_axis=0, concat_axis=0, tiled=True)  19.5 us
    unnamed x14, local copies, waits for them, and re-layouts  6.75 us
  transfers between devices with their start and end apart: 3, of which 3 were waited for; matrix products, arithmetic and copies ran while one was open for 0% of the time, Pallas kernels for 1%

profile of v1, /device:TPU:1, one launch (start us, length us, event | category | flops | bytes accessed | tf_op | source)
XLA Modules:
  0.0 283.0 jit_solution(15011563758223450052)
XLA Ops:
  7.2 0.0 copy-start.5
  7.2 0.0 all-gather.3.cloned.1.call-start
  7.2 1.9 copy.7.lat_ref
  9.1 0.1 pad_add_fusion.pos_ref
  9.2 1.6 shard_map.60
  10.8 0.0 all-gather.3.cloned.1.call-update
  10.8 0.0 all-gather.5.cloned.1.call-start
  10.9 0.0 copy-done.5
  10.9 0.1 copy.6.picks_ref
  11.0 0.0 copy-start.3
  11.0 0.0 copy-start.4
  11.0 3.2 %shard_map.59 = (bf16[144,2560]{1,0:T(8,128)(2,1)S(1)}, f32[2304,128]{1,0:T(8,128)S(1)}, bf16[144,256]{1,0:T(8,128)(2,1)S(1)}, f32[144,128]{1,0:T(8,128)S(1)}) custom-call(s32[2]{0:T(128)S(1)} %pad_add_fusion.pos_ref, s32[128,32]{1,0:T(8,128)S(1)} %copy.6.picks_ref), custom_call_target="tpu_custom_call" | custom-call | flops 4000000000 | bytes 4000000 | tf_op jit(solution)/shard_map/pallas_call | solution.py:37
  14.3 84.9 %all-gather.3.cloned.1.call-done.all_ref = bf16[2560,576]{1,0:T(8,128)(2,1)} async-done(((bf16[80,576]{1,0:T(8,128)(2,1)}), bf16[2560,576]{1,0:T(8,128)(2,1)}) %all-gather.3.cloned.1.call-update) | async-done | bytes 2949136 | tf_op jit(solution)/shard_map/all_gather | solution.py:235
  99.1 0.0 copy-start
  99.1 1.9 copy-done
  101.1 1.4 shard_map.61
  102.5 0.0 all-gather.5.cloned.1.call-update
  102.5 0.0 reduce-scatter.2.cloned.1.call-start
  102.6 45.3 %all-gather.5.cloned.1.call-done.k_ref = bf16[2304,576]{1,0:T(8,128)(2,1)} async-done(((bf16[144,576]{1,0:T(8,128)(2,1)}), bf16[2304,576]{1,0:T(8,128)(2,1)}) %all-gather.5.cloned.1.call-update) | async-done | bytes 2654224 | tf_op jit(solution)/shard_map/all_gather | solution.py:250
  147.9 0.0 copy-done.3
  147.9 0.0 copy-done.4
  147.9 0.0 copy-start.2
  147.9 1.8 copy-done.2
  149.7 15.5 %shard_map.62 = (bf16[128,2304]{1,0:T(8,128)(2,1)}, f32[2304,576]{1,0:T(8,128)}) custom-call(bf16[2304,576]{1,0:T(8,128)(2,1)S(1)} %copy-done.2, bf16[128,2304]{1,0:T(8,128)(2,1)S(1)} %copy-done.3, bf16[128,2048]{1,0:T(8,128)(2,1)S(1)} %copy-done.4, f32[2304,128]{1,0:T(8,128)S(1)} %get-tuple-element.9.bias_ref), custom_call_target="tpu_custom_call" | custom-call | flops 7000000000 | bytes 10000000 | tf_op jit(solution)/shard_map/pallas_call | solution.py:37
  165.2 0.0 reduce-scatter.2.cloned.1.call-update
  165.3 64.1 %reduce-scatter.2.cloned.1.call-done.grad_ref = f32[144,576]{1,0:T(8,128)} async-done(((f32[2304,576]{1,0:T(8,128)}), f32[144,576]{1,0:T(8,128)}) %reduce-scatter.2.cloned.1.call-update) | async-done | bytes 331792 | tf_op jit(solution)/shard_map/reduce_scatter | solution.py:270
  229.4 1.0 copy-done.1
  230.3 0.3 shard_map.63
  230.7 19.5 %all_to_all.22 = bf16[32,8,640]{2,1,0:T(8,128)(2,1)S(1)} all-to-all(bf16[32,8,640]{2,1,0:T(8,128)(2,1)S(1)} %bitcast.6), channel_id=1, replica_groups=mesh['ctx'=32,'head'=16] {'ctx'}, dimensions={0} | all-to-all | bytes 655360 | tf_op jit(solution)/shard_map/all_to_all | solution.py:273
  250.1 0.9 shard_map.64
  251.0 23.8 %all_to_all.23 = f32[16,8,576]{2,1,0:T(8,128)S(1)} all-to-all(f32[16,8,576]{2,1,0:T(8,128)S(1)} %bitcast.9), channel_id=1, replica_groups=mesh['ctx'=32,'head'=16] {'head'}, dimensions={0} | all-to-all | bytes 589824 | tf_op jit(solution)/shard_map/all_to_all | solution.py:280
  274.9 1.6 shard_map.65
  (1 shorter events, 0.0 us)
Async XLA Ops:
  7.2 3.7 %copy-start.5 = (s32[128,32]{0,1:T(8,128)S(1)}, s32[128,32]{0,1:T(8,128)}, u32[]{:S(2)}) copy-start(s32[128,32]{0,1:T(8,128)} %param.7) | copy-start | bytes 49156
  7.2 92.0 %all-gather.3.cloned.1.call-start = ((), (), s32[]{:S(2)}) async-start(), calls=%async_computation.3 | async-start | bytes 3379200 | tf_op jit(solution)/shard_map/all_gather | solution.py:235
  10.8 137.0 %all-gather.5.cloned.1.call-start = ((), (), s32[]{:S(2)}) async-start(), calls=%async_computation.4 | async-start | bytes 3133440 | tf_op jit(solution)/shard_map/all_gather | solution.py:250
  11.0 136.9 %copy-start.3 = (bf16[128,2304]{1,0:T(8,128)(2,1)S(1)}, bf16[128,2304]{1,0:T(8,128)(2,1)}, u32[]{:S(2)}) copy-start(bf16[128,2304]{1,0:T(8,128)(2,1)} %q_ref.1) | copy-start | bytes 1769476
  11.0 136.9 %copy-start.4 = (bf16[128,2048]{1,0:T(8,128)(2,1)S(1)}, bf16[128,2048]{1,0:T(8,128)(2,1)}, u32[]{:S(2)}) copy-start(bf16[128,2048]{1,0:T(8,128)(2,1)} %g_ref.1) | copy-start | bytes 1572868
  99.1 1.9 copy-start
  102.5 126.8 %reduce-scatter.2.cloned.1.call-start = ((), (), s32[]{:S(2)}) async-start(), calls=%async_computation.5 | async-start | bytes 6266880 | tf_op jit(solution)/shard_map/reduce_scatter | solution.py:270
  147.9 1.8 copy-start.2
  229.4 1.0 copy-start.1
Sparse Core Ops, SparseCore 0:
  11.8 87.3 all-gather.2
  102.6 45.1 all-gather.4
  165.4 63.9 reduce-scatter.1

commit v2 on v1

v2 whole, which is shorter than its diff:
```python
import functools

import jax
import jax.numpy as jnp
from jax import lax
from jax.experimental import pallas as pl
from jax.experimental.pallas import tpu as pltpu
from jax.sharding import PartitionSpec as P

LAT = 512
BLOCK = 64
POOL = 36
CAP = 2
NEG = -1e30

score_scale = 192.0 ** (-0.5)
bf16 = jnp.bfloat16
f32 = jnp.float32


def iota(shape, dim):
    return lax.broadcasted_iota(jnp.int32, shape, dim)


def by20(x):
    return (x * 3277) >> 16


def dot(a, b, ca, cb):
    return lax.dot_general(a, b, (((ca,), (cb,)), ((), ())), preferred_element_type=f32)


def call(body, out_shape, *args, scratch=(), flops=0, traffic=0, mib=16):
    vmem = pl.BlockSpec(memory_space=pltpu.VMEM)
    smem = pl.BlockSpec(memory_space=pltpu.SMEM)
    specs = [smem if a.dtype == jnp.int32 and a.ndim == 1 else vmem for a in args]
    return pl.pallas_call(
        body,
        out_shape=out_shape,
        in_specs=specs,
        out_specs=jax.tree.map(lambda _: vmem, out_shape),
        scratch_shapes=list(scratch),
        compiler_params=pltpu.CompilerParams(vmem_limit_bytes=mib * 1024 * 1024),
        cost_estimate=pl.CostEstimate(flops=flops, bytes_accessed=traffic, transcendentals=0),
    )(*args)


def part_of(head):
    return head & 7


def near(head, core_flip, step):
    z = head >> 1
    core = (head & 1) ^ core_flip
    return 2 * ((z + step) & 3) + core


def choose(picks_ref, hit_ref, info_ref, ask_ref, *, per_owner):
    picks, queries = picks_ref.shape
    blocks = hit_ref.shape[0]
    block = iota((blocks, queries), 0)
    hit = jnp.zeros((blocks, queries), jnp.bool_)
    for k in range(picks):
        hit = jnp.logical_or(hit, picks_ref[k : k + 1, :] == block)
    hit = jnp.where(hit, 1.0, 0.0).astype(bf16)
    hit_ref[...] = hit
    count = dot(jnp.ones((8, queries), bf16), hit, 1, 1)
    chosen = jnp.where(count > 0.5, 1.0, 0.0)
    lo, hi = iota((blocks, blocks), 0), iota((blocks, blocks), 1)
    same = jnp.logical_and(lo < hi, by20(lo) == by20(hi))
    rank = dot(chosen.astype(bf16), jnp.where(same, 1.0, 0.0).astype(bf16), 1, 0)
    info_ref[0:8, :] = chosen
    info_ref[8:16, :] = rank
    chosen, rank = chosen[:1], rank[:1]
    rows = ask_ref.shape[0]
    row, col = iota((rows, blocks), 0), iota((rows, blocks), 1)
    key = jnp.where(chosen > 0.5, by20(col[:1]) * CAP + rank.astype(jnp.int32), -1)
    local_id = (col[:1] - by20(col[:1]) * per_owner).astype(f32)
    ask = jnp.sum(jnp.where((row >> 3) == key, local_id, 0.0), axis=1, keepdims=True)
    ask_ref[...] = jnp.broadcast_to(ask, ask_ref.shape).astype(bf16)


def arrange(pos_ref, hit_ref, info_ref, bias_ref, send_ref, *, part, first):
    blocks, queries = hit_ref.shape
    rows = send_ref.shape[0]
    chosen8 = info_ref[0:8, :]
    chosen = chosen8[:1]
    rank = info_ref[8:9, :]
    lo, hi = iota((blocks, blocks), 0), iota((blocks, blocks), 1)
    before = jnp.where(lo < hi, 1.0, 0.0).astype(bf16)
    order = dot(chosen8.astype(bf16), before, 1, 0)[:1]
    row = iota((rows, blocks), 0)
    slot = (row >> 3).astype(f32)
    here = jnp.where(jnp.logical_and(order == slot, chosen > 0.5), 1.0, 0.0)
    block_id = jnp.sum(here * iota((rows, blocks), 1).astype(f32), axis=1, keepdims=True)
    block_rank = jnp.sum(here * rank, axis=1, keepdims=True)
    block_id = block_id.astype(jnp.int32)
    block_rank = block_rank.astype(jnp.int32)
    picked = dot(here.astype(bf16), hit_ref[...], 1, 0)
    query_pos = first + pos_ref[0] * queries + iota((rows, queries), 1)
    base = block_id * BLOCK + (iota((rows, queries), 0) & 7) - query_pos
    piece = 0
    for flip in (0, 1):
        for step in (0, -1, 1, 2):
            p = near(pos_ref[1], flip, step)
            allowed = jnp.logical_and(picked > 0.5, base + p * part <= 0)
            bias_ref[piece * rows : (piece + 1) * rows, :] = jnp.where(allowed, 0.0, NEG)
            piece += 1
    row = iota(send_ref.shape, 0)
    col = iota(send_ref.shape, 1)
    target = (by20(block_id) * CAP + block_rank) * part + (row & 7)
    send_ref[...] = jnp.where(col == target, 1.0, 0.0).astype(bf16)


def fetch(pos_ref, ask_ref, lat_ref, out_ref, *, part):
    rows, tokens = out_ref.shape[0], lat_ref.shape[0]
    row, col = iota((rows, tokens), 0), iota((rows, tokens), 1)
    want = ask_ref[:, :1].astype(f32).astype(jnp.int32) * BLOCK
    want = want + part_of(pos_ref[1]) * part + (row & 7)
    pick = jnp.where(col == want, 1.0, 0.0).astype(bf16)
    out_ref[...] = dot(pick, lat_ref[...], 1, 0).astype(bf16)


def compact(send_ref, all_ref, out_ref):
    out_ref[...] = dot(send_ref[...], all_ref[...], 1, 0).astype(bf16)


def attend(
    ka_ref, kb_ref, q_ref, g_ref, bias_ref, da_ref, db_ref, ds_ref, s_ref, d_ref, qs_ref, gs_ref
):
    half, width = ka_ref.shape
    queries = q_ref.shape[0]
    heads = g_ref.shape[1] // LAT
    cols = heads * queries
    step = 384
    steps = half // step
    for h in range(heads):
        qs_ref[h * queries : (h + 1) * queries, :] = q_ref[:, h * width : (h + 1) * width]
        gs_ref[h * queries : (h + 1) * queries, :] = g_ref[:, h * LAT : (h + 1) * LAT]
    pieces = ((ka_ref, da_ref, 0), (kb_ref, db_ref, half))

    def fold(x):
        return jnp.sum(x.reshape(step // 8, 8, cols), axis=0)

    top = jnp.full((8, cols), -jnp.inf, f32)
    for k_ref, _, base in pieces:

        def one(i, top, k_ref=k_ref, base=base):
            keys = k_ref[pl.ds(pl.multiple_of(i * step, step), step), :]
            at = pl.ds(pl.multiple_of(base + i * step, step), step)
            bias = bias_ref[at, :]
            s = dot(keys, qs_ref[...], 1, 1) * score_scale + jnp.concatenate([bias] * heads, axis=1)
            s_ref[at, :] = s
            d_ref[at, :] = dot(keys[:, :LAT], gs_ref[...], 1, 1)
            return jnp.maximum(top, jnp.max(s.reshape(step // 8, 8, cols), axis=0))

        top = lax.fori_loop(0, steps, one, top)
    top = jnp.max(top, axis=0, keepdims=True)

    def two(i, carry):
        total, mixed = carry
        at = pl.ds(pl.multiple_of(i * step, step), step)
        e = jnp.exp(s_ref[at, :] - top)
        s_ref[at, :] = e
        return total + fold(e), mixed + fold(e * d_ref[at, :])

    zero = jnp.zeros((8, cols), f32)
    total, mixed = lax.fori_loop(0, 2 * steps, two, (zero, zero))
    inv = 1.0 / jnp.sum(total, axis=0, keepdims=True)
    delta = jnp.sum(mixed, axis=0, keepdims=True) * inv
    for _, dk_ref, base in pieces:

        def three(i, carry, dk_ref=dk_ref, base=base):
            here = pl.ds(pl.multiple_of(i * step, step), step)
            at = pl.ds(pl.multiple_of(base + i * step, step), step)
            p = s_ref[at, :] * inv
            ds = (p * (d_ref[at, :] - delta)).astype(bf16)
            ds_ref[at, :] = ds
            dk = dot(ds, qs_ref[...], 1, 0) * score_scale
            dv = dot(p.astype(bf16), gs_ref[...], 1, 0)
            dk_ref[here, :LAT] = (dk[:, :LAT] + dv).astype(dk_ref.dtype)
            dk_ref[here, LAT:] = dk[:, LAT:].astype(dk_ref.dtype)
            return carry

        lax.fori_loop(0, steps, three, 0)


def query_side(ds_ref, ka_ref, kb_ref, dq_ref, dqs_ref):
    half, width = ka_ref.shape
    queries = dq_ref.shape[0]
    heads = dq_ref.shape[1] // width
    step = 384
    dqs_ref[...] = jnp.zeros_like(dqs_ref)
    for k_ref, base in ((ka_ref, 0), (kb_ref, half)):

        def one(i, carry, k_ref=k_ref, base=base):
            here = pl.ds(pl.multiple_of(i * step, step), step)
            at = pl.ds(pl.multiple_of(base + i * step, step), step)
            dqs_ref[...] += dot(ds_ref[at, :], k_ref[here, :], 0, 0)
            return carry

        lax.fori_loop(0, half // step, one, 0)
    for h in range(heads):
        part = dqs_ref[h * queries : (h + 1) * queries, :] * score_scale
        dq_ref[:, h * width : (h + 1) * width] = part.astype(bf16)


def merge(keep_ref, got_ref, down_ref, up_ref, far_ref):
    rows = down_ref.shape[0]
    for i, out_ref in enumerate((down_ref, up_ref, far_ref)):
        at = slice((i + 1) * rows, (i + 2) * rows)
        out_ref[...] = (keep_ref[at, :] + got_ref[at, :].astype(f32)).astype(bf16)


def outgoing(send_ref, keep_ref, got_ref, up_ref, down_ref, far_ref, out_ref):
    rows = up_ref.shape[0]
    total = keep_ref[:rows, :] + got_ref[:rows, :].astype(f32) + up_ref[...].astype(f32)
    total = total + down_ref[...].astype(f32) + far_ref[...].astype(f32)
    out_ref[...] = dot(send_ref[...], total.astype(bf16), 0, 0).astype(bf16)


def gather_back(pos_ref, ask_ref, in_ref, out_ref, *, per_dest):
    rows, outs = in_ref.shape[0], out_ref.shape[0]
    e = part_of(pos_ref[1])
    block = ask_ref[:, :1].astype(f32).astype(jnp.int32)
    row = iota((rows, outs), 0)
    col = iota((rows, outs), 1)
    dest = col >> 4
    start = ((per_dest * dest - e + 7) >> 3) + ((col >> 3) & 1)
    inside = 8 * start + e < per_dest * (dest + 1)
    match = jnp.logical_and(block == start, (row & 7) == (col & 7))
    match = jnp.where(jnp.logical_and(match, inside), 1.0, 0.0).astype(bf16)
    out_ref[...] = dot(match, in_ref[...], 0, 0).astype(out_ref.dtype)


def place(pos_ref, in_ref, out_ref, *, per_dest):
    outs, rows = out_ref.shape[0], in_ref.shape[0]
    mine = pos_ref[1]
    row = iota((outs, rows), 0)
    col = iota((outs, rows), 1)
    e = part_of(col >> 4)
    start = ((per_dest * mine - e + 7) >> 3) + ((col >> 3) & 1)
    match = jnp.logical_and(8 * start + e == per_dest * mine + (row >> 3), (row & 7) == (col & 7))
    match = jnp.where(match, 1.0, 0.0).astype(bf16)
    out_ref[...] = dot(match, in_ref[...], 1, 0)


def local(latent, query, grad_out, picks):
    n_ctx = lax.axis_size("ctx")
    n_head = lax.axis_size("head")
    ctx_rows, width = latent.shape
    queries = query.shape[0]
    per_owner = ctx_rows // BLOCK
    blocks = per_owner * n_ctx
    part = 8
    pool_rows = POOL * part
    slots = n_ctx * CAP * part
    pos = jnp.stack([lax.axis_index("ctx"), lax.axis_index("head")]).astype(jnp.int32)
    first = (ctx_rows - queries) * n_ctx
    per_dest = ctx_rows // n_head // part
    shape = jax.ShapeDtypeStruct
    up = [(i, (i + 2) % n_head) for i in range(n_head)]
    down = [(i, (i - 2) % n_head) for i in range(n_head)]
    across = [(i, (i + 4 - 8 * (i & 1)) % n_head) for i in range(n_head)]
    twin = [(i, i ^ 1) for i in range(n_head)]

    def swap_ctx(x):
        return lax.all_to_all(
            x.reshape(n_ctx, -1, x.shape[1]), "ctx", split_axis=0, concat_axis=0, tiled=True
        ).reshape(x.shape)

    hit, info, ask = call(
        functools.partial(choose, per_owner=per_owner),
        (shape((blocks, queries), bf16), shape((16, blocks), f32), shape((slots, 128), bf16)),
        picks.T,
    )
    asked = swap_ctx(ask)
    rows_out = call(
        functools.partial(fetch, part=part), shape((slots, width), bf16), pos, asked, latent
    )
    bias, send = call(
        functools.partial(arrange, part=part, first=first),
        (shape((POOL * BLOCK, queries), f32), shape((pool_rows, slots), bf16)),
        pos,
        hit,
        info,
        flops=3 * 10**9,
        traffic=3 * 10**6,
    )
    rows_in = swap_ctx(rows_out)
    mine = call(compact, shape((pool_rows, width), bf16), send, rows_in)
    from_below = lax.ppermute(mine, "head", up)
    from_above = lax.ppermute(mine, "head", down)
    from_far = lax.ppermute(mine, "head", across)
    half = POOL * BLOCK // 2
    keys = jnp.stack([mine, from_below, from_above, from_far])
    twin_keys = lax.ppermute(keys, "head", twin).reshape(half, width)
    keys = keys.reshape(half, width)
    rows = queries * (grad_out.shape[1] // LAT)
    keep, give, score_grad = call(
        attend,
        (
            shape((half, width), f32),
            shape((half, width), bf16),
            shape((2 * half, rows), bf16),
        ),
        keys,
        twin_keys,
        query,
        grad_out,
        bias,
        scratch=(
            pltpu.VMEM((2 * half, rows), f32),
            pltpu.VMEM((2 * half, rows), f32),
            pltpu.VMEM((rows, width), bf16),
            pltpu.VMEM((rows, LAT), bf16),
        ),
        flops=6 * 10**9,
        traffic=10**7,
        mib=24,
    )
    got = lax.ppermute(give.reshape(4, pool_rows, width), "head", twin).reshape(half, width)
    piece = shape((pool_rows, width), bf16)
    to_down, to_up, to_far = call(merge, (piece, piece, piece), keep, got)
    sum_up = lax.ppermute(to_up, "head", up)
    sum_down = lax.ppermute(to_down, "head", down)
    sum_far = lax.ppermute(to_far, "head", across)
    query_grad = call(
        query_side,
        shape(query.shape, bf16),
        score_grad,
        keys,
        twin_keys,
        scratch=(pltpu.VMEM((rows, width), f32),),
        flops=3 * 10**9,
        traffic=10**7,
    )
    outbox = call(
        outgoing, shape((slots, width), bf16), send, keep, got, sum_up, sum_down, sum_far
    )
    inbox = swap_ctx(outbox)
    totals = call(
        functools.partial(gather_back, per_dest=per_dest),
        shape((n_head * CAP * part, width), bf16),
        pos,
        asked,
        inbox,
    )
    spread = lax.all_to_all(
        totals.reshape(n_head, CAP * part, width), "head", split_axis=0, concat_axis=0, tiled=True
    ).reshape(totals.shape)
    grad_latent = call(
        functools.partial(place, per_dest=per_dest),
        shape((ctx_rows // n_head, width), f32),
        pos,
        spread,
    )
    return (query_grad, grad_latent)


def solution(mesh):
    return jax.shard_map(
        local,
        mesh=mesh,
        in_specs=(P("ctx", None), P("ctx", "head"), P("ctx", "head"), P("ctx", None)),
        out_specs=(P("ctx", "head"), P(("ctx", "head"), None)),
        check_vma=False,
    )
```

time: 283 us -> 171 us (0.60)
  waiting for transfers between devices: 194 us -> 61.5 us
  starting transfers between devices: 0.12 us -> 53.8 us
  blocking collectives: 43.3 us -> 23.5 us
  between operations: 13.8 us -> 0.81 us
    all_gather x2 -> x0, waiting for transfers between devices: 130 us -> none  [the longest x1 84.9 us: local(): everyone = lax.all_gather(own, 'ctx', axis=0, tiled=True)]
    reduce_scatter x1 -> x0, waiting for transfers between devices: 64.1 us -> none  [local(): lax.psum_scatter(key_grad, 'head', scatter_dimension=0, tiled=True)]
    ppermute x0 -> x8, starting transfers between devices: none -> 32.8 us  [the longest x1 10.7 us: local(): from_far = lax.ppermute(mine, 'head', across)]
    ppermute x0 -> x8, waiting for transfers between devices: none -> 31.9 us  [the longest x1 8.74 us: local(): sum_far = lax.ppermute(to_far, 'head', across)]
    all_to_all x0 -> x3, waiting for transfers between devices: none -> 29.6 us  [the longest x2 22.8 us: swap_ctx(): lax.all_to_all(x.reshape(n_ctx, -1, x.shape[1]), 'ctx', split_axis=0, con...]
    all_to_all x0 -> x3, starting transfers between devices: none -> 21 us  [the longest x2 14.4 us: swap_ctx(): lax.all_to_all(x.reshape(n_ctx, -1, x.shape[1]), 'ctx', split_axis=0, con...]
    all_to_all x2 -> x1, blocking collectives: 43.3 us -> 23.5 us  [swap_ctx(): lax.all_to_all(x.reshape(n_ctx, -1, x.shape[1]), 'ctx', split_axis=0, con...]
    unnamed x14 -> x15, local copies, waits for them, and re-layouts: 6.75 us -> 5.3 us
  transfers between devices with their start and end apart: 3 -> 11, of which waited for: 3 -> 11; matrix products, arithmetic and copies ran while one was open for 0% -> 1% of each run, Pallas kernels for 1% -> 3%
where the time goes in v2:
time: 171 us; the launch traced here: 170 us
  waiting for transfers between devices  61.5 us (36%)
  starting transfers between devices  53.8 us (31%)
  Pallas kernels  24.8 us (15%)
  blocking collectives  23.5 us (14%)
  local copies, waits for them, and re-layouts  5.3 us (3%)
    pallas_call x10, Pallas kernels, call(): pl.pallas_call(body, out_shape=out_shape, in_specs=specs, out_specs=jax.t...  24.8 us
    all_to_all x1, blocking collectives, swap_ctx(): lax.all_to_all(x.reshape(n_ctx, -1, x.shape[1]), 'ctx', split_axis=0, con...  23.5 us
    all_to_all x2, waiting for transfers between devices, swap_ctx(): lax.all_to_all(x.reshape(n_ctx, -1, x.shape[1]), 'ctx', split_axis=0, con...  22.8 us
    all_to_all x2, starting transfers between devices, swap_ctx(): lax.all_to_all(x.reshape(n_ctx, -1, x.shape[1]), 'ctx', split_axis=0, con...  14.4 us
    ppermute x1, starting transfers between devices, local(): from_far = lax.ppermute(mine, 'head', across)  10.7 us
    ppermute x1, waiting for transfers between devices, local(): sum_far = lax.ppermute(to_far, 'head', across)  8.74 us
    ppermute x1, waiting for transfers between devices, local(): from_above = lax.ppermute(mine, 'head', down)  8.21 us
    all_to_all x1, waiting for transfers between devices, local(): lax.all_to_all(totals.reshape(n_head, CAP * part, width), 'head', split_a...  6.79 us
  transfers between devices with their start and end apart: 11, of which 11 were waited for; matrix products, arithmetic and copies ran while one was open for 1% of the time, Pallas kernels for 3%

profile of v2, /device:TPU:1, one launch (start us, length us, event | category | flops | bytes accessed | tf_op | source)
XLA Modules:
  0.0 170.2 jit_solution(7732531656061260291)
XLA Ops:
  1.3 2.4 %shard_map.59 = (bf16[640,128]{1,0:T(8,128)(2,1)S(1)}, f32[16,640]{1,0:T(8,128)S(1)}, bf16[512,128]{1,0:T(8,128)(2,1)}) custom-call(s32[32,128]{1,0:T(8,128)S(1)} %bitcast.30), custom_call_target="tpu_custom_call" | custom-call | tf_op jit(solution)/shard_map/pallas_call | solution.py:37
  3.8 10.5 %all-to-all-start = ((bf16[32,16,128]{2,1,0:T(8,128)(2,1)}), bf16[32,16,128]{2,1,0:T(8,128)(2,1)S(1)}, u32[]{:S(2)}, u32[]{:S(2)}) async-start(bf16[32,16,128]{2,1,0:T(8,128)(2,1)} %bitcast.3), calls=%async_computation | async-start | bytes 262144 | tf_op jit(solution)/shard_map/all_to_all | solution.py:268
  14.3 1.9 %copy.6.lat_ref = bf16[1280,576]{1,0:T(8,128)(2,1)S(1)} copy(bf16[1280,576]{0,1:T(8,128)(2,1)} %param.4) | data formatting | bytes 2949120 | tf_op args[0]
  16.3 7.4 %all-to-all-done = bf16[32,16,128]{2,1,0:T(8,128)(2,1)S(1)} async-done(((bf16[32,16,128]{2,1,0:T(8,128)(2,1)}), bf16[32,16,128]{2,1,0:T(8,128)(2,1)S(1)}, u32[]{:S(2)}, u32[]{:S(2)}) %all-to-all-start) | async-done | bytes 131104 | tf_op jit(solution)/shard_map/all_to_all | solution.py:268
  23.6 2.6 %shard_map.61 = bf16[512,576]{1,0:T(8,128)(2,1)} custom-call(s32[2]{0:T(128)S(1)} %pad_add_fusion.pos_ref, bf16[512,128]{1,0:T(8,128)(2,1)S(1)} %bitcast.28, bf16[1280,576]{1,0:T(8,128)(2,1)S(1)} %copy.6.lat_ref), custom_call_target="tpu_custom_call" | custom-call | tf_op jit(solution)/shard_map/pallas_call | solution.py:37
  26.2 3.9 %all-to-all-start.1 = ((bf16[32,16,576]{2,1,0:T(8,128)(2,1)}), bf16[32,16,576]{2,1,0:T(8,128)(2,1)S(1)}, u32[]{:S(2)}, u32[]{:S(2)}) async-start(bf16[32,16,576]{2,1,0:T(8,128)(2,1)} %bitcast.5), calls=%async_computation.1 | async-start | bytes 1310720 | tf_op jit(solution)/shard_map/all_to_all | solution.py:268
  30.1 1.2 shard_map.60
  32.3 15.4 %all-to-all-done.1 = bf16[32,16,576]{2,1,0:T(8,128)(2,1)S(1)} async-done(((bf16[32,16,576]{2,1,0:T(8,128)(2,1)}), bf16[32,16,576]{2,1,0:T(8,128)(2,1)S(1)}, u32[]{:S(2)}, u32[]{:S(2)}) %all-to-all-start.1) | async-done | bytes 589856 | tf_op jit(solution)/shard_map/all_to_all | solution.py:268
  48.2 10.7 %collective-permute-start.2 = (bf16[288,576]{1,0:T(8,128)(2,1)S(1)}, bf16[288,576]{1,0:T(8,128)(2,1)S(1)}, u32[]{:S(2)}, u32[]{:S(2)}) collective-permute-start(bf16[288,576]{1,0:T(8,128)(2,1)S(1)} %shard_map.62), channel_id=1, source_target_pairs={{0,4},{1,13},{2,6},{3,15},{4,8},{5,1},{6,10},{7,3},{8,12},{9,5},{1... | collective-permute-start | bytes 995336 | tf_op jit(solution)/shard_map/ppermute | solution.py:294
  58.9 2.2 %collective-permute-start.1 = (bf16[288,576]{1,0:T(8,128)(2,1)S(1)}, bf16[288,576]{1,0:T(8,128)(2,1)S(1)}, u32[]{:S(2)}, u32[]{:S(2)}) collective-permute-start(bf16[288,576]{1,0:T(8,128)(2,1)S(1)} %shard_map.62), channel_id=1, source_target_pairs={{0,14},{1,15},{2,0},{3,1},{4,2},{5,3},{6,4},{7,5},{8,6},{9,7},{10,... | collective-permute-start | bytes 995336 | tf_op jit(solution)/shard_map/ppermute | solution.py:293
  61.0 3.1 %collective-permute-start = (bf16[288,576]{1,0:T(8,128)(2,1)S(1)}, bf16[288,576]{1,0:T(8,128)(2,1)S(1)}, u32[]{:S(2)}, u32[]{:S(2)}) collective-permute-start(bf16[288,576]{1,0:T(8,128)(2,1)S(1)} %shard_map.62), channel_id=1, source_target_pairs={{0,2},{1,3},{2,4},{3,5},{4,6},{5,7},{6,8},{7,9},{8,10},{9,11},{10,... | collective-permute-start | bytes 995336 | tf_op jit(solution)/shard_map/ppermute | solution.py:292
  64.2 2.8 %collective-permute-done.2 = bf16[288,576]{1,0:T(8,128)(2,1)S(1)} collective-permute-done((bf16[288,576]{1,0:T(8,128)(2,1)S(1)}, bf16[288,576]{1,0:T(8,128)(2,1)S(1)}, u32[]{:S(2)}, u32[]{:S(2)}) %collective-permute-start.2) | collective-permute-done | bytes 331808 | tf_op jit(solution)/shard_map/ppermute | solution.py:294
  66.9 8.2 %collective-permute-done.1 = bf16[288,576]{1,0:T(8,128)(2,1)S(1)} collective-permute-done((bf16[288,576]{1,0:T(8,128)(2,1)S(1)}, bf16[288,576]{1,0:T(8,128)(2,1)S(1)}, u32[]{:S(2)}, u32[]{:S(2)}) %collective-permute-start.1) | collective-permute-done | bytes 331808 | tf_op jit(solution)/shard_map/ppermute | solution.py:293
  75.1 1.4 collective-permute-done
  76.8 5.6 %collective-permute-start.3 = (bf16[4,288,576]{2,1,0:T(8,128)(2,1)S(1)}, bf16[4,288,576]{2,1,0:T(8,128)(2,1)S(1)}, u32[]{:S(2)}, u32[]{:S(2)}) collective-permute-start(bf16[4,288,576]{2,1,0:T(8,128)(2,1)S(1)} %pad_maximum_fusion), channel_id=1, source_target_pairs={{0,1},{1,0},{2,3},{3,2},{4,5},{5,4},{6,7},{7,6},{8,9},{9,8},{10,11... | collective-permute-start | bytes 3981320 | tf_op jit(solution)/shard_map/ppermute | solution.py:297
  82.5 2.9 %collective-permute-done.3 = bf16[4,288,576]{2,1,0:T(8,128)(2,1)S(1)} collective-permute-done((bf16[4,288,576]{2,1,0:T(8,128)(2,1)S(1)}, bf16[4,288,576]{2,1,0:T(8,128)(2,1)S(1)}, u32[]{:S(2)}, u32[]{:S(2)}) %collective-permute-start.3) | collective-permute-done | bytes 1327136 | tf_op jit(solution)/shard_map/ppermute | solution.py:297
  85.3 9.6 %shard_map.63 = (f32[1152,576]{1,0:T(8,128)S(1)}, bf16[1152,576]{1,0:T(8,128)(2,1)S(1)}, bf16[2304,512]{1,0:T(8,128)(2,1)S(1)}) custom-call(bf16[1152,576]{1,0:T(8,128)(2,1)S(1)} %bitcast.25, bf16[1152,576]{1,0:T(8,128)(2,1)S(1)} %bitcast.31, bf16[128,2304]{1,0:T(8,128)(2,1)S(1)} %copy-done.1, bf16[128,2048]{1,0:T(8,128)(2,1)S(1)} %copy-done.2, ...), custom_call_target="tpu_custom_call" | custom-call | flops 6000000000 | bytes 10000000 | tf_op jit(solution)/shard_map/pallas_call | solution.py:37
  95.0 2.3 %collective-permute-start.4 = (bf16[4,288,576]{2,1,0:T(8,128)(2,1)S(1)}, bf16[4,288,576]{2,1,0:T(8,128)(2,1)S(1)}, u32[]{:S(2)}, u32[]{:S(2)}) collective-permute-start(bf16[4,288,576]{2,1,0:T(8,128)(2,1)S(1)} %bitcast.33), channel_id=1, source_target_pairs={{0,1},{1,0},{2,3},{3,2},{4,5},{5,4},{6,7},{7,6},{8,9},{9,8},{10,11... | collective-permute-start | bytes 3981320 | tf_op jit(solution)/shard_map/ppermute | solution.py:322
  97.3 2.9 %collective-permute-done.4 = bf16[4,288,576]{2,1,0:T(8,128)(2,1)S(1)} collective-permute-done((bf16[4,288,576]{2,1,0:T(8,128)(2,1)S(1)}, bf16[4,288,576]{2,1,0:T(8,128)(2,1)S(1)}, u32[]{:S(2)}, u32[]{:S(2)}) %collective-permute-start.4) | collective-permute-done | bytes 1327136 | tf_op jit(solution)/shard_map/ppermute | solution.py:322
  100.3 1.9 %collective-permute-start.5 = (bf16[288,576]{1,0:T(8,128)(2,1)S(1)}, bf16[288,576]{1,0:T(8,128)(2,1)S(1)}, u32[]{:S(2)}, u32[]{:S(2)}) collective-permute-start(bf16[288,576]{1,0:T(8,128)(2,1)S(1)} %get-tuple-element.21), channel_id=1, source_target_pairs={{0,2},{1,3},{2,4},{3,5},{4,6},{5,7},{6,8},{7,9},{8,10},{9,11},{10,... | collective-permute-start | bytes 995336 | tf_op jit(solution)/shard_map/ppermute | solution.py:325
  102.3 4.6 %collective-permute-start.6 = (bf16[288,576]{1,0:T(8,128)(2,1)S(1)}, bf16[288,576]{1,0:T(8,128)(2,1)S(1)}, u32[]{:S(2)}, u32[]{:S(2)}) collective-permute-start(bf16[288,576]{1,0:T(8,128)(2,1)S(1)} %get-tuple-element.22), channel_id=1, source_target_pairs={{0,14},{1,15},{2,0},{3,1},{4,2},{5,3},{6,4},{7,5},{8,6},{9,7},{10,... | collective-permute-start | bytes 995336 | tf_op jit(solution)/shard_map/ppermute | solution.py:326
  106.8 2.4 %collective-permute-start.7 = (bf16[288,576]{1,0:T(8,128)(2,1)S(1)}, bf16[288,576]{1,0:T(8,128)(2,1)S(1)}, u32[]{:S(2)}, u32[]{:S(2)}) collective-permute-start(bf16[288,576]{1,0:T(8,128)(2,1)S(1)} %get-tuple-element.23), channel_id=1, source_target_pairs={{0,4},{1,13},{2,6},{3,15},{4,8},{5,1},{6,10},{7,3},{8,12},{9,5},{1... | collective-permute-start | bytes 995336 | tf_op jit(solution)/shard_map/ppermute | solution.py:327
  109.3 3.9 %collective-permute-done.5.up_ref = bf16[288,576]{1,0:T(8,128)(2,1)S(1)} collective-permute-done((bf16[288,576]{1,0:T(8,128)(2,1)S(1)}, bf16[288,576]{1,0:T(8,128)(2,1)S(1)}, u32[]{:S(2)}, u32[]{:S(2)}) %collective-permute-start.5) | collective-permute-done | bytes 331808 | tf_op jit(solution)/shard_map/ppermute | solution.py:325
  113.2 1.1 collective-permute-done.6.down_ref
  114.4 8.7 %collective-permute-done.7.far_ref = bf16[288,576]{1,0:T(8,128)(2,1)S(1)} collective-permute-done((bf16[288,576]{1,0:T(8,128)(2,1)S(1)}, bf16[288,576]{1,0:T(8,128)(2,1)S(1)}, u32[]{:S(2)}, u32[]{:S(2)}) %collective-permute-start.7) | collective-permute-done | bytes 331808 | tf_op jit(solution)/shard_map/ppermute | solution.py:327
  123.8 23.5 %all_to_all.20 = bf16[32,16,576]{2,1,0:T(8,128)(2,1)S(1)} all-to-all(bf16[32,16,576]{2,1,0:T(8,128)(2,1)S(1)} %bitcast.21), channel_id=1, replica_groups=mesh['ctx'=32,'head'=16] {'ctx'}, dimensions={0} | all-to-all | bytes 1179648 | tf_op jit(solution)/shard_map/all_to_all | solution.py:268
  147.3 1.8 %shard_map.67 = bf16[256,576]{1,0:T(8,128)(2,1)} custom-call(s32[2]{0:T(128)S(1)} %pad_add_fusion.pos_ref, bf16[512,128]{1,0:T(8,128)(2,1)S(1)} %bitcast.29, bf16[512,576]{1,0:T(8,128)(2,1)S(1)} %bitcast.23), custom_call_target="tpu_custom_call" | custom-call | tf_op jit(solution)/shard_map/pallas_call | solution.py:37
  149.1 6.6 %all-to-all-start.3 = ((bf16[16,16,576]{2,1,0:T(8,128)(2,1)}), bf16[16,16,576]{2,1,0:T(8,128)(2,1)S(1)}, u32[]{:S(2)}, u32[]{:S(2)}) async-start(bf16[16,16,576]{2,1,0:T(8,128)(2,1)} %bitcast.17), calls=%async_computation.3 | async-start | bytes 655360 | tf_op jit(solution)/shard_map/all_to_all | solution.py:349
  155.7 1.7 copy-done.4
  157.3 4.6 %shard_map.64 = bf16[128,2304]{1,0:T(8,128)(2,1)} custom-call(bf16[2304,512]{1,0:T(8,128)(2,1)S(1)} %copy-done.4, bf16[1152,576]{1,0:T(8,128)(2,1)S(1)} %bitcast.26, bf16[1152,576]{1,0:T(8,128)(2,1)S(1)} %bitcast.32), custom_call_target="tpu_custom_call" | custom-call | flops 3000000000 | bytes 10000000 | tf_op jit(solution)/shard_map/pallas_call | solution.py:37
  162.0 6.8 %all-to-all-done.3 = bf16[16,16,576]{2,1,0:T(8,128)(2,1)S(1)} async-done(((bf16[16,16,576]{2,1,0:T(8,128)(2,1)}), bf16[16,16,576]{2,1,0:T(8,128)(2,1)S(1)}, u32[]{:S(2)}, u32[]{:S(2)}) %all-to-all-start.3) | async-done | bytes 294944 | tf_op jit(solution)/shard_map/all_to_all | solution.py:349
  168.7 1.4 shard_map.68
  (18 shorter events, 3.3 us)
Async XLA Ops:
  0.6 0.7 copy-start
  3.8 19.9 %all-to-all-start = ((bf16[32,16,128]{2,1,0:T(8,128)(2,1)}), bf16[32,16,128]{2,1,0:T(8,128)(2,1)S(1)}, u32[]{:S(2)}, u32[]{:S(2)}) async-start(bf16[32,16,128]{2,1,0:T(8,128)(2,1)} %bitcast.3), calls=%async_computation | async-start | bytes 262144 | tf_op jit(solution)/shard_map/all_to_all | solution.py:268
  26.2 21.6 %all-to-all-start.1 = ((bf16[32,16,576]{2,1,0:T(8,128)(2,1)}), bf16[32,16,576]{2,1,0:T(8,128)(2,1)S(1)}, u32[]{:S(2)}, u32[]{:S(2)}) async-start(bf16[32,16,576]{2,1,0:T(8,128)(2,1)} %bitcast.5), calls=%async_computation.1 | async-start | bytes 1310720 | tf_op jit(solution)/shard_map/all_to_all | solution.py:268
  31.3 1.0 copy-start.5
  48.2 18.7 %collective-permute-start.2 = (bf16[288,576]{1,0:T(8,128)(2,1)S(1)}, bf16[288,576]{1,0:T(8,128)(2,1)S(1)}, u32[]{:S(2)}, u32[]{:S(2)}) collective-permute-start(bf16[288,576]{1,0:T(8,128)(2,1)S(1)} %shard_map.62), channel_id=1, source_target_pairs={{0,4},{1,13},{2,6},{3,15},{4,8},{5,1},{6,10},{7,3},{8,12},{9,5},{1... | collective-permute-start | bytes 995336 | tf_op jit(solution)/shard_map/ppermute | solution.py:294
  58.9 16.3 %collective-permute-start.1 = (bf16[288,576]{1,0:T(8,128)(2,1)S(1)}, bf16[288,576]{1,0:T(8,128)(2,1)S(1)}, u32[]{:S(2)}, u32[]{:S(2)}) collective-permute-start(bf16[288,576]{1,0:T(8,128)(2,1)S(1)} %shard_map.62), channel_id=1, source_target_pairs={{0,14},{1,15},{2,0},{3,1},{4,2},{5,3},{6,4},{7,5},{8,6},{9,7},{10,... | collective-permute-start | bytes 995336 | tf_op jit(solution)/shard_map/ppermute | solution.py:293
  61.0 15.5 %collective-permute-start = (bf16[288,576]{1,0:T(8,128)(2,1)S(1)}, bf16[288,576]{1,0:T(8,128)(2,1)S(1)}, u32[]{:S(2)}, u32[]{:S(2)}) collective-permute-start(bf16[288,576]{1,0:T(8,128)(2,1)S(1)} %shard_map.62), channel_id=1, source_target_pairs={{0,2},{1,3},{2,4},{3,5},{4,6},{5,7},{6,8},{7,9},{8,10},{9,11},{10,... | collective-permute-start | bytes 995336 | tf_op jit(solution)/shard_map/ppermute | solution.py:292
  76.5 8.8 %copy-start.1 = (bf16[128,2304]{1,0:T(8,128)(2,1)S(1)}, bf16[128,2304]{1,0:T(8,128)(2,1)}, u32[]{:S(2)}) copy-start(bf16[128,2304]{1,0:T(8,128)(2,1)} %q_ref.1) | copy-start | bytes 1769476
  76.5 8.8 %copy-start.2 = (bf16[128,2048]{1,0:T(8,128)(2,1)S(1)}, bf16[128,2048]{1,0:T(8,128)(2,1)}, u32[]{:S(2)}) copy-start(bf16[128,2048]{1,0:T(8,128)(2,1)} %g_ref.1) | copy-start | bytes 1572868
  76.5 8.8 %copy-start.6 = (f32[2304,128]{1,0:T(8,128)S(1)}, f32[2304,128]{1,0:T(8,128)}, u32[]{:S(2)}) copy-start(f32[2304,128]{1,0:T(8,128)} %copy-done.5) | copy-start | bytes 3538948
  76.8 8.5 %collective-permute-start.3 = (bf16[4,288,576]{2,1,0:T(8,128)(2,1)S(1)}, bf16[4,288,576]{2,1,0:T(8,128)(2,1)S(1)}, u32[]{:S(2)}, u32[]{:S(2)}) collective-permute-start(bf16[4,288,576]{2,1,0:T(8,128)(2,1)S(1)} %pad_maximum_fusion), channel_id=1, source_target_pairs={{0,1},{1,0},{2,3},{3,2},{4,5},{5,4},{6,7},{7,6},{8,9},{9,8},{10,11... | collective-permute-start | bytes 3981320 | tf_op jit(solution)/shard_map/ppermute | solution.py:297
  95.0 5.4 %copy-start.3 = (bf16[2304,512]{1,0:T(8,128)(2,1)}, bf16[2304,512]{1,0:T(8,128)(2,1)S(1)}, u32[]{:S(2)}) copy-start(bf16[2304,512]{1,0:T(8,128)(2,1)S(1)} %get-tuple-element.18.ds_ref) | copy-start | bytes 7077892
  95.0 5.2 %collective-permute-start.4 = (bf16[4,288,576]{2,1,0:T(8,128)(2,1)S(1)}, bf16[4,288,576]{2,1,0:T(8,128)(2,1)S(1)}, u32[]{:S(2)}, u32[]{:S(2)}) collective-permute-start(bf16[4,288,576]{2,1,0:T(8,128)(2,1)S(1)} %bitcast.33), channel_id=1, source_target_pairs={{0,1},{1,0},{2,3},{3,2},{4,5},{5,4},{6,7},{7,6},{8,9},{9,8},{10,11... | collective-permute-start | bytes 3981320 | tf_op jit(solution)/shard_map/ppermute | solution.py:322
  100.3 12.9 %collective-permute-start.5 = (bf16[288,576]{1,0:T(8,128)(2,1)S(1)}, bf16[288,576]{1,0:T(8,128)(2,1)S(1)}, u32[]{:S(2)}, u32[]{:S(2)}) collective-permute-start(bf16[288,576]{1,0:T(8,128)(2,1)S(1)} %get-tuple-element.21), channel_id=1, source_target_pairs={{0,2},{1,3},{2,4},{3,5},{4,6},{5,7},{6,8},{7,9},{8,10},{9,11},{10,... | collective-permute-start | bytes 995336 | tf_op jit(solution)/shard_map/ppermute | solution.py:325
  102.3 12.1 %collective-permute-start.6 = (bf16[288,576]{1,0:T(8,128)(2,1)S(1)}, bf16[288,576]{1,0:T(8,128)(2,1)S(1)}, u32[]{:S(2)}, u32[]{:S(2)}) collective-permute-start(bf16[288,576]{1,0:T(8,128)(2,1)S(1)} %get-tuple-element.22), channel_id=1, source_target_pairs={{0,14},{1,15},{2,0},{3,1},{4,2},{5,3},{6,4},{7,5},{8,6},{9,7},{10,... | collective-permute-start | bytes 995336 | tf_op jit(solution)/shard_map/ppermute | solution.py:326
  106.8 16.3 %collective-permute-start.7 = (bf16[288,576]{1,0:T(8,128)(2,1)S(1)}, bf16[288,576]{1,0:T(8,128)(2,1)S(1)}, u32[]{:S(2)}, u32[]{:S(2)}) collective-permute-start(bf16[288,576]{1,0:T(8,128)(2,1)S(1)} %get-tuple-element.23), channel_id=1, source_target_pairs={{0,4},{1,13},{2,6},{3,15},{4,8},{5,1},{6,10},{7,3},{8,12},{9,5},{1... | collective-permute-start | bytes 995336 | tf_op jit(solution)/shard_map/ppermute | solution.py:327
  149.1 19.7 %all-to-all-start.3 = ((bf16[16,16,576]{2,1,0:T(8,128)(2,1)}), bf16[16,16,576]{2,1,0:T(8,128)(2,1)S(1)}, u32[]{:S(2)}, u32[]{:S(2)}) async-start(bf16[16,16,576]{2,1,0:T(8,128)(2,1)} %bitcast.17), calls=%async_computation.3 | async-start | bytes 655360 | tf_op jit(solution)/shard_map/all_to_all | solution.py:349
  155.7 1.7 copy-start.4

commit v3 on v2

v3 whole, which is shorter than its diff:
```python
import functools

import jax
import jax.numpy as jnp
from jax import lax
from jax.experimental import pallas as pl
from jax.experimental.pallas import tpu as pltpu
from jax.sharding import PartitionSpec as P

LAT = 512
BLOCK = 64
POOL = 36
CAP = 2
NEG = -1e30

score_scale = 192.0 ** (-0.5)
bf16 = jnp.bfloat16
f32 = jnp.float32


def iota(shape, dim):
    return lax.broadcasted_iota(jnp.int32, shape, dim)


def by20(x):
    return (x * 3277) >> 16


def dot(a, b, ca, cb):
    return lax.dot_general(a, b, (((ca,), (cb,)), ((), ())), preferred_element_type=f32)


def call(body, out_shape, *args, scratch=(), flops=0, traffic=0, mib=16):
    vmem = pl.BlockSpec(memory_space=pltpu.VMEM)
    smem = pl.BlockSpec(memory_space=pltpu.SMEM)
    specs = [smem if a.dtype == jnp.int32 and a.ndim == 1 else vmem for a in args]
    return pl.pallas_call(
        body,
        out_shape=out_shape,
        in_specs=specs,
        out_specs=jax.tree.map(lambda _: vmem, out_shape),
        scratch_shapes=list(scratch),
        compiler_params=pltpu.CompilerParams(vmem_limit_bytes=mib * 1024 * 1024),
        cost_estimate=pl.CostEstimate(flops=flops, bytes_accessed=traffic, transcendentals=0),
    )(*args)


PART = 8
LINES = 4


def part_of(head):
    return head & 7


def near(head, core_flip, step):
    z = head >> 1
    core = (head & 1) ^ core_flip
    return 2 * ((z + step) & 3) + core


def one_hot(mask):
    return jnp.where(mask, 1.0, 0.0).astype(bf16)


def own_part(pos_ref, lat_ref, out_ref):
    rows, tokens, width = out_ref.shape[0], lat_ref.shape[0], lat_ref.shape[1]
    row, col = iota((rows, tokens), 0), iota((rows, tokens), 1)
    want = (row >> 2) * BLOCK + part_of(pos_ref[1]) * PART + (row & 3)
    for u in (0, 1):
        lines = dot(one_hot(col == want + u * LINES), lat_ref[...], 1, 0)
        out_ref[:, u * width : (u + 1) * width] = lines.astype(bf16)


def choose(picks_ref, hit_ref, info_ref, ask_ref, *, per_owner):
    picks, queries = picks_ref.shape
    blocks = hit_ref.shape[0]
    block = iota((blocks, queries), 0)
    hit = jnp.zeros((blocks, queries), jnp.bool_)
    for k in range(picks):
        hit = jnp.logical_or(hit, picks_ref[k : k + 1, :] == block)
    hit = one_hot(hit)
    hit_ref[...] = hit
    count = dot(jnp.ones((8, queries), bf16), hit, 1, 1)
    chosen = jnp.where(count > 0.5, 1.0, 0.0)
    lo, hi = iota((blocks, blocks), 0), iota((blocks, blocks), 1)
    same = jnp.logical_and(lo < hi, lo >= by20(hi[:1]) * per_owner)
    rank = dot(chosen.astype(bf16), one_hot(same), 1, 0)
    info_ref[0:8, :] = chosen
    info_ref[8:16, :] = rank
    chosen, rank = chosen[:1], rank[:1]
    rows = ask_ref.shape[0]
    row, col = iota((rows, blocks), 0), iota((1, blocks), 1)
    key = jnp.where(chosen > 0.5, by20(col) * CAP + rank.astype(jnp.int32), -1)
    local_id = (col - by20(col) * per_owner).astype(f32)
    ask = jnp.sum(jnp.where((row >> 2) == key, local_id, 0.0), axis=1, keepdims=True)
    ask_ref[...] = jnp.broadcast_to(ask, ask_ref.shape).astype(bf16)


def fetch(ask_ref, own_ref, out_ref):
    rows, lines = out_ref.shape[0], own_ref.shape[0]
    row, col = iota((rows, lines), 0), iota((rows, lines), 1)
    want = ask_ref[:, :1].astype(f32).astype(jnp.int32) * LINES + (row & 3)
    out_ref[...] = dot(one_hot(col == want), own_ref[...], 1, 0).astype(bf16)


def arrange(
    pos_ref, hit_ref, info_ref, ask_ref, bias_ref, send_ref, back_ref, sum_ref, place_ref, *, first, per_dest
):
    blocks, queries = hit_ref.shape
    rows, slots = send_ref.shape
    head = pos_ref[1]
    chosen8 = info_ref[0:8, :]
    chosen = chosen8[:1]
    rank = info_ref[8:9, :]
    lo, hi = iota((blocks, blocks), 0), iota((blocks, blocks), 1)
    order = dot(chosen8.astype(bf16), one_hot(lo < hi), 1, 0)[:1]
    row = iota((rows, blocks), 0)
    slot = (row >> 2).astype(f32)
    here = jnp.where(jnp.logical_and(order == slot, chosen > 0.5), 1.0, 0.0)
    block_id = jnp.sum(here * iota((rows, blocks), 1).astype(f32), axis=1, keepdims=True)
    block_rank = jnp.sum(here * rank, axis=1, keepdims=True)
    block_id = block_id.astype(jnp.int32)
    block_rank = block_rank.astype(jnp.int32)
    picked = dot(here.astype(bf16), hit_ref[...], 1, 0)
    query_pos = first + pos_ref[0] * queries + iota((rows, queries), 1)
    base = block_id * BLOCK + (iota((rows, queries), 0) & 3) - query_pos
    piece = 0
    for flip in (0, 1):
        for u in (0, 1):
            for step in (0, -1, 1, 2):
                offset = near(head, flip, step) * PART + u * LINES
                allowed = jnp.logical_and(picked > 0.5, base + offset <= 0)
                bias_ref[piece * rows : (piece + 1) * rows, :] = jnp.where(allowed, 0.0, NEG)
                piece += 1
    row = iota(send_ref.shape, 0)
    col = iota(send_ref.shape, 1)
    send = one_hot(col == (by20(block_id) * CAP + block_rank) * LINES + (row & 3))
    send_ref[...] = send
    unit = one_hot(iota((rows, rows), 0) == iota((rows, rows), 1))
    back_ref[...] = dot(send, unit, 0, 0).astype(bf16)
    ids = dot(one_hot(iota((8, 128), 1) == 0), ask_ref[...], 1, 1)[:1].astype(jnp.int32)
    row = iota(sum_ref.shape, 0)
    col = iota(sum_ref.shape, 1)
    e = part_of(head)
    dest = row >> 3
    start = ((per_dest * dest - e + 7) >> 3) + ((row >> 2) & 1)
    inside = 8 * start + e < per_dest * (dest + 1)
    match = jnp.logical_and(ids == start, (row & 3) == (col & 3))
    sum_ref[...] = one_hot(jnp.logical_and(match, inside))
    outs = place_ref.shape[0] // 2
    row = iota((outs, place_ref.shape[1]), 0)
    col = iota((outs, place_ref.shape[1]), 1)
    e = part_of(col >> 3)
    start = ((per_dest * head - e + 7) >> 3) + ((col >> 2) & 1)
    match = jnp.logical_and(8 * start + e == per_dest * head + (row >> 3), (row & 3) == (col & 3))
    for u in (0, 1):
        mine = jnp.logical_and(match, ((row >> 2) & 1) == u)
        place_ref[u * outs : (u + 1) * outs, :] = one_hot(mine)


def multiply(a_ref, b_ref, out_ref):
    out_ref[...] = dot(a_ref[...], b_ref[...], 1, 0).astype(out_ref.dtype)


def attend(
    ka_ref, kb_ref, q_ref, g_ref, bias_ref, keep_ref, give_ref, ds_ref, k_ref, s_ref, d_ref, qs_ref, gs_ref
):
    tokens, width = k_ref.shape
    queries = q_ref.shape[0]
    heads = g_ref.shape[1] // LAT
    cols = heads * queries
    quarter = tokens // 4
    for i, (piece_ref, u) in enumerate(((ka_ref, 0), (ka_ref, 1), (kb_ref, 0), (kb_ref, 1))):
        k_ref[i * quarter : (i + 1) * quarter, :] = piece_ref[:, u * width : (u + 1) * width]
    for h in range(heads):
        qs_ref[h * queries : (h + 1) * queries, :] = q_ref[:, h * width : (h + 1) * width]
        gs_ref[h * queries : (h + 1) * queries, :] = g_ref[:, h * LAT : (h + 1) * LAT]
    step = 384

    def fold(x):
        return jnp.sum(x.reshape(step // 8, 8, cols), axis=0)

    def one(i, top):
        at = pl.ds(pl.multiple_of(i * step, step), step)
        keys = k_ref[at, :]
        bias = bias_ref[at, :]
        s = dot(keys, qs_ref[...], 1, 1) * score_scale + jnp.concatenate([bias] * heads, axis=1)
        s_ref[at, :] = s
        d_ref[at, :] = dot(keys[:, :LAT], gs_ref[...], 1, 1)
        return jnp.maximum(top, jnp.max(s.reshape(step // 8, 8, cols), axis=0))

    top = lax.fori_loop(0, tokens // step, one, jnp.full((8, cols), -jnp.inf, f32))
    top = jnp.max(top, axis=0, keepdims=True)

    def two(i, carry):
        total, mixed = carry
        at = pl.ds(pl.multiple_of(i * step, step), step)
        e = jnp.exp(s_ref[at, :] - top)
        s_ref[at, :] = e
        return total + fold(e), mixed + fold(e * d_ref[at, :])

    zero = jnp.zeros((8, cols), f32)
    total, mixed = lax.fori_loop(0, tokens // step, two, (zero, zero))
    inv = 1.0 / jnp.sum(total, axis=0, keepdims=True)
    delta = jnp.sum(mixed, axis=0, keepdims=True) * inv
    less = quarter // 2
    for i, (out_ref, u) in enumerate(((keep_ref, 0), (keep_ref, 1), (give_ref, 0), (give_ref, 1))):

        def three(j, carry, i=i, out_ref=out_ref, u=u):
            here = pl.ds(pl.multiple_of(j * less, less), less)
            at = pl.ds(pl.multiple_of(i * quarter + j * less, less), less)
            p = s_ref[at, :] * inv
            ds = (p * (d_ref[at, :] - delta)).astype(bf16)
            ds_ref[at, :] = ds
            dk = dot(ds, qs_ref[...], 1, 0) * score_scale
            dv = dot(p.astype(bf16), gs_ref[...], 1, 0)
            both = jnp.concatenate([dk[:, :LAT] + dv, dk[:, LAT:]], axis=1)
            out_ref[here, u * width : (u + 1) * width] = both.astype(out_ref.dtype)
            return carry

        lax.fori_loop(0, 2, three, 0)


def query_side(ds_ref, k_ref, dq_ref, dqs_ref):
    tokens, width = k_ref.shape
    queries = dq_ref.shape[0]
    heads = dq_ref.shape[1] // width
    step = 768
    dqs_ref[...] = jnp.zeros_like(dqs_ref)

    def one(i, carry):
        at = pl.ds(pl.multiple_of(i * step, step), step)
        dqs_ref[...] += dot(ds_ref[at, :], k_ref[at, :], 0, 0)
        return carry

    lax.fori_loop(0, tokens // step, one, 0)
    for h in range(heads):
        part = dqs_ref[h * queries : (h + 1) * queries, :] * score_scale
        dq_ref[:, h * width : (h + 1) * width] = part.astype(bf16)


def merge(keep_ref, got_ref, down_ref, up_ref, far_ref):
    rows = down_ref.shape[0]
    for i, out_ref in enumerate((down_ref, up_ref, far_ref)):
        at = slice((i + 1) * rows, (i + 2) * rows)
        out_ref[...] = (keep_ref[at, :] + got_ref[at, :].astype(f32)).astype(bf16)


def outgoing(back_ref, keep_ref, got_ref, up_ref, down_ref, far_ref, out_ref):
    rows = up_ref.shape[0]
    total = keep_ref[:rows, :] + got_ref[:rows, :].astype(f32) + up_ref[...].astype(f32)
    total = total + down_ref[...].astype(f32) + far_ref[...].astype(f32)
    out_ref[...] = dot(back_ref[...], total.astype(bf16), 1, 0).astype(bf16)


def place(place_ref, in_ref, out_ref):
    outs, width = out_ref.shape
    first = dot(place_ref[:outs, :], in_ref[:, :width], 1, 0)
    out_ref[...] = first + dot(place_ref[outs:, :], in_ref[:, width:], 1, 0)


def local(latent, query, grad_out, picks):
    n_ctx = lax.axis_size("ctx")
    n_head = lax.axis_size("head")
    ctx_rows, width = latent.shape
    queries = query.shape[0]
    per_owner = ctx_rows // BLOCK
    blocks = per_owner * n_ctx
    line = 2 * width
    pool_lines = POOL * LINES
    slots = n_ctx * CAP * LINES
    tokens = POOL * BLOCK
    outs = ctx_rows // n_head
    pos = jnp.stack([lax.axis_index("ctx"), lax.axis_index("head")]).astype(jnp.int32)
    first = (ctx_rows - queries) * n_ctx
    shape = jax.ShapeDtypeStruct
    up = [(i, (i + 2) % n_head) for i in range(n_head)]
    down = [(i, (i - 2) % n_head) for i in range(n_head)]
    across = [(i, (i + 4 - 8 * (i & 1)) % n_head) for i in range(n_head)]
    twin = [(i, i ^ 1) for i in range(n_head)]

    def swap(x, axis):
        n = lax.axis_size(axis)
        x3 = x.reshape(n, -1, x.shape[1])
        return lax.all_to_all(x3, axis, split_axis=0, concat_axis=0, tiled=True).reshape(x.shape)

    hit, info, ask = call(
        functools.partial(choose, per_owner=per_owner),
        (shape((blocks, queries), bf16), shape((16, blocks), f32), shape((slots, 128), bf16)),
        picks.T,
    )
    own = call(own_part, shape((per_owner * LINES, line), bf16), pos, latent, flops=10**9, traffic=10**6)
    asked = swap(ask, "ctx")
    lines_out = call(fetch, shape((slots, line), bf16), asked, own)
    bias, send, back, sums, places = call(
        functools.partial(arrange, first=first, per_dest=outs // PART),
        (
            shape((tokens, queries), f32),
            shape((pool_lines, slots), bf16),
            shape((slots, pool_lines), bf16),
            shape((n_head * CAP * LINES, slots), bf16),
            shape((2 * outs, n_head * CAP * LINES), bf16),
        ),
        pos,
        hit,
        info,
        asked,
        flops=3 * 10**9,
        traffic=3 * 10**6,
    )
    lines_in = swap(lines_out, "ctx")
    mine = call(multiply, shape((pool_lines, line), bf16), send, lines_in)
    from_below = lax.ppermute(mine, "head", up)
    from_above = lax.ppermute(mine, "head", down)
    from_far = lax.ppermute(mine, "head", across)
    keys = jnp.stack([mine, from_below, from_above, from_far])
    twin_keys = lax.ppermute(keys, "head", twin).reshape(4 * pool_lines, line)
    keys = keys.reshape(4 * pool_lines, line)
    rows = queries * (grad_out.shape[1] // LAT)
    keep, give, score_grad, all_keys = call(
        attend,
        (
            shape((4 * pool_lines, line), f32),
            shape((4 * pool_lines, line), bf16),
            shape((tokens, rows), bf16),
            shape((tokens, width), bf16),
        ),
        keys,
        twin_keys,
        query,
        grad_out,
        bias,
        scratch=(
            pltpu.VMEM((tokens, rows), f32),
            pltpu.VMEM((tokens, rows), f32),
            pltpu.VMEM((rows, width), bf16),
            pltpu.VMEM((rows, LAT), bf16),
        ),
        flops=6 * 10**9,
        traffic=10**7,
        mib=24,
    )
    got = lax.ppermute(give.reshape(4, pool_lines, line), "head", twin)
    got = got.reshape(4 * pool_lines, line)
    piece = shape((pool_lines, line), bf16)
    to_down, to_up, to_far = call(merge, (piece, piece, piece), keep, got)
    sum_up = lax.ppermute(to_up, "head", up)
    sum_down = lax.ppermute(to_down, "head", down)
    sum_far = lax.ppermute(to_far, "head", across)
    query_grad = call(
        query_side,
        shape(query.shape, bf16),
        score_grad,
        all_keys,
        scratch=(pltpu.VMEM((rows, width), f32),),
        flops=3 * 10**9,
        traffic=10**7,
    )
    outbox = call(
        outgoing, shape((slots, line), bf16), back, keep, got, sum_up, sum_down, sum_far
    )
    inbox = swap(outbox, "ctx")
    totals = call(multiply, shape((n_head * CAP * LINES, line), bf16), sums, inbox)
    spread = swap(totals, "head")
    grad_latent = call(place, shape((outs, width), f32), places, spread)
    return (query_grad, grad_latent)


def solution(mesh):
    return jax.shard_map(
        local,
        mesh=mesh,
        in_specs=(P("ctx", None), P("ctx", "head"), P("ctx", "head"), P("ctx", None)),
        out_specs=(P("ctx", "head"), P(("ctx", "head"), None)),
        check_vma=False,
    )
```

time: 171 us -> 162 us (0.947)
  waiting for transfers between devices: 61.5 us -> 56.1 us
  blocking collectives: 23.5 us -> 21.7 us
    all_to_all x3, waiting for transfers between devices: 29.6 us -> 26.2 us  [swap(): lax.all_to_all(x3, axis, split_axis=0, concat_axis=0, tiled=True)]
    all_to_all x1, blocking collectives: 23.5 us -> 21.7 us  [swap(): lax.all_to_all(x3, axis, split_axis=0, concat_axis=0, tiled=True)]
    pallas_call x10 -> x11, Pallas kernels: 24.8 us -> 23.3 us  [call(): pl.pallas_call(body, out_shape=out_shape, in_specs=specs, out_specs=jax.t...]
  transfers between devices with their start and end apart: 11 -> 11, of which waited for: 11 -> 11; matrix products, arithmetic and copies ran while one was open for 1% -> 1% of each run, Pallas kernels for 3% -> 4%
where the time goes in v3:
time: 162 us; the launch traced here: 161 us
  waiting for transfers between devices  56.1 us (35%)
  starting transfers between devices  53.7 us (33%)
  Pallas kernels  23.3 us (14%)
  blocking collectives  21.7 us (13%)
  local copies, waits for them, and re-layouts  5.48 us (3%)
    all_to_all x3, waiting for transfers between devices, swap(): lax.all_to_all(x3, axis, split_axis=0, concat_axis=0, tiled=True)  26.2 us
    pallas_call x11, Pallas kernels, call(): pl.pallas_call(body, out_shape=out_shape, in_specs=specs, out_specs=jax.t...  23.3 us
    all_to_all x3, starting transfers between devices, swap(): lax.all_to_all(x3, axis, split_axis=0, concat_axis=0, tiled=True)  21.8 us
    all_to_all x1, blocking collectives, swap(): lax.all_to_all(x3, axis, split_axis=0, concat_axis=0, tiled=True)  21.7 us
    ppermute x1, starting transfers between devices, local(): from_far = lax.ppermute(mine, 'head', across)  10.6 us
    ppermute x1, waiting for transfers between devices, local(): sum_far = lax.ppermute(to_far, 'head', across)  7.94 us
    ppermute x1, waiting for transfers between devices, local(): from_above = lax.ppermute(mine, 'head', down)  6.96 us
    unnamed x15, local copies, waits for them, and re-layouts  5.48 us
  transfers between devices with their start and end apart: 11, of which 11 were waited for; matrix products, arithmetic and copies ran while one was open for 1% of the time, Pallas kernels for 4%

profile of v3, /device:TPU:1, one launch (start us, length us, event | category | flops | bytes accessed | tf_op | source)
XLA Modules:
  0.0 161.3 jit_solution(17436040593602379896)
XLA Ops:
  1.3 2.3 %shard_map.59 = (bf16[640,128]{1,0:T(8,128)(2,1)S(1)}, f32[16,640]{1,0:T(8,128)S(1)}, bf16[256,128]{1,0:T(8,128)(2,1)}) custom-call(s32[32,128]{1,0:T(8,128)S(1)} %bitcast.29), custom_call_target="tpu_custom_call" | custom-call | tf_op jit(solution)/shard_map/pallas_call | solution.py:37
  3.7 10.5 %all-to-all-start = ((bf16[32,8,128]{2,1,0:T(8,128)(2,1)}), bf16[32,8,128]{2,1,0:T(8,128)(2,1)S(1)}, u32[]{:S(2)}, u32[]{:S(2)}) async-start(bf16[32,8,128]{2,1,0:T(8,128)(2,1)} %bitcast.3), calls=%async_computation | async-start | bytes 131072 | tf_op jit(solution)/shard_map/all_to_all | solution.py:286
  14.3 1.9 %copy.6.lat_ref = bf16[1280,576]{1,0:T(8,128)(2,1)S(1)} copy(bf16[1280,576]{0,1:T(8,128)(2,1)} %param.4) | data formatting | bytes 2949120 | tf_op args[0]
  16.2 1.3 shard_map.61.own_ref
  17.5 5.6 %all-to-all-done = bf16[32,8,128]{2,1,0:T(8,128)(2,1)S(1)} async-done(((bf16[32,8,128]{2,1,0:T(8,128)(2,1)}), bf16[32,8,128]{2,1,0:T(8,128)(2,1)S(1)}, u32[]{:S(2)}, u32[]{:S(2)}) %all-to-all-start) | async-done | bytes 65568 | tf_op jit(solution)/shard_map/all_to_all | solution.py:286
  23.0 1.2 shard_map.62
  24.2 3.9 %all-to-all-start.1 = ((bf16[32,8,1152]{2,1,0:T(8,128)(2,1)}), bf16[32,8,1152]{2,1,0:T(8,128)(2,1)S(1)}, u32[]{:S(2)}, u32[]{:S(2)}) async-start(bf16[32,8,1152]{2,1,0:T(8,128)(2,1)} %bitcast.5), calls=%async_computation.1 | async-start | bytes 1179648 | tf_op jit(solution)/shard_map/all_to_all | solution.py:286
  28.1 1.2 shard_map.60
  29.4 1.0 copy-done.5
  30.4 13.6 %all-to-all-done.1 = bf16[32,8,1152]{2,1,0:T(8,128)(2,1)S(1)} async-done(((bf16[32,8,1152]{2,1,0:T(8,128)(2,1)}), bf16[32,8,1152]{2,1,0:T(8,128)(2,1)S(1)}, u32[]{:S(2)}, u32[]{:S(2)}) %all-to-all-start.1) | async-done | bytes 589856 | tf_op jit(solution)/shard_map/all_to_all | solution.py:286
  44.3 10.6 %collective-permute-start.2 = (bf16[144,1152]{1,0:T(8,128)(2,1)S(1)}, bf16[144,1152]{1,0:T(8,128)(2,1)S(1)}, u32[]{:S(2)}, u32[]{:S(2)}) collective-permute-start(bf16[144,1152]{1,0:T(8,128)(2,1)S(1)} %shard_map.63), channel_id=1, source_target_pairs={{0,4},{1,13},{2,6},{3,15},{4,8},{5,1},{6,10},{7,3},{8,12},{9,5},{1... | collective-permute-start | bytes 995336 | tf_op jit(solution)/shard_map/ppermute | solution.py:316
  54.9 2.2 %collective-permute-start.1 = (bf16[144,1152]{1,0:T(8,128)(2,1)S(1)}, bf16[144,1152]{1,0:T(8,128)(2,1)S(1)}, u32[]{:S(2)}, u32[]{:S(2)}) collective-permute-start(bf16[144,1152]{1,0:T(8,128)(2,1)S(1)} %shard_map.63), channel_id=1, source_target_pairs={{0,14},{1,15},{2,0},{3,1},{4,2},{5,3},{6,4},{7,5},{8,6},{9,7},{10,... | collective-permute-start | bytes 995336 | tf_op jit(solution)/shard_map/ppermute | solution.py:315
  57.1 3.1 %collective-permute-start = (bf16[144,1152]{1,0:T(8,128)(2,1)S(1)}, bf16[144,1152]{1,0:T(8,128)(2,1)S(1)}, u32[]{:S(2)}, u32[]{:S(2)}) collective-permute-start(bf16[144,1152]{1,0:T(8,128)(2,1)S(1)} %shard_map.63), channel_id=1, source_target_pairs={{0,2},{1,3},{2,4},{3,5},{4,6},{5,7},{6,8},{7,9},{8,10},{9,11},{10,... | collective-permute-start | bytes 995336 | tf_op jit(solution)/shard_map/ppermute | solution.py:314
  60.2 2.4 %collective-permute-done.2 = bf16[144,1152]{1,0:T(8,128)(2,1)S(1)} collective-permute-done((bf16[144,1152]{1,0:T(8,128)(2,1)S(1)}, bf16[144,1152]{1,0:T(8,128)(2,1)S(1)}, u32[]{:S(2)}, u32[]{:S(2)}) %collective-permute-start.2) | collective-permute-done | bytes 331808 | tf_op jit(solution)/shard_map/ppermute | solution.py:316
  62.7 7.0 %collective-permute-done.1 = bf16[144,1152]{1,0:T(8,128)(2,1)S(1)} collective-permute-done((bf16[144,1152]{1,0:T(8,128)(2,1)S(1)}, bf16[144,1152]{1,0:T(8,128)(2,1)S(1)}, u32[]{:S(2)}, u32[]{:S(2)}) %collective-permute-start.1) | collective-permute-done | bytes 331808 | tf_op jit(solution)/shard_map/ppermute | solution.py:315
  69.6 2.4 %collective-permute-done = bf16[144,1152]{1,0:T(8,128)(2,1)S(1)} collective-permute-done((bf16[144,1152]{1,0:T(8,128)(2,1)S(1)}, bf16[144,1152]{1,0:T(8,128)(2,1)S(1)}, u32[]{:S(2)}, u32[]{:S(2)}) %collective-permute-start) | collective-permute-done | bytes 331808 | tf_op jit(solution)/shard_map/ppermute | solution.py:314
  72.2 5.3 %collective-permute-start.3 = (bf16[4,144,1152]{2,1,0:T(8,128)(2,1)S(1)}, bf16[4,144,1152]{2,1,0:T(8,128)(2,1)S(1)}, u32[]{:S(2)}, u32[]{:S(2)}) collective-permute-start(bf16[4,144,1152]{2,1,0:T(8,128)(2,1)S(1)} %pad_maximum_fusion), channel_id=1, source_target_pairs={{0,1},{1,0},{2,3},{3,2},{4,5},{5,4},{6,7},{7,6},{8,9},{9,8},{10,11... | collective-permute-start | bytes 3981320 | tf_op jit(solution)/shard_map/ppermute | solution.py:318
  77.5 2.7 %collective-permute-done.3 = bf16[4,144,1152]{2,1,0:T(8,128)(2,1)S(1)} collective-permute-done((bf16[4,144,1152]{2,1,0:T(8,128)(2,1)S(1)}, bf16[4,144,1152]{2,1,0:T(8,128)(2,1)S(1)}, u32[]{:S(2)}, u32[]{:S(2)}) %collective-permute-start.3) | collective-permute-done | bytes 1327136 | tf_op jit(solution)/shard_map/ppermute | solution.py:318
  80.2 10.9 %shard_map.64 = (f32[576,1152]{1,0:T(8,128)S(1)}, bf16[576,1152]{1,0:T(8,128)(2,1)S(1)}, bf16[2304,512]{1,0:T(8,128)(2,1)S(1)}, bf16[2304,576]{1,0:T(8,128)(2,1)S(1)}) custom-call(bf16[576,1152]{1,0:T(8,128)(2,1)S(1)} %bitcast.24, bf16[576,1152]{1,0:T(8,128)(2,1)S(1)} %bitcast.31, bf16[128,2304]{1,0:T(8,128)(2,1)S(1)} %copy-done.1, ...), custom_call_target="tpu_custom_call" | custom-call | flops 6000000000 | bytes 10000000 | tf_op jit(solution)/shard_map/pallas_call | solution.py:37
  91.1 2.3 %collective-permute-start.4 = (bf16[4,144,1152]{2,1,0:T(8,128)(2,1)S(1)}, bf16[4,144,1152]{2,1,0:T(8,128)(2,1)S(1)}, u32[]{:S(2)}, u32[]{:S(2)}) collective-permute-start(bf16[4,144,1152]{2,1,0:T(8,128)(2,1)S(1)} %bitcast.30), channel_id=1, source_target_pairs={{0,1},{1,0},{2,3},{3,2},{4,5},{5,4},{6,7},{7,6},{8,9},{9,8},{10,11... | collective-permute-start | bytes 3981320 | tf_op jit(solution)/shard_map/ppermute | solution.py:344
  93.4 2.7 %collective-permute-done.4 = bf16[4,144,1152]{2,1,0:T(8,128)(2,1)S(1)} collective-permute-done((bf16[4,144,1152]{2,1,0:T(8,128)(2,1)S(1)}, bf16[4,144,1152]{2,1,0:T(8,128)(2,1)S(1)}, u32[]{:S(2)}, u32[]{:S(2)}) %collective-permute-start.4) | collective-permute-done | bytes 1327136 | tf_op jit(solution)/shard_map/ppermute | solution.py:344
  96.3 1.9 %collective-permute-start.5 = (bf16[144,1152]{1,0:T(8,128)(2,1)S(1)}, bf16[144,1152]{1,0:T(8,128)(2,1)S(1)}, u32[]{:S(2)}, u32[]{:S(2)}) collective-permute-start(bf16[144,1152]{1,0:T(8,128)(2,1)S(1)} %get-tuple-element.29), channel_id=1, source_target_pairs={{0,2},{1,3},{2,4},{3,5},{4,6},{5,7},{6,8},{7,9},{8,10},{9,11},{10,... | collective-permute-start | bytes 995336 | tf_op jit(solution)/shard_map/ppermute | solution.py:348
  98.2 4.6 %collective-permute-start.6 = (bf16[144,1152]{1,0:T(8,128)(2,1)S(1)}, bf16[144,1152]{1,0:T(8,128)(2,1)S(1)}, u32[]{:S(2)}, u32[]{:S(2)}) collective-permute-start(bf16[144,1152]{1,0:T(8,128)(2,1)S(1)} %get-tuple-element.30), channel_id=1, source_target_pairs={{0,14},{1,15},{2,0},{3,1},{4,2},{5,3},{6,4},{7,5},{8,6},{9,7},{10,... | collective-permute-start | bytes 995336 | tf_op jit(solution)/shard_map/ppermute | solution.py:349
  102.8 1.9 %collective-permute-start.7 = (bf16[144,1152]{1,0:T(8,128)(2,1)S(1)}, bf16[144,1152]{1,0:T(8,128)(2,1)S(1)}, u32[]{:S(2)}, u32[]{:S(2)}) collective-permute-start(bf16[144,1152]{1,0:T(8,128)(2,1)S(1)} %get-tuple-element.31), channel_id=1, source_target_pairs={{0,4},{1,13},{2,6},{3,15},{4,8},{5,1},{6,10},{7,3},{8,12},{9,5},{1... | collective-permute-start | bytes 995336 | tf_op jit(solution)/shard_map/ppermute | solution.py:350
  104.7 3.7 %collective-permute-done.5.up_ref = bf16[144,1152]{1,0:T(8,128)(2,1)S(1)} collective-permute-done((bf16[144,1152]{1,0:T(8,128)(2,1)S(1)}, bf16[144,1152]{1,0:T(8,128)(2,1)S(1)}, u32[]{:S(2)}, u32[]{:S(2)}) %collective-permute-start.5) | collective-permute-done | bytes 331808 | tf_op jit(solution)/shard_map/ppermute | solution.py:348
  108.4 1.1 collective-permute-done.6.down_ref
  109.5 7.9 %collective-permute-done.7.far_ref = bf16[144,1152]{1,0:T(8,128)(2,1)S(1)} collective-permute-done((bf16[144,1152]{1,0:T(8,128)(2,1)S(1)}, bf16[144,1152]{1,0:T(8,128)(2,1)S(1)}, u32[]{:S(2)}, u32[]{:S(2)}) %collective-permute-start.7) | collective-permute-done | bytes 331808 | tf_op jit(solution)/shard_map/ppermute | solution.py:350
  118.0 21.7 %all_to_all.20 = bf16[32,8,1152]{2,1,0:T(8,128)(2,1)S(1)} all-to-all(bf16[32,8,1152]{2,1,0:T(8,128)(2,1)S(1)} %bitcast.21), channel_id=1, replica_groups=mesh['ctx'=32,'head'=16] {'ctx'}, dimensions={0} | all-to-all | bytes 1179648 | tf_op jit(solution)/shard_map/all_to_all | solution.py:286
  140.6 7.4 %all-to-all-start.3 = ((bf16[16,8,1152]{2,1,0:T(8,128)(2,1)}), bf16[16,8,1152]{2,1,0:T(8,128)(2,1)S(1)}, u32[]{:S(2)}, u32[]{:S(2)}) async-start(bf16[16,8,1152]{2,1,0:T(8,128)(2,1)} %bitcast.17), calls=%async_computation.3 | async-start | bytes 589824 | tf_op jit(solution)/shard_map/all_to_all | solution.py:286
  148.0 1.8 %copy-done.4 = bf16[2304,576]{1,0:T(8,128)(2,1)S(1)} copy-done((bf16[2304,576]{1,0:T(8,128)(2,1)S(1)}, bf16[2304,576]{1,0:T(8,128)(2,1)}, u32[]{:S(2)}) %copy-start.4) | copy-done | bytes 2654232
  149.8 3.5 %shard_map.65 = bf16[128,2304]{1,0:T(8,128)(2,1)} custom-call(bf16[2304,512]{1,0:T(8,128)(2,1)S(1)} %get-tuple-element.22.ds_ref, bf16[2304,576]{1,0:T(8,128)(2,1)S(1)} %copy-done.4), custom_call_target="tpu_custom_call" | custom-call | flops 3000000000 | bytes 10000000 | tf_op jit(solution)/shard_map/pallas_call | solution.py:37
  153.3 7.0 %all-to-all-done.3 = bf16[16,8,1152]{2,1,0:T(8,128)(2,1)S(1)} async-done(((bf16[16,8,1152]{2,1,0:T(8,128)(2,1)}), bf16[16,8,1152]{2,1,0:T(8,128)(2,1)S(1)}, u32[]{:S(2)}, u32[]{:S(2)}) %all-to-all-start.3) | async-done | bytes 294944 | tf_op jit(solution)/shard_map/all_to_all | solution.py:286
  (19 shorter events, 3.8 us)
Async XLA Ops:
  0.6 0.7 copy-start
  3.7 19.3 %all-to-all-start = ((bf16[32,8,128]{2,1,0:T(8,128)(2,1)}), bf16[32,8,128]{2,1,0:T(8,128)(2,1)S(1)}, u32[]{:S(2)}, u32[]{:S(2)}) async-start(bf16[32,8,128]{2,1,0:T(8,128)(2,1)} %bitcast.3), calls=%async_computation | async-start | bytes 131072 | tf_op jit(solution)/shard_map/all_to_all | solution.py:286
  24.2 19.8 %all-to-all-start.1 = ((bf16[32,8,1152]{2,1,0:T(8,128)(2,1)}), bf16[32,8,1152]{2,1,0:T(8,128)(2,1)S(1)}, u32[]{:S(2)}, u32[]{:S(2)}) async-start(bf16[32,8,1152]{2,1,0:T(8,128)(2,1)} %bitcast.5), calls=%async_computation.1 | async-start | bytes 1179648 | tf_op jit(solution)/shard_map/all_to_all | solution.py:286
  29.4 1.0 copy-start.5
  44.3 18.4 %collective-permute-start.2 = (bf16[144,1152]{1,0:T(8,128)(2,1)S(1)}, bf16[144,1152]{1,0:T(8,128)(2,1)S(1)}, u32[]{:S(2)}, u32[]{:S(2)}) collective-permute-start(bf16[144,1152]{1,0:T(8,128)(2,1)S(1)} %shard_map.63), channel_id=1, source_target_pairs={{0,4},{1,13},{2,6},{3,15},{4,8},{5,1},{6,10},{7,3},{8,12},{9,5},{1... | collective-permute-start | bytes 995336 | tf_op jit(solution)/shard_map/ppermute | solution.py:316
  54.9 14.7 %collective-permute-start.1 = (bf16[144,1152]{1,0:T(8,128)(2,1)S(1)}, bf16[144,1152]{1,0:T(8,128)(2,1)S(1)}, u32[]{:S(2)}, u32[]{:S(2)}) collective-permute-start(bf16[144,1152]{1,0:T(8,128)(2,1)S(1)} %shard_map.63), channel_id=1, source_target_pairs={{0,14},{1,15},{2,0},{3,1},{4,2},{5,3},{6,4},{7,5},{8,6},{9,7},{10,... | collective-permute-start | bytes 995336 | tf_op jit(solution)/shard_map/ppermute | solution.py:315
  57.1 14.9 %collective-permute-start = (bf16[144,1152]{1,0:T(8,128)(2,1)S(1)}, bf16[144,1152]{1,0:T(8,128)(2,1)S(1)}, u32[]{:S(2)}, u32[]{:S(2)}) collective-permute-start(bf16[144,1152]{1,0:T(8,128)(2,1)S(1)} %shard_map.63), channel_id=1, source_target_pairs={{0,2},{1,3},{2,4},{3,5},{4,6},{5,7},{6,8},{7,9},{8,10},{9,11},{10,... | collective-permute-start | bytes 995336 | tf_op jit(solution)/shard_map/ppermute | solution.py:314
  72.0 8.2 %copy-start.1 = (bf16[128,2304]{1,0:T(8,128)(2,1)S(1)}, bf16[128,2304]{1,0:T(8,128)(2,1)}, u32[]{:S(2)}) copy-start(bf16[128,2304]{1,0:T(8,128)(2,1)} %q_ref.1) | copy-start | bytes 1769476
  72.0 8.2 %copy-start.2 = (bf16[128,2048]{1,0:T(8,128)(2,1)S(1)}, bf16[128,2048]{1,0:T(8,128)(2,1)}, u32[]{:S(2)}) copy-start(bf16[128,2048]{1,0:T(8,128)(2,1)} %g_ref.1) | copy-start | bytes 1572868
  72.0 8.2 %copy-start.6 = (f32[2304,128]{1,0:T(8,128)S(1)}, f32[2304,128]{1,0:T(8,128)}, u32[]{:S(2)}) copy-start(f32[2304,128]{1,0:T(8,128)} %copy-done.5) | copy-start | bytes 3538948
  72.2 8.0 %collective-permute-start.3 = (bf16[4,144,1152]{2,1,0:T(8,128)(2,1)S(1)}, bf16[4,144,1152]{2,1,0:T(8,128)(2,1)S(1)}, u32[]{:S(2)}, u32[]{:S(2)}) collective-permute-start(bf16[4,144,1152]{2,1,0:T(8,128)(2,1)S(1)} %pad_maximum_fusion), channel_id=1, source_target_pairs={{0,1},{1,0},{2,3},{3,2},{4,5},{5,4},{6,7},{7,6},{8,9},{9,8},{10,11... | collective-permute-start | bytes 3981320 | tf_op jit(solution)/shard_map/ppermute | solution.py:318
  91.1 5.1 %copy-start.3 = (bf16[2304,576]{1,0:T(8,128)(2,1)}, bf16[2304,576]{1,0:T(8,128)(2,1)S(1)}, u32[]{:S(2)}) copy-start(bf16[2304,576]{1,0:T(8,128)(2,1)S(1)} %get-tuple-element.23.k_ref) | copy-start | bytes 7962628
  91.1 5.0 %collective-permute-start.4 = (bf16[4,144,1152]{2,1,0:T(8,128)(2,1)S(1)}, bf16[4,144,1152]{2,1,0:T(8,128)(2,1)S(1)}, u32[]{:S(2)}, u32[]{:S(2)}) collective-permute-start(bf16[4,144,1152]{2,1,0:T(8,128)(2,1)S(1)} %bitcast.30), channel_id=1, source_target_pairs={{0,1},{1,0},{2,3},{3,2},{4,5},{5,4},{6,7},{7,6},{8,9},{9,8},{10,11... | collective-permute-start | bytes 3981320 | tf_op jit(solution)/shard_map/ppermute | solution.py:344
  96.3 12.1 %collective-permute-start.5 = (bf16[144,1152]{1,0:T(8,128)(2,1)S(1)}, bf16[144,1152]{1,0:T(8,128)(2,1)S(1)}, u32[]{:S(2)}, u32[]{:S(2)}) collective-permute-start(bf16[144,1152]{1,0:T(8,128)(2,1)S(1)} %get-tuple-element.29), channel_id=1, source_target_pairs={{0,2},{1,3},{2,4},{3,5},{4,6},{5,7},{6,8},{7,9},{8,10},{9,11},{10,... | collective-permute-start | bytes 995336 | tf_op jit(solution)/shard_map/ppermute | solution.py:348
  98.2 11.3 %collective-permute-start.6 = (bf16[144,1152]{1,0:T(8,128)(2,1)S(1)}, bf16[144,1152]{1,0:T(8,128)(2,1)S(1)}, u32[]{:S(2)}, u32[]{:S(2)}) collective-permute-start(bf16[144,1152]{1,0:T(8,128)(2,1)S(1)} %get-tuple-element.30), channel_id=1, source_target_pairs={{0,14},{1,15},{2,0},{3,1},{4,2},{5,3},{6,4},{7,5},{8,6},{9,7},{10,... | collective-permute-start | bytes 995336 | tf_op jit(solution)/shard_map/ppermute | solution.py:349
  102.8 14.7 %collective-permute-start.7 = (bf16[144,1152]{1,0:T(8,128)(2,1)S(1)}, bf16[144,1152]{1,0:T(8,128)(2,1)S(1)}, u32[]{:S(2)}, u32[]{:S(2)}) collective-permute-start(bf16[144,1152]{1,0:T(8,128)(2,1)S(1)} %get-tuple-element.31), channel_id=1, source_target_pairs={{0,4},{1,13},{2,6},{3,15},{4,8},{5,1},{6,10},{7,3},{8,12},{9,5},{1... | collective-permute-start | bytes 995336 | tf_op jit(solution)/shard_map/ppermute | solution.py:350
  140.6 19.7 %all-to-all-start.3 = ((bf16[16,8,1152]{2,1,0:T(8,128)(2,1)}), bf16[16,8,1152]{2,1,0:T(8,128)(2,1)S(1)}, u32[]{:S(2)}, u32[]{:S(2)}) async-start(bf16[16,8,1152]{2,1,0:T(8,128)(2,1)} %bitcast.17), calls=%async_computation.3 | async-start | bytes 589824 | tf_op jit(solution)/shard_map/all_to_all | solution.py:286
  148.0 1.8 %copy-start.4 = (bf16[2304,576]{1,0:T(8,128)(2,1)S(1)}, bf16[2304,576]{1,0:T(8,128)(2,1)}, u32[]{:S(2)}) copy-start(bf16[2304,576]{1,0:T(8,128)(2,1)} %copy-done.3) | copy-start | bytes 7962628

commit v4 on v3

--- a/solution.py
+++ b/solution.py
@@ -53,10 +53,8 @@
     return head & 7
 
 
-def near(head, core_flip, step):
-    z = head >> 1
-    core = (head & 1) ^ core_flip
-    return 2 * ((z + step) & 3) + core
+def near(head, step):
+    return 2 * (((head >> 1) + step) & 3) + (head & 1)
 
 
 def one_hot(mask):
@@ -126,13 +124,12 @@
     query_pos = first + pos_ref[0] * queries + iota((rows, queries), 1)
     base = block_id * BLOCK + (iota((rows, queries), 0) & 3) - query_pos
     piece = 0
-    for flip in (0, 1):
-        for u in (0, 1):
-            for step in (0, -1, 1, 2):
-                offset = near(head, flip, step) * PART + u * LINES
-                allowed = jnp.logical_and(picked > 0.5, base + offset <= 0)
-                bias_ref[piece * rows : (piece + 1) * rows, :] = jnp.where(allowed, 0.0, NEG)
-                piece += 1
+    for u in (0, 1):
+        for step in (0, -1, 1, 2):
+            offset = near(head, step) * PART + u * LINES
+            allowed = jnp.logical_and(picked > 0.5, base + offset <= 0)
+            bias_ref[piece * rows : (piece + 1) * rows, :] = jnp.where(allowed, 0.0, NEG)
+            piece += 1
     row = iota(send_ref.shape, 0)
     col = iota(send_ref.shape, 1)
     send = one_hot(col == (by20(block_id) * CAP + block_rank) * LINES + (row & 3))
@@ -163,19 +160,24 @@
     out_ref[...] = dot(a_ref[...], b_ref[...], 1, 0).astype(out_ref.dtype)
 
 
-def attend(
-    ka_ref, kb_ref, q_ref, g_ref, bias_ref, keep_ref, give_ref, ds_ref, k_ref, s_ref, d_ref, qs_ref, gs_ref
+def score(
+    own_ref, below_ref, above_ref, far_ref, q_ref, g_ref, qt_ref, gt_ref, bias_ref,
+    e_ref, d_ref, stat_ref, k_ref, qs_ref, gs_ref,
 ):
     tokens, width = k_ref.shape
     queries = q_ref.shape[0]
     heads = g_ref.shape[1] // LAT
-    cols = heads * queries
-    quarter = tokens // 4
-    for i, (piece_ref, u) in enumerate(((ka_ref, 0), (ka_ref, 1), (kb_ref, 0), (kb_ref, 1))):
-        k_ref[i * quarter : (i + 1) * quarter, :] = piece_ref[:, u * width : (u + 1) * width]
-    for h in range(heads):
-        qs_ref[h * queries : (h + 1) * queries, :] = q_ref[:, h * width : (h + 1) * width]
-        gs_ref[h * queries : (h + 1) * queries, :] = g_ref[:, h * LAT : (h + 1) * LAT]
+    cols = 2 * heads * queries
+    lines = own_ref.shape[0]
+    for u in (0, 1):
+        for i, piece_ref in enumerate((own_ref, below_ref, above_ref, far_ref)):
+            at = (4 * u + i) * lines
+            k_ref[at : at + lines, :] = piece_ref[:, u * width : (u + 1) * width]
+    for c, (x_ref, y_ref) in enumerate(((q_ref, g_ref), (qt_ref, gt_ref))):
+        for h in range(heads):
+            at = (c * heads + h) * queries
+            qs_ref[at : at + queries, :] = x_ref[:, h * width : (h + 1) * width]
+            gs_ref[at : at + queries, :] = y_ref[:, h * LAT : (h + 1) * LAT]
     step = 384
 
     def fold(x):
@@ -184,9 +186,9 @@
     def one(i, top):
         at = pl.ds(pl.multiple_of(i * step, step), step)
         keys = k_ref[at, :]
-        bias = bias_ref[at, :]
-        s = dot(keys, qs_ref[...], 1, 1) * score_scale + jnp.concatenate([bias] * heads, axis=1)
-        s_ref[at, :] = s
+        bias = jnp.concatenate([bias_ref[at, :]] * (2 * heads), axis=1)
+        s = dot(keys, qs_ref[...], 1, 1) * score_scale + bias
+        e_ref[at, :] = s
         d_ref[at, :] = dot(keys[:, :LAT], gs_ref[...], 1, 1)
         return jnp.maximum(top, jnp.max(s.reshape(step // 8, 8, cols), axis=0))
 
@@ -196,37 +198,53 @@
     def two(i, carry):
         total, mixed = carry
         at = pl.ds(pl.multiple_of(i * step, step), step)
-        e = jnp.exp(s_ref[at, :] - top)
-        s_ref[at, :] = e
+        e = jnp.exp(e_ref[at, :] - top)
+        e_ref[at, :] = e
         return total + fold(e), mixed + fold(e * d_ref[at, :])
 
     zero = jnp.zeros((8, cols), f32)
     total, mixed = lax.fori_loop(0, tokens // step, two, (zero, zero))
-    inv = 1.0 / jnp.sum(total, axis=0, keepdims=True)
-    delta = jnp.sum(mixed, axis=0, keepdims=True) * inv
-    less = quarter // 2
-    for i, (out_ref, u) in enumerate(((keep_ref, 0), (keep_ref, 1), (give_ref, 0), (give_ref, 1))):
-
-        def three(j, carry, i=i, out_ref=out_ref, u=u):
-            here = pl.ds(pl.multiple_of(j * less, less), less)
-            at = pl.ds(pl.multiple_of(i * quarter + j * less, less), less)
-            p = s_ref[at, :] * inv
-            ds = (p * (d_ref[at, :] - delta)).astype(bf16)
-            ds_ref[at, :] = ds
-            dk = dot(ds, qs_ref[...], 1, 0) * score_scale
-            dv = dot(p.astype(bf16), gs_ref[...], 1, 0)
-            both = jnp.concatenate([dk[:, :LAT] + dv, dk[:, LAT:]], axis=1)
-            out_ref[here, u * width : (u + 1) * width] = both.astype(out_ref.dtype)
-            return carry
-
-        lax.fori_loop(0, 2, three, 0)
-
-
-def query_side(ds_ref, k_ref, dq_ref, dqs_ref):
+    stat_ref[0:1, :] = top
+    stat_ref[1:2, :] = jnp.sum(total, axis=0, keepdims=True)
+    stat_ref[2:3, :] = jnp.sum(mixed, axis=0, keepdims=True)
+    stat_ref[3:8, :] = jnp.zeros((5, cols), f32)
+
+
+def key_side(
+    e_ref, d_ref, stat_ref, other_ref, qs_ref, gs_ref, own_ref, down_ref, up_ref, far_ref, ds_ref
+):
+    tokens, cols = e_ref.shape
+    width = qs_ref.shape[1]
+    lines = own_ref.shape[0]
+    mine = stat_ref[...]
+    other = other_ref[...]
+    other = jnp.concatenate([other[:, cols // 2 :], other[:, : cols // 2]], axis=1)
+    top = jnp.maximum(mine[0:1], other[0:1])
+    a, b = jnp.exp(mine[0:1] - top), jnp.exp(other[0:1] - top)
+    inv = 1.0 / (mine[1:2] * a + other[1:2] * b)
+    delta = (mine[2:3] * a + other[2:3] * b) * inv
+    scale = a * inv
+    outs = (own_ref, down_ref, up_ref, far_ref)
+    step = 2 * lines
+    for i in range(tokens // step):
+        at = slice(i * step, (i + 1) * step)
+        u = i // 2
+        p = e_ref[at, :] * scale
+        ds = (p * (d_ref[at, :] - delta)).astype(bf16)
+        ds_ref[at, :] = ds
+        dk = dot(ds, qs_ref[...], 1, 0) * score_scale
+        dv = dot(p.astype(bf16), gs_ref[...], 1, 0)
+        both = jnp.concatenate([dk[:, :LAT] + dv, dk[:, LAT:]], axis=1)
+        for j in (0, 1):
+            out_ref = outs[2 * (i % 2) + j]
+            part = both[j * lines : (j + 1) * lines, :]
+            out_ref[:, u * width : (u + 1) * width] = part.astype(out_ref.dtype)
+
+
+def query_side(ds_ref, k_ref, mine_ref, other_ref, dqs_ref):
     tokens, width = k_ref.shape
-    queries = dq_ref.shape[0]
-    heads = dq_ref.shape[1] // width
-    step = 768
+    rows = mine_ref.shape[0]
+    step = 384
     dqs_ref[...] = jnp.zeros_like(dqs_ref)
 
     def one(i, carry):
@@ -235,21 +253,26 @@
         return carry
 
     lax.fori_loop(0, tokens // step, one, 0)
+    for i, out_ref in enumerate((mine_ref, other_ref)):
+        for u in (0, 1):
+            at = (2 * i + u) * rows
+            out_ref[:, u * width : (u + 1) * width] = dqs_ref[at : at + rows, :]
+
+
+def query_sum(mine_ref, got_ref, dq_ref):
+    queries = dq_ref.shape[0]
+    heads, line = mine_ref.shape[0] // queries, mine_ref.shape[1]
+    width = line // 2
     for h in range(heads):
-        part = dqs_ref[h * queries : (h + 1) * queries, :] * score_scale
-        dq_ref[:, h * width : (h + 1) * width] = part.astype(bf16)
-
-
-def merge(keep_ref, got_ref, down_ref, up_ref, far_ref):
-    rows = down_ref.shape[0]
-    for i, out_ref in enumerate((down_ref, up_ref, far_ref)):
-        at = slice((i + 1) * rows, (i + 2) * rows)
-        out_ref[...] = (keep_ref[at, :] + got_ref[at, :].astype(f32)).astype(bf16)
-
-
-def outgoing(back_ref, keep_ref, got_ref, up_ref, down_ref, far_ref, out_ref):
-    rows = up_ref.shape[0]
-    total = keep_ref[:rows, :] + got_ref[:rows, :].astype(f32) + up_ref[...].astype(f32)
+        at = slice(h * queries, (h + 1) * queries)
+        total = ((mine_ref[at, :] + got_ref[at, :]) * score_scale).astype(bf16)
+        dq_ref[:, h * width : (h + 1) * width] = total[:, :width]
+        h2 = h + heads
+        dq_ref[:, h2 * width : (h2 + 1) * width] = total[:, width:]
+
+
+def outgoing(back_ref, own_ref, up_ref, down_ref, far_ref, out_ref):
+    total = own_ref[...] + up_ref[...].astype(f32)
     total = total + down_ref[...].astype(f32) + far_ref[...].astype(f32)
     out_ref[...] = dot(back_ref[...], total.astype(bf16), 1, 0).astype(bf16)
 
@@ -270,7 +293,7 @@
     line = 2 * width
     pool_lines = POOL * LINES
     slots = n_ctx * CAP * LINES
-    tokens = POOL * BLOCK
+    tokens = POOL * BLOCK // 2
     outs = ctx_rows // n_head
     pos = jnp.stack([lax.axis_index("ctx"), lax.axis_index("head")]).astype(jnp.int32)
     first = (ctx_rows - queries) * n_ctx
@@ -309,57 +332,69 @@
         flops=3 * 10**9,
         traffic=3 * 10**6,
     )
+    query, grad_out, bias = lax.optimization_barrier((query, grad_out, bias))
+    twin_query = lax.ppermute(query, "head", twin)
+    twin_grad = lax.ppermute(grad_out, "head", twin)
     lines_in = swap(lines_out, "ctx")
     mine = call(multiply, shape((pool_lines, line), bf16), send, lines_in)
     from_below = lax.ppermute(mine, "head", up)
     from_above = lax.ppermute(mine, "head", down)
     from_far = lax.ppermute(mine, "head", across)
-    keys = jnp.stack([mine, from_below, from_above, from_far])
-    twin_keys = lax.ppermute(keys, "head", twin).reshape(4 * pool_lines, line)
-    keys = keys.reshape(4 * pool_lines, line)
     rows = queries * (grad_out.shape[1] // LAT)
-    keep, give, score_grad, all_keys = call(
-        attend,
+    scores, prob_grad, stats, keys, query_rows, grad_rows = call(
+        score,
         (
-            shape((4 * pool_lines, line), f32),
-            shape((4 * pool_lines, line), bf16),
-            shape((tokens, rows), bf16),
+            shape((tokens, 2 * rows), f32),
+            shape((tokens, 2 * rows), f32),
+            shape((8, 2 * rows), f32),
             shape((tokens, width), bf16),
+            shape((2 * rows, width), bf16),
+            shape((2 * rows, LAT), bf16),
         ),
-        keys,
-        twin_keys,
+        mine,
+        from_below,
+        from_above,
+        from_far,
         query,
         grad_out,
+        twin_query,
+        twin_grad,
         bias,
-        scratch=(
-            pltpu.VMEM((tokens, rows), f32),
-            pltpu.VMEM((tokens, rows), f32),
-            pltpu.VMEM((rows, width), bf16),
-            pltpu.VMEM((rows, LAT), bf16),
-        ),
-        flops=6 * 10**9,
+        flops=3 * 10**9,
         traffic=10**7,
-        mib=24,
-    )
-    got = lax.ppermute(give.reshape(4, pool_lines, line), "head", twin)
-    got = got.reshape(4 * pool_lines, line)
+        mib=20,
+    )
+    twin_stats = lax.ppermute(stats, "head", twin)
     piece = shape((pool_lines, line), bf16)
-    to_down, to_up, to_far = call(merge, (piece, piece, piece), keep, got)
+    to_own, to_down, to_up, to_far, score_grad = call(
+        key_side,
+        (shape((pool_lines, line), f32), piece, piece, piece, shape((tokens, 2 * rows), bf16)),
+        scores,
+        prob_grad,
+        stats,
+        twin_stats,
+        query_rows,
+        grad_rows,
+        flops=3 * 10**9,
+        traffic=10**7,
+        mib=20,
+    )
     sum_up = lax.ppermute(to_up, "head", up)
     sum_down = lax.ppermute(to_down, "head", down)
     sum_far = lax.ppermute(to_far, "head", across)
-    query_grad = call(
+    half_grad = shape((rows // 2, line), f32)
+    query_mine, query_other = call(
         query_side,
-        shape(query.shape, bf16),
+        (half_grad, half_grad),
         score_grad,
-        all_keys,
-        scratch=(pltpu.VMEM((rows, width), f32),),
+        keys,
+        scratch=(pltpu.VMEM((2 * rows, width), f32),),
         flops=3 * 10**9,
         traffic=10**7,
     )
-    outbox = call(
-        outgoing, shape((slots, line), bf16), back, keep, got, sum_up, sum_down, sum_far
-    )
+    query_got = lax.ppermute(query_other, "head", twin)
+    query_grad = call(query_sum, shape(query.shape, bf16), query_mine, query_got)
+    outbox = call(outgoing, shape((slots, line), bf16), back, to_own, sum_up, sum_down, sum_far)
     inbox = swap(outbox, "ctx")
     totals = call(multiply, shape((n_head * CAP * LINES, line), bf16), sums, inbox)
     spread = swap(totals, "head")

time: 162 us -> 156 us (0.963)
  blocking collectives: 21.7 us -> 0 us
  starting transfers between devices: 53.7 us -> 64.2 us
  local copies, waits for them, and re-layouts: 5.48 us -> 7.51 us
    all_to_all x1 -> x0, blocking collectives: 21.7 us -> none  [swap(): lax.all_to_all(x3, axis, split_axis=0, concat_axis=0, tiled=True)]
    ppermute x2 -> x4, starting transfers between devices: 7.59 us -> 13.7 us  [the longest x1 5.18 us: local(): twin_stats = lax.ppermute(stats, 'head', twin)]
    all_to_all x3 -> x4, waiting for transfers between devices: 26.2 us -> 32.2 us  [swap(): lax.all_to_all(x3, axis, split_axis=0, concat_axis=0, tiled=True)]
    ppermute x2 -> x4, waiting for transfers between devices: 5.33 us -> 0.85 us  [the longest x1 0.84 us: local(): twin_stats = lax.ppermute(stats, 'head', twin)]
    all_to_all x3 -> x4, starting transfers between devices: 21.8 us -> 26.2 us  [swap(): lax.all_to_all(x3, axis, split_axis=0, concat_axis=0, tiled=True)]
    unnamed x15 -> x19, local copies, waits for them, and re-layouts: 5.48 us -> 7.51 us
    pallas_call x11 -> x12, Pallas kernels: 23.3 us -> 24.8 us  [call(): pl.pallas_call(body, out_shape=out_shape, in_specs=specs, out_specs=jax.t...]
  transfers between devices with their start and end apart: 11 -> 14, of which waited for: 11 -> 11; matrix products, arithmetic and copies ran while one was open for 1% -> 1% of each run, Pallas kernels for 4% -> 6%
where the time goes in v4:
time: 156 us; the launch traced here: 155 us
  starting transfers between devices  64.2 us (41%)
  waiting for transfers between devices  57.6 us (37%)
  Pallas kernels  24.8 us (16%)
  local copies, waits for them, and re-layouts  7.51 us (5%)
    all_to_all x4, waiting for transfers between devices, swap(): lax.all_to_all(x3, axis, split_axis=0, concat_axis=0, tiled=True)  32.2 us
    all_to_all x4, starting transfers between devices, swap(): lax.all_to_all(x3, axis, split_axis=0, concat_axis=0, tiled=True)  26.2 us
    pallas_call x12, Pallas kernels, call(): pl.pallas_call(body, out_shape=out_shape, in_specs=specs, out_specs=jax.t...  24.8 us
    ppermute x1, starting transfers between devices, local(): from_far = lax.ppermute(mine, 'head', across)  10.7 us
    ppermute x1, waiting for transfers between devices, local(): sum_far = lax.ppermute(to_far, 'head', across)  7.94 us
    unnamed x19, local copies, waits for them, and re-layouts  7.51 us
    ppermute x1, waiting for transfers between devices, local(): from_above = lax.ppermute(mine, 'head', down)  6.95 us
    ppermute x1, starting transfers between devices, local(): twin_stats = lax.ppermute(stats, 'head', twin)  5.18 us
  transfers between devices with their start and end apart: 14, of which 11 were waited for; matrix products, arithmetic and copies ran while one was open for 1% of the time, Pallas kernels for 6%

profile of v4, /device:TPU:1, one launch (start us, length us, event | category | flops | bytes accessed | tf_op | source)
XLA Modules:
  0.0 155.1 jit_solution(15334197384882328463)
XLA Ops:
  1.3 2.3 %shard_map.59 = (bf16[640,128]{1,0:T(8,128)(2,1)S(1)}, f32[16,640]{1,0:T(8,128)S(1)}, bf16[256,128]{1,0:T(8,128)(2,1)}) custom-call(s32[32,128]{1,0:T(8,128)S(1)} %bitcast.16), custom_call_target="tpu_custom_call" | custom-call | tf_op jit(solution)/shard_map/pallas_call | solution.py:37
  3.7 10.5 %all-to-all-start = ((bf16[32,8,128]{2,1,0:T(8,128)(2,1)}), bf16[32,8,128]{2,1,0:T(8,128)(2,1)S(1)}, u32[]{:S(2)}, u32[]{:S(2)}) async-start(bf16[32,8,128]{2,1,0:T(8,128)(2,1)} %bitcast.3), calls=%async_computation | async-start | bytes 131072 | tf_op jit(solution)/shard_map/all_to_all | solution.py:309
  14.3 1.9 %copy.6.lat_ref = bf16[1280,576]{1,0:T(8,128)(2,1)S(1)} copy(bf16[1280,576]{0,1:T(8,128)(2,1)} %param.4) | data formatting | bytes 2949120 | tf_op args[0]
  16.2 1.3 shard_map.61.own_ref
  17.4 5.6 %all-to-all-done = bf16[32,8,128]{2,1,0:T(8,128)(2,1)S(1)} async-done(((bf16[32,8,128]{2,1,0:T(8,128)(2,1)}), bf16[32,8,128]{2,1,0:T(8,128)(2,1)S(1)}, u32[]{:S(2)}, u32[]{:S(2)}) %all-to-all-start) | async-done | bytes 65568 | tf_op jit(solution)/shard_map/all_to_all | solution.py:309
  24.2 3.9 %all-to-all-start.1 = ((bf16[32,8,1152]{2,1,0:T(8,128)(2,1)}), bf16[32,8,1152]{2,1,0:T(8,128)(2,1)S(1)}, u32[]{:S(2)}, u32[]{:S(2)}) async-start(bf16[32,8,1152]{2,1,0:T(8,128)(2,1)} %bitcast.5), calls=%async_computation.1 | async-start | bytes 1179648 | tf_op jit(solution)/shard_map/all_to_all | solution.py:309
  30.1 4.0 %collective-permute-start.3 = (bf16[128,2304]{1,0:T(8,128)(2,1)S(1)}, bf16[128,2304]{1,0:T(8,128)(2,1)S(1)}, u32[]{:S(2)}, u32[]{:S(2)}) collective-permute-start(bf16[128,2304]{1,0:T(8,128)(2,1)S(1)} %copy-done.3), channel_id=1, source_target_pairs={{0,1},{1,0},{2,3},{3,2},{4,5},{5,4},{6,7},{7,6},{8,9},{9,8},{10,11... | collective-permute-start | bytes 1769480 | tf_op jit(solution)/shard_map/ppermute | solution.py:336
  34.1 1.9 %collective-permute-start.4 = (bf16[128,2048]{1,0:T(8,128)(2,1)S(1)}, bf16[128,2048]{1,0:T(8,128)(2,1)}, u32[]{:S(2)}, u32[]{:S(2)}) collective-permute-start(bf16[128,2048]{1,0:T(8,128)(2,1)S(1)} %copy-done.4), channel_id=1, source_target_pairs={{0,1},{1,0},{2,3},{3,2},{4,5},{5,4},{6,7},{7,6},{8,9},{9,8},{10,11... | collective-permute-start | bytes 1572872 | tf_op jit(solution)/shard_map/ppermute | solution.py:337
  36.1 7.9 %all-to-all-done.1 = bf16[32,8,1152]{2,1,0:T(8,128)(2,1)S(1)} async-done(((bf16[32,8,1152]{2,1,0:T(8,128)(2,1)}), bf16[32,8,1152]{2,1,0:T(8,128)(2,1)S(1)}, u32[]{:S(2)}, u32[]{:S(2)}) %all-to-all-start.1) | async-done | bytes 589856 | tf_op jit(solution)/shard_map/all_to_all | solution.py:309
  44.3 10.7 %collective-permute-start.2 = (bf16[144,1152]{1,0:T(8,128)(2,1)S(1)}, bf16[144,1152]{1,0:T(8,128)(2,1)S(1)}, u32[]{:S(2)}, u32[]{:S(2)}) collective-permute-start(bf16[144,1152]{1,0:T(8,128)(2,1)S(1)} %shard_map.63.own_ref), channel_id=1, source_target_pairs={{0,4},{1,13},{2,6},{3,15},{4,8},{5,1},{6,10},{7,3},{8,12},{9,5},{1... | collective-permute-start | bytes 995336 | tf_op jit(solution)/shard_map/ppermute | solution.py:342
  54.9 2.2 %collective-permute-start.1 = (bf16[144,1152]{1,0:T(8,128)(2,1)S(1)}, bf16[144,1152]{1,0:T(8,128)(2,1)S(1)}, u32[]{:S(2)}, u32[]{:S(2)}) collective-permute-start(bf16[144,1152]{1,0:T(8,128)(2,1)S(1)} %shard_map.63.own_ref), channel_id=1, source_target_pairs={{0,14},{1,15},{2,0},{3,1},{4,2},{5,3},{6,4},{7,5},{8,6},{9,7},{10,... | collective-permute-start | bytes 995336 | tf_op jit(solution)/shard_map/ppermute | solution.py:341
  57.1 3.1 %collective-permute-start = (bf16[144,1152]{1,0:T(8,128)(2,1)S(1)}, bf16[144,1152]{1,0:T(8,128)(2,1)S(1)}, u32[]{:S(2)}, u32[]{:S(2)}) collective-permute-start(bf16[144,1152]{1,0:T(8,128)(2,1)S(1)} %shard_map.63.own_ref), channel_id=1, source_target_pairs={{0,2},{1,3},{2,4},{3,5},{4,6},{5,7},{6,8},{7,9},{8,10},{9,11},{10,... | collective-permute-start | bytes 995336 | tf_op jit(solution)/shard_map/ppermute | solution.py:340
  60.2 2.4 %collective-permute-done.2.far_ref = bf16[144,1152]{1,0:T(8,128)(2,1)S(1)} collective-permute-done((bf16[144,1152]{1,0:T(8,128)(2,1)S(1)}, bf16[144,1152]{1,0:T(8,128)(2,1)S(1)}, u32[]{:S(2)}, u32[]{:S(2)}) %collective-permute-start.2) | collective-permute-done | bytes 331808 | tf_op jit(solution)/shard_map/ppermute | solution.py:342
  62.7 7.0 %collective-permute-done.1.above_ref = bf16[144,1152]{1,0:T(8,128)(2,1)S(1)} collective-permute-done((bf16[144,1152]{1,0:T(8,128)(2,1)S(1)}, bf16[144,1152]{1,0:T(8,128)(2,1)S(1)}, u32[]{:S(2)}, u32[]{:S(2)}) %collective-permute-start.1) | collective-permute-done | bytes 331808 | tf_op jit(solution)/shard_map/ppermute | solution.py:341
  69.6 2.4 %collective-permute-done.below_ref = bf16[144,1152]{1,0:T(8,128)(2,1)S(1)} collective-permute-done((bf16[144,1152]{1,0:T(8,128)(2,1)S(1)}, bf16[144,1152]{1,0:T(8,128)(2,1)S(1)}, u32[]{:S(2)}, u32[]{:S(2)}) %collective-permute-start) | collective-permute-done | bytes 331808 | tf_op jit(solution)/shard_map/ppermute | solution.py:340
  73.1 6.4 %shard_map.64 = (f32[1152,1024]{1,0:T(8,128)S(1)}, f32[1152,1024]{1,0:T(8,128)S(1)}, f32[8,1024]{1,0:T(8,128)S(1)}, bf16[1152,576]{1,0:T(8,128)(2,1)S(1)}, bf16[...) custom-call(bf16[144,1152]{1,0:T(8,128)(2,1)S(1)} %shard_map.63.own_ref, ...), custom_call_target="tpu_custom_call" | custom-call | flops 3000000000 | bytes 10000000 | tf_op jit(solution)/shard_map/pallas_call | solution.py:37
  79.5 5.2 %collective-permute-start.5 = (f32[8,1024]{1,0:T(8,128)S(1)}, f32[8,1024]{1,0:T(8,128)S(1)}, u32[]{:S(2)}, u32[]{:S(2)}) collective-permute-start(f32[8,1024]{1,0:T(8,128)S(1)} %get-tuple-element.36.stat_ref), channel_id=1, source_target_pairs={{0,1},{1,0},{2,3},{3,2},{4,5},{5,4},{6,7},{7,6},{8,9},{9,8},{10,11... | collective-permute-start | bytes 98312 | tf_op jit(solution)/shard_map/ppermute | solution.py:367
  85.5 3.6 %shard_map.65 = (f32[144,1152]{1,0:T(8,128)S(1)}, bf16[144,1152]{1,0:T(8,128)(2,1)S(1)}, bf16[144,1152]{1,0:T(8,128)(2,1)S(1)}, bf16[144,1152]{1,0:T(8,128)(2,1)S(1)}, bf16[1152,1024]{1,0:T(8,128)(2,1)S(1)}) custom-call(f32[1152,1024]{1,0:T(8,128)S(1)} %get-tuple-element.34.e_ref, f32[1152,1024]{1,0:T(8,128)S(1)} %get-tuple-element.35.d_ref, ...), custom_call_target="tpu_custom_call" | custom-call | flops 3000000000 | bytes 10000000 | tf_op jit(solution)/shard_map/pallas_call | solution.py:37
  89.1 1.9 %collective-permute-start.7 = (bf16[144,1152]{1,0:T(8,128)(2,1)S(1)}, bf16[144,1152]{1,0:T(8,128)(2,1)S(1)}, u32[]{:S(2)}, u32[]{:S(2)}) collective-permute-start(bf16[144,1152]{1,0:T(8,128)(2,1)S(1)} %get-tuple-element.47), channel_id=1, source_target_pairs={{0,2},{1,3},{2,4},{3,5},{4,6},{5,7},{6,8},{7,9},{8,10},{9,11},{10,... | collective-permute-start | bytes 995336 | tf_op jit(solution)/shard_map/ppermute | solution.py:382
  91.1 4.6 %collective-permute-start.8 = (bf16[144,1152]{1,0:T(8,128)(2,1)S(1)}, bf16[144,1152]{1,0:T(8,128)(2,1)S(1)}, u32[]{:S(2)}, u32[]{:S(2)}) collective-permute-start(bf16[144,1152]{1,0:T(8,128)(2,1)S(1)} %get-tuple-element.48), channel_id=1, source_target_pairs={{0,14},{1,15},{2,0},{3,1},{4,2},{5,3},{6,4},{7,5},{8,6},{9,7},{10,... | collective-permute-start | bytes 995336 | tf_op jit(solution)/shard_map/ppermute | solution.py:383
  95.6 1.9 %collective-permute-start.9 = (bf16[144,1152]{1,0:T(8,128)(2,1)S(1)}, bf16[144,1152]{1,0:T(8,128)(2,1)S(1)}, u32[]{:S(2)}, u32[]{:S(2)}) collective-permute-start(bf16[144,1152]{1,0:T(8,128)(2,1)S(1)} %get-tuple-element.49), channel_id=1, source_target_pairs={{0,4},{1,13},{2,6},{3,15},{4,8},{5,1},{6,10},{7,3},{8,12},{9,5},{1... | collective-permute-start | bytes 995336 | tf_op jit(solution)/shard_map/ppermute | solution.py:384
  97.6 3.7 %collective-permute-done.7.up_ref = bf16[144,1152]{1,0:T(8,128)(2,1)S(1)} collective-permute-done((bf16[144,1152]{1,0:T(8,128)(2,1)S(1)}, bf16[144,1152]{1,0:T(8,128)(2,1)S(1)}, u32[]{:S(2)}, u32[]{:S(2)}) %collective-permute-start.7) | collective-permute-done | bytes 331808 | tf_op jit(solution)/shard_map/ppermute | solution.py:382
  102.4 7.9 %collective-permute-done.9.far_ref = bf16[144,1152]{1,0:T(8,128)(2,1)S(1)} collective-permute-done((bf16[144,1152]{1,0:T(8,128)(2,1)S(1)}, bf16[144,1152]{1,0:T(8,128)(2,1)S(1)}, u32[]{:S(2)}, u32[]{:S(2)}) %collective-permute-start.9) | collective-permute-done | bytes 331808 | tf_op jit(solution)/shard_map/ppermute | solution.py:384
  110.3 1.2 shard_map.68
  111.6 4.4 %all-to-all-start.2 = ((bf16[32,8,1152]{2,1,0:T(8,128)(2,1)}), bf16[32,8,1152]{2,1,0:T(8,128)(2,1)S(1)}, u32[]{:S(2)}, u32[]{:S(2)}) async-start(bf16[32,8,1152]{2,1,0:T(8,128)(2,1)} %bitcast.7), calls=%async_computation.2 | async-start | bytes 1179648 | tf_op jit(solution)/shard_map/all_to_all | solution.py:309
  116.0 1.7 %copy-done.2 = bf16[1152,1024]{1,0:T(8,128)(2,1)S(1)} copy-done((bf16[1152,1024]{1,0:T(8,128)(2,1)S(1)}, bf16[1152,1024]{1,0:T(8,128)(2,1)}, u32[]{:S(2)}) %copy-start.2) | copy-done | bytes 2359320
  117.7 1.4 copy-done.6
  119.0 4.5 %shard_map.66 = (f32[256,1152]{1,0:T(8,128)S(1)}, f32[256,1152]{1,0:T(8,128)}) custom-call(bf16[1152,1024]{1,0:T(8,128)(2,1)S(1)} %copy-done.2, bf16[1152,576]{1,0:T(8,128)(2,1)S(1)} %copy-done.6), custom_call_target="tpu_custom_call" | custom-call | flops 3000000000 | bytes 10000000 | tf_op jit(solution)/shard_map/pallas_call | solution.py:37
  123.5 2.5 %collective-permute-start.6 = (f32[256,1152]{1,0:T(8,128)}, f32[256,1152]{1,0:T(8,128)S(1)}, u32[]{:S(2)}, u32[]{:S(2)}) collective-permute-start(f32[256,1152]{1,0:T(8,128)} %get-tuple-element.42), channel_id=1, source_target_pairs={{0,1},{1,0},{2,3},{3,2},{4,5},{5,4},{6,7},{7,6},{8,9},{9,8},{10,11... | collective-permute-start | bytes 3538952 | tf_op jit(solution)/shard_map/ppermute | solution.py:395
  126.1 7.4 %all-to-all-done.2 = bf16[32,8,1152]{2,1,0:T(8,128)(2,1)S(1)} async-done(((bf16[32,8,1152]{2,1,0:T(8,128)(2,1)}), bf16[32,8,1152]{2,1,0:T(8,128)(2,1)S(1)}, u32[]{:S(2)}, u32[]{:S(2)}) %all-to-all-start.2) | async-done | bytes 589856 | tf_op jit(solution)/shard_map/all_to_all | solution.py:309
  134.4 7.3 %all-to-all-start.3 = ((bf16[16,8,1152]{2,1,0:T(8,128)(2,1)}), bf16[16,8,1152]{2,1,0:T(8,128)(2,1)S(1)}, u32[]{:S(2)}, u32[]{:S(2)}) async-start(bf16[16,8,1152]{2,1,0:T(8,128)(2,1)} %bitcast.9), calls=%async_computation.3 | async-start | bytes 589824 | tf_op jit(solution)/shard_map/all_to_all | solution.py:309
  142.8 11.4 %all-to-all-done.3 = bf16[16,8,1152]{2,1,0:T(8,128)(2,1)S(1)} async-done(((bf16[16,8,1152]{2,1,0:T(8,128)(2,1)}), bf16[16,8,1152]{2,1,0:T(8,128)(2,1)S(1)}, u32[]{:S(2)}, u32[]{:S(2)}) %all-to-all-start.3) | async-done | bytes 294944 | tf_op jit(solution)/shard_map/all_to_all | solution.py:309
  (28 shorter events, 10.2 us)
Async XLA Ops:
  0.6 0.7 copy-start
  3.7 19.3 %all-to-all-start = ((bf16[32,8,128]{2,1,0:T(8,128)(2,1)}), bf16[32,8,128]{2,1,0:T(8,128)(2,1)S(1)}, u32[]{:S(2)}, u32[]{:S(2)}) async-start(bf16[32,8,128]{2,1,0:T(8,128)(2,1)} %bitcast.3), calls=%async_computation | async-start | bytes 131072 | tf_op jit(solution)/shard_map/all_to_all | solution.py:309
  24.2 19.8 %all-to-all-start.1 = ((bf16[32,8,1152]{2,1,0:T(8,128)(2,1)}), bf16[32,8,1152]{2,1,0:T(8,128)(2,1)S(1)}, u32[]{:S(2)}, u32[]{:S(2)}) async-start(bf16[32,8,1152]{2,1,0:T(8,128)(2,1)} %bitcast.5), calls=%async_computation.1 | async-start | bytes 1179648 | tf_op jit(solution)/shard_map/all_to_all | solution.py:309
  28.1 2.0 %copy-start.3 = (bf16[128,2304]{1,0:T(8,128)(2,1)S(1)}, bf16[128,2304]{1,0:T(8,128)(2,1)}, u32[]{:S(2)}) copy-start(bf16[128,2304]{1,0:T(8,128)(2,1)} %q_ref) | copy-start | bytes 1769476
  28.1 6.0 %copy-start.4 = (bf16[128,2048]{1,0:T(8,128)(2,1)S(1)}, bf16[128,2048]{1,0:T(8,128)(2,1)}, u32[]{:S(2)}) copy-start(bf16[128,2048]{1,0:T(8,128)(2,1)} %g_ref) | copy-start | bytes 1572868
  29.3 0.8 copy-start.7
  30.1 30.1 %collective-permute-start.3 = (bf16[128,2304]{1,0:T(8,128)(2,1)S(1)}, bf16[128,2304]{1,0:T(8,128)(2,1)S(1)}, u32[]{:S(2)}, u32[]{:S(2)}) collective-permute-start(bf16[128,2304]{1,0:T(8,128)(2,1)S(1)} %copy-done.3), channel_id=1, source_target_pairs={{0,1},{1,0},{2,3},{3,2},{4,5},{5,4},{6,7},{7,6},{8,9},{9,8},{10,11... | collective-permute-start | bytes 1769480 | tf_op jit(solution)/shard_map/ppermute | solution.py:336
  34.1 26.1 %collective-permute-start.4 = (bf16[128,2048]{1,0:T(8,128)(2,1)S(1)}, bf16[128,2048]{1,0:T(8,128)(2,1)}, u32[]{:S(2)}, u32[]{:S(2)}) collective-permute-start(bf16[128,2048]{1,0:T(8,128)(2,1)S(1)} %copy-done.4), channel_id=1, source_target_pairs={{0,1},{1,0},{2,3},{3,2},{4,5},{5,4},{6,7},{7,6},{8,9},{9,8},{10,11... | collective-permute-start | bytes 1572872 | tf_op jit(solution)/shard_map/ppermute | solution.py:337
  44.3 18.4 %collective-permute-start.2 = (bf16[144,1152]{1,0:T(8,128)(2,1)S(1)}, bf16[144,1152]{1,0:T(8,128)(2,1)S(1)}, u32[]{:S(2)}, u32[]{:S(2)}) collective-permute-start(bf16[144,1152]{1,0:T(8,128)(2,1)S(1)} %shard_map.63.own_ref), channel_id=1, source_target_pairs={{0,4},{1,13},{2,6},{3,15},{4,8},{5,1},{6,10},{7,3},{8,12},{9,5},{1... | collective-permute-start | bytes 995336 | tf_op jit(solution)/shard_map/ppermute | solution.py:342
  54.9 14.7 %collective-permute-start.1 = (bf16[144,1152]{1,0:T(8,128)(2,1)S(1)}, bf16[144,1152]{1,0:T(8,128)(2,1)S(1)}, u32[]{:S(2)}, u32[]{:S(2)}) collective-permute-start(bf16[144,1152]{1,0:T(8,128)(2,1)S(1)} %shard_map.63.own_ref), channel_id=1, source_target_pairs={{0,14},{1,15},{2,0},{3,1},{4,2},{5,3},{6,4},{7,5},{8,6},{9,7},{10,... | collective-permute-start | bytes 995336 | tf_op jit(solution)/shard_map/ppermute | solution.py:341
  57.1 14.9 %collective-permute-start = (bf16[144,1152]{1,0:T(8,128)(2,1)S(1)}, bf16[144,1152]{1,0:T(8,128)(2,1)S(1)}, u32[]{:S(2)}, u32[]{:S(2)}) collective-permute-start(bf16[144,1152]{1,0:T(8,128)(2,1)S(1)} %shard_map.63.own_ref), channel_id=1, source_target_pairs={{0,2},{1,3},{2,4},{3,5},{4,6},{5,7},{6,8},{7,9},{8,10},{9,11},{10,... | collective-permute-start | bytes 995336 | tf_op jit(solution)/shard_map/ppermute | solution.py:340
  72.0 1.1 copy-start.8
  79.5 9.6 %copy-start.5 = (bf16[1152,576]{1,0:T(8,128)(2,1)}, bf16[1152,576]{1,0:T(8,128)(2,1)S(1)}, u32[]{:S(2)}) copy-start(bf16[1152,576]{1,0:T(8,128)(2,1)S(1)} %get-tuple-element.40.k_ref) | copy-start | bytes 3981316
  79.5 6.0 %collective-permute-start.5 = (f32[8,1024]{1,0:T(8,128)S(1)}, f32[8,1024]{1,0:T(8,128)S(1)}, u32[]{:S(2)}, u32[]{:S(2)}) collective-permute-start(f32[8,1024]{1,0:T(8,128)S(1)} %get-tuple-element.36.stat_ref), channel_id=1, source_target_pairs={{0,1},{1,0},{2,3},{3,2},{4,5},{5,4},{6,7},{7,6},{8,9},{9,8},{10,11... | collective-permute-start | bytes 98312 | tf_op jit(solution)/shard_map/ppermute | solution.py:367
  89.1 22.5 %copy-start.1 = (bf16[1152,1024]{1,0:T(8,128)(2,1)}, bf16[1152,1024]{1,0:T(8,128)(2,1)S(1)}, u32[]{:S(2)}) copy-start(bf16[1152,1024]{1,0:T(8,128)(2,1)S(1)} %get-tuple-element.39.ds_ref) | copy-start | bytes 7077892
  89.1 12.1 %collective-permute-start.7 = (bf16[144,1152]{1,0:T(8,128)(2,1)S(1)}, bf16[144,1152]{1,0:T(8,128)(2,1)S(1)}, u32[]{:S(2)}, u32[]{:S(2)}) collective-permute-start(bf16[144,1152]{1,0:T(8,128)(2,1)S(1)} %get-tuple-element.47), channel_id=1, source_target_pairs={{0,2},{1,3},{2,4},{3,5},{4,6},{5,7},{6,8},{7,9},{8,10},{9,11},{10,... | collective-permute-start | bytes 995336 | tf_op jit(solution)/shard_map/ppermute | solution.py:382
  91.1 11.3 %collective-permute-start.8 = (bf16[144,1152]{1,0:T(8,128)(2,1)S(1)}, bf16[144,1152]{1,0:T(8,128)(2,1)S(1)}, u32[]{:S(2)}, u32[]{:S(2)}) collective-permute-start(bf16[144,1152]{1,0:T(8,128)(2,1)S(1)} %get-tuple-element.48), channel_id=1, source_target_pairs={{0,14},{1,15},{2,0},{3,1},{4,2},{5,3},{6,4},{7,5},{8,6},{9,7},{10,... | collective-permute-start | bytes 995336 | tf_op jit(solution)/shard_map/ppermute | solution.py:383
  95.6 14.7 %collective-permute-start.9 = (bf16[144,1152]{1,0:T(8,128)(2,1)S(1)}, bf16[144,1152]{1,0:T(8,128)(2,1)S(1)}, u32[]{:S(2)}, u32[]{:S(2)}) collective-permute-start(bf16[144,1152]{1,0:T(8,128)(2,1)S(1)} %get-tuple-element.49), channel_id=1, source_target_pairs={{0,4},{1,13},{2,6},{3,15},{4,8},{5,1},{6,10},{7,3},{8,12},{9,5},{1... | collective-permute-start | bytes 995336 | tf_op jit(solution)/shard_map/ppermute | solution.py:384
  111.6 21.9 %all-to-all-start.2 = ((bf16[32,8,1152]{2,1,0:T(8,128)(2,1)}), bf16[32,8,1152]{2,1,0:T(8,128)(2,1)S(1)}, u32[]{:S(2)}, u32[]{:S(2)}) async-start(bf16[32,8,1152]{2,1,0:T(8,128)(2,1)} %bitcast.7), calls=%async_computation.2 | async-start | bytes 1179648 | tf_op jit(solution)/shard_map/all_to_all | solution.py:309
  116.0 1.7 %copy-start.2 = (bf16[1152,1024]{1,0:T(8,128)(2,1)S(1)}, bf16[1152,1024]{1,0:T(8,128)(2,1)}, u32[]{:S(2)}) copy-start(bf16[1152,1024]{1,0:T(8,128)(2,1)} %copy-done.1) | copy-start | bytes 7077892
  117.7 1.4 copy-start.6
  123.5 18.2 %collective-permute-start.6 = (f32[256,1152]{1,0:T(8,128)}, f32[256,1152]{1,0:T(8,128)S(1)}, u32[]{:S(2)}, u32[]{:S(2)}) collective-permute-start(f32[256,1152]{1,0:T(8,128)} %get-tuple-element.42), channel_id=1, source_target_pairs={{0,1},{1,0},{2,3},{3,2},{4,5},{5,4},{6,7},{7,6},{8,9},{9,8},{10,11... | collective-permute-start | bytes 3538952 | tf_op jit(solution)/shard_map/ppermute | solution.py:395
  134.4 19.7 %all-to-all-start.3 = ((bf16[16,8,1152]{2,1,0:T(8,128)(2,1)}), bf16[16,8,1152]{2,1,0:T(8,128)(2,1)S(1)}, u32[]{:S(2)}, u32[]{:S(2)}) async-start(bf16[16,8,1152]{2,1,0:T(8,128)(2,1)} %bitcast.9), calls=%async_computation.3 | async-start | bytes 589824 | tf_op jit(solution)/shard_map/all_to_all | solution.py:309

commit v5 on v4

--- a/solution.py
+++ b/solution.py
@@ -30,10 +30,12 @@
     return lax.dot_general(a, b, (((ca,), (cb,)), ((), ())), preferred_element_type=f32)
 
 
-def call(body, out_shape, *args, scratch=(), flops=0, traffic=0, mib=16):
+def call(body, out_shape, *args, scratch=(), flops=0, traffic=0, mib=16, hbm=()):
     vmem = pl.BlockSpec(memory_space=pltpu.VMEM)
     smem = pl.BlockSpec(memory_space=pltpu.SMEM)
     specs = [smem if a.dtype == jnp.int32 and a.ndim == 1 else vmem for a in args]
+    for i in hbm:
+        specs[i] = pl.BlockSpec(memory_space=pl.ANY)
     return pl.pallas_call(
         body,
         out_shape=out_shape,
@@ -103,7 +105,8 @@
 
 
 def arrange(
-    pos_ref, hit_ref, info_ref, ask_ref, bias_ref, send_ref, back_ref, sum_ref, place_ref, *, first, per_dest
+    pos_ref, hit_ref, info_ref, ask_ref, bias_ref, rest_ref, send_ref, back_ref, sum_ref, place_ref,
+    *, first, per_dest,
 ):
     blocks, queries = hit_ref.shape
     rows, slots = send_ref.shape
@@ -123,13 +126,13 @@
     picked = dot(here.astype(bf16), hit_ref[...], 1, 0)
     query_pos = first + pos_ref[0] * queries + iota((rows, queries), 1)
     base = block_id * BLOCK + (iota((rows, queries), 0) & 3) - query_pos
-    piece = 0
-    for u in (0, 1):
-        for step in (0, -1, 1, 2):
+    for i, step in enumerate((0, -1, 1, 2)):
+        out_ref = rest_ref if i else bias_ref
+        for u in (0, 1):
             offset = near(head, step) * PART + u * LINES
             allowed = jnp.logical_and(picked > 0.5, base + offset <= 0)
-            bias_ref[piece * rows : (piece + 1) * rows, :] = jnp.where(allowed, 0.0, NEG)
-            piece += 1
+            at = (2 * max(i - 1, 0) + u) * rows
+            out_ref[at : at + rows, :] = jnp.where(allowed, 0.0, NEG)
     row = iota(send_ref.shape, 0)
     col = iota(send_ref.shape, 1)
     send = one_hot(col == (by20(block_id) * CAP + block_rank) * LINES + (row & 3))
@@ -160,62 +163,76 @@
     out_ref[...] = dot(a_ref[...], b_ref[...], 1, 0).astype(out_ref.dtype)
 
 
-def score(
-    own_ref, below_ref, above_ref, far_ref, q_ref, g_ref, qt_ref, gt_ref, bias_ref,
-    e_ref, d_ref, stat_ref, k_ref, qs_ref, gs_ref,
+def score_piece(keys, bias, qs_ref, gs_ref, e_ref, d_ref, at):
+    tokens, cols = keys.shape[0], qs_ref.shape[0]
+    wide = jnp.concatenate([bias] * (cols // bias.shape[1]), axis=1)
+    s = dot(keys, qs_ref[...], 1, 1) * score_scale + wide
+    d = dot(keys[:, :LAT], gs_ref[...], 1, 1)
+    top = jnp.max(s, axis=0, keepdims=True)
+    e = jnp.exp(s - top)
+    e_ref[at : at + tokens, :] = e
+    d_ref[at : at + tokens, :] = d
+    return top, jnp.sum(e, axis=0, keepdims=True), jnp.sum(e * d, axis=0, keepdims=True)
+
+
+def unpack(piece_ref, k_ref, at):
+    lines, width = piece_ref.shape[0], k_ref.shape[1]
+    for u in (0, 1):
+        here = slice(at + u * lines, at + (u + 1) * lines)
+        k_ref[here, :] = piece_ref[:, u * width : (u + 1) * width]
+
+
+def score_own(
+    own_ref, q_ref, g_ref, qt_ref, gt_ref, bias_ref, e_ref, d_ref, stat_ref, k_ref, qs_ref, gs_ref
 ):
-    tokens, width = k_ref.shape
+    width = k_ref.shape[1]
     queries = q_ref.shape[0]
     heads = g_ref.shape[1] // LAT
-    cols = 2 * heads * queries
-    lines = own_ref.shape[0]
-    for u in (0, 1):
-        for i, piece_ref in enumerate((own_ref, below_ref, above_ref, far_ref)):
-            at = (4 * u + i) * lines
-            k_ref[at : at + lines, :] = piece_ref[:, u * width : (u + 1) * width]
+    unpack(own_ref, k_ref, 0)
     for c, (x_ref, y_ref) in enumerate(((q_ref, g_ref), (qt_ref, gt_ref))):
         for h in range(heads):
             at = (c * heads + h) * queries
             qs_ref[at : at + queries, :] = x_ref[:, h * width : (h + 1) * width]
             gs_ref[at : at + queries, :] = y_ref[:, h * LAT : (h + 1) * LAT]
-    step = 384
-
-    def fold(x):
-        return jnp.sum(x.reshape(step // 8, 8, cols), axis=0)
-
-    def one(i, top):
-        at = pl.ds(pl.multiple_of(i * step, step), step)
-        keys = k_ref[at, :]
-        bias = jnp.concatenate([bias_ref[at, :]] * (2 * heads), axis=1)
-        s = dot(keys, qs_ref[...], 1, 1) * score_scale + bias
-        e_ref[at, :] = s
-        d_ref[at, :] = dot(keys[:, :LAT], gs_ref[...], 1, 1)
-        return jnp.maximum(top, jnp.max(s.reshape(step // 8, 8, cols), axis=0))
-
-    top = lax.fori_loop(0, tokens // step, one, jnp.full((8, cols), -jnp.inf, f32))
-    top = jnp.max(top, axis=0, keepdims=True)
-
-    def two(i, carry):
-        total, mixed = carry
-        at = pl.ds(pl.multiple_of(i * step, step), step)
-        e = jnp.exp(e_ref[at, :] - top)
-        e_ref[at, :] = e
-        return total + fold(e), mixed + fold(e * d_ref[at, :])
-
-    zero = jnp.zeros((8, cols), f32)
-    total, mixed = lax.fori_loop(0, tokens // step, two, (zero, zero))
+    found = score_piece(k_ref[...], bias_ref[...], qs_ref, gs_ref, e_ref, d_ref, 0)
+    for i in range(3):
+        stat_ref[i : i + 1, :] = found[i]
+    stat_ref[3:8, :] = jnp.zeros((5, stat_ref.shape[1]), f32)
+
+
+def score_rest(
+    below_ref, above_ref, far_ref, qs_ref, gs_ref, bias_hbm, first_ref,
+    e_ref, d_ref, stat_ref, tops_ref, k_ref, bias_ref, sem,
+):
+    copy = pltpu.make_async_copy(bias_hbm, bias_ref, sem)
+    copy.start()
+    size = 2 * below_ref.shape[0]
+    pieces = (below_ref, above_ref, far_ref)
+    for i, piece_ref in enumerate(pieces):
+        unpack(piece_ref, k_ref, i * size)
+    copy.wait()
+    found = [tuple(first_ref[i : i + 1, :] for i in range(3))]
+    for i in range(len(pieces)):
+        at = slice(i * size, (i + 1) * size)
+        found.append(
+            score_piece(k_ref[at, :], bias_ref[at, :], qs_ref, gs_ref, e_ref, d_ref, i * size)
+        )
+    top = functools.reduce(jnp.maximum, [f[0] for f in found])
+    weights = [jnp.exp(f[0] - top) for f in found]
     stat_ref[0:1, :] = top
-    stat_ref[1:2, :] = jnp.sum(total, axis=0, keepdims=True)
-    stat_ref[2:3, :] = jnp.sum(mixed, axis=0, keepdims=True)
-    stat_ref[3:8, :] = jnp.zeros((5, cols), f32)
+    stat_ref[1:2, :] = sum(f[1] * w for f, w in zip(found, weights))
+    stat_ref[2:3, :] = sum(f[2] * w for f, w in zip(found, weights))
+    stat_ref[3:8, :] = jnp.zeros((5, stat_ref.shape[1]), f32)
+    for i, f in enumerate(found):
+        tops_ref[i : i + 1, :] = f[0]
+    tops_ref[4:8, :] = jnp.zeros((4, stat_ref.shape[1]), f32)
 
 
 def key_side(
-    e_ref, d_ref, stat_ref, other_ref, qs_ref, gs_ref, own_ref, down_ref, up_ref, far_ref, ds_ref
+    e_ref, d_ref, stat_ref, other_ref, tops_ref, qs_ref, gs_ref, *out_refs, first
 ):
-    tokens, cols = e_ref.shape
-    width = qs_ref.shape[1]
-    lines = own_ref.shape[0]
+    *outs, ds_ref = out_refs
+    cols, width = qs_ref.shape
     mine = stat_ref[...]
     other = other_ref[...]
     other = jnp.concatenate([other[:, cols // 2 :], other[:, : cols // 2]], axis=1)
@@ -223,40 +240,29 @@
     a, b = jnp.exp(mine[0:1] - top), jnp.exp(other[0:1] - top)
     inv = 1.0 / (mine[1:2] * a + other[1:2] * b)
     delta = (mine[2:3] * a + other[2:3] * b) * inv
-    scale = a * inv
-    outs = (own_ref, down_ref, up_ref, far_ref)
-    step = 2 * lines
-    for i in range(tokens // step):
-        at = slice(i * step, (i + 1) * step)
-        u = i // 2
+    lines = outs[0].shape[0]
+    size = 2 * lines
+    for i, out_ref in enumerate(outs):
+        at = slice(i * size, (i + 1) * size)
+        scale = jnp.exp(tops_ref[first + i : first + i + 1, :] - top) * inv
         p = e_ref[at, :] * scale
         ds = (p * (d_ref[at, :] - delta)).astype(bf16)
         ds_ref[at, :] = ds
         dk = dot(ds, qs_ref[...], 1, 0) * score_scale
         dv = dot(p.astype(bf16), gs_ref[...], 1, 0)
-        both = jnp.concatenate([dk[:, :LAT] + dv, dk[:, LAT:]], axis=1)
-        for j in (0, 1):
-            out_ref = outs[2 * (i % 2) + j]
-            part = both[j * lines : (j + 1) * lines, :]
-            out_ref[:, u * width : (u + 1) * width] = part.astype(out_ref.dtype)
-
-
-def query_side(ds_ref, k_ref, mine_ref, other_ref, dqs_ref):
-    tokens, width = k_ref.shape
-    rows = mine_ref.shape[0]
-    step = 384
-    dqs_ref[...] = jnp.zeros_like(dqs_ref)
-
-    def one(i, carry):
-        at = pl.ds(pl.multiple_of(i * step, step), step)
-        dqs_ref[...] += dot(ds_ref[at, :], k_ref[at, :], 0, 0)
-        return carry
-
-    lax.fori_loop(0, tokens // step, one, 0)
+        both = jnp.concatenate([dk[:, :LAT] + dv, dk[:, LAT:]], axis=1).astype(out_ref.dtype)
+        for u in (0, 1):
+            out_ref[:, u * width : (u + 1) * width] = both[u * lines : (u + 1) * lines, :]
+
+
+def query_side(ds_ref, rest_ref, k_ref, rest_k_ref, mine_ref, other_ref):
+    rows, width = mine_ref.shape[0], k_ref.shape[1]
     for i, out_ref in enumerate((mine_ref, other_ref)):
         for u in (0, 1):
-            at = (2 * i + u) * rows
-            out_ref[:, u * width : (u + 1) * width] = dqs_ref[at : at + rows, :]
+            at = slice((2 * i + u) * rows, (2 * i + u + 1) * rows)
+            part = dot(ds_ref[:, at], k_ref[...], 0, 0)
+            part = part + dot(rest_ref[:, at], rest_k_ref[...], 0, 0)
+            out_ref[:, u * width : (u + 1) * width] = part
 
 
 def query_sum(mine_ref, got_ref, dq_ref):
@@ -293,7 +299,7 @@
     line = 2 * width
     pool_lines = POOL * LINES
     slots = n_ctx * CAP * LINES
-    tokens = POOL * BLOCK // 2
+    piece_rows = 2 * pool_lines
     outs = ctx_rows // n_head
     pos = jnp.stack([lax.axis_index("ctx"), lax.axis_index("head")]).astype(jnp.int32)
     first = (ctx_rows - queries) * n_ctx
@@ -316,10 +322,11 @@
     own = call(own_part, shape((per_owner * LINES, line), bf16), pos, latent, flops=10**9, traffic=10**6)
     asked = swap(ask, "ctx")
     lines_out = call(fetch, shape((slots, line), bf16), asked, own)
-    bias, send, back, sums, places = call(
+    bias, rest_bias, send, back, sums, places = call(
         functools.partial(arrange, first=first, per_dest=outs // PART),
         (
-            shape((tokens, queries), f32),
+            shape((piece_rows, queries), f32),
+            shape((3 * piece_rows, queries), f32),
             shape((pool_lines, slots), bf16),
             shape((slots, pool_lines), bf16),
             shape((n_head * CAP * LINES, slots), bf16),
@@ -341,54 +348,88 @@
     from_above = lax.ppermute(mine, "head", down)
     from_far = lax.ppermute(mine, "head", across)
     rows = queries * (grad_out.shape[1] // LAT)
-    scores, prob_grad, stats, keys, query_rows, grad_rows = call(
-        score,
+    cols = 2 * rows
+
+    def arrays(n):
+        return shape((n * piece_rows, cols), f32), shape((n * piece_rows, cols), f32)
+
+    row_stats = shape((8, cols), f32)
+    scores, prob_grad, first_stats, keys, query_rows, grad_rows = call(
+        score_own,
         (
-            shape((tokens, 2 * rows), f32),
-            shape((tokens, 2 * rows), f32),
-            shape((8, 2 * rows), f32),
-            shape((tokens, width), bf16),
-            shape((2 * rows, width), bf16),
-            shape((2 * rows, LAT), bf16),
+            *arrays(1),
+            row_stats,
+            shape((piece_rows, width), bf16),
+            shape((cols, width), bf16),
+            shape((cols, LAT), bf16),
         ),
         mine,
-        from_below,
-        from_above,
-        from_far,
         query,
         grad_out,
         twin_query,
         twin_grad,
         bias,
+        flops=10**9,
+        traffic=10**6,
+        mib=20,
+    )
+    rest_scores, rest_prob_grad, stats, tops, rest_keys = call(
+        score_rest,
+        (*arrays(3), row_stats, row_stats, shape((3 * piece_rows, width), bf16)),
+        from_below,
+        from_above,
+        from_far,
+        query_rows,
+        grad_rows,
+        rest_bias,
+        first_stats,
+        scratch=(pltpu.VMEM((3 * piece_rows, queries), f32), pltpu.SemaphoreType.DMA(())),
         flops=3 * 10**9,
-        traffic=10**7,
+        traffic=10**6,
         mib=20,
+        hbm=(5,),
     )
     twin_stats = lax.ppermute(stats, "head", twin)
     piece = shape((pool_lines, line), bf16)
-    to_own, to_down, to_up, to_far, score_grad = call(
-        key_side,
-        (shape((pool_lines, line), f32), piece, piece, piece, shape((tokens, 2 * rows), bf16)),
+    to_down, to_up, to_far, rest_score_grad = call(
+        functools.partial(key_side, first=1),
+        (piece, piece, piece, shape((3 * piece_rows, cols), bf16)),
+        rest_scores,
+        rest_prob_grad,
+        stats,
+        twin_stats,
+        tops,
+        query_rows,
+        grad_rows,
+        flops=3 * 10**9,
+        traffic=10**6,
+        mib=20,
+    )
+    sum_far = lax.ppermute(to_far, "head", across)
+    sum_up = lax.ppermute(to_up, "head", up)
+    sum_down = lax.ppermute(to_down, "head", down)
+    to_own, score_grad = call(
+        functools.partial(key_side, first=0),
+        (shape((pool_lines, line), f32), shape((piece_rows, cols), bf16)),
         scores,
         prob_grad,
         stats,
         twin_stats,
+        tops,
         query_rows,
         grad_rows,
-        flops=3 * 10**9,
-        traffic=10**7,
+        flops=10**9,
+        traffic=10**6,
         mib=20,
     )
-    sum_up = lax.ppermute(to_up, "head", up)
-    sum_down = lax.ppermute(to_down, "head", down)
-    sum_far = lax.ppermute(to_far, "head", across)
     half_grad = shape((rows // 2, line), f32)
     query_mine, query_other = call(
         query_side,
         (half_grad, half_grad),
         score_grad,
+        rest_score_grad,
         keys,
-        scratch=(pltpu.VMEM((2 * rows, width), f32),),
+        rest_keys,
         flops=3 * 10**9,
         traffic=10**7,
     )

time: 156 us -> 151 us (0.968)
  waiting for transfers between devices: 57.6 us -> 54.2 us
    ppermute x1, starting transfers between devices: 10.7 us -> 3.37 us  [local(): from_far = lax.ppermute(mine, 'head', across)]
    ppermute x1, waiting for transfers between devices: 6.95 us -> 0.01 us  [local(): from_above = lax.ppermute(mine, 'head', down)]
    ppermute x1, starting transfers between devices: 2.17 us -> 8.59 us  [local(): from_above = lax.ppermute(mine, 'head', down)]
    ppermute x1, waiting for transfers between devices: 2.44 us -> 7.42 us  [local(): from_far = lax.ppermute(mine, 'head', across)]
    ppermute x1, waiting for transfers between devices: 2.39 us -> 0.01 us  [local(): from_below = lax.ppermute(mine, 'head', up)]
    all_to_all x4, waiting for transfers between devices: 32.2 us -> 34.5 us  [swap(): lax.all_to_all(x3, axis, split_axis=0, concat_axis=0, tiled=True)]
    all_to_all x4, starting transfers between devices: 26.2 us -> 24 us  [swap(): lax.all_to_all(x3, axis, split_axis=0, concat_axis=0, tiled=True)]
    ppermute x1, starting transfers between devices: 5.18 us -> 7.23 us  [local(): twin_stats = lax.ppermute(stats, 'head', twin)]
  transfers between devices with their start and end apart: 14 -> 14, of which waited for: 11 -> 9; matrix products, arithmetic and copies ran while one was open for 1% -> 1% of each run, Pallas kernels for 6% -> 8%
where the time goes in v5:
time: 151 us; the launch traced here: 150 us
  starting transfers between devices  63.6 us (42%)
  waiting for transfers between devices  54.2 us (36%)
  Pallas kernels  23.4 us (15%)
  local copies, waits for them, and re-layouts  7.67 us (5%)
    all_to_all x4, waiting for transfers between devices, swap(): lax.all_to_all(x3, axis, split_axis=0, concat_axis=0, tiled=True)  34.5 us
    all_to_all x4, starting transfers between devices, swap(): lax.all_to_all(x3, axis, split_axis=0, concat_axis=0, tiled=True)  24 us
    pallas_call x14, Pallas kernels, call(): pl.pallas_call(body, out_shape=out_shape, in_specs=specs, out_specs=jax.t...  23.4 us
    ppermute x1, starting transfers between devices, local(): from_above = lax.ppermute(mine, 'head', down)  8.59 us
    unnamed x23, local copies, waits for them, and re-layouts  7.67 us
    ppermute x1, waiting for transfers between devices, local(): from_far = lax.ppermute(mine, 'head', across)  7.42 us
    ppermute x1, starting transfers between devices, local(): twin_stats = lax.ppermute(stats, 'head', twin)  7.23 us
    ppermute x1, waiting for transfers between devices, local(): sum_far = lax.ppermute(to_far, 'head', across)  5.96 us
  transfers between devices with their start and end apart: 14, of which 9 were waited for; matrix products, arithmetic and copies ran while one was open for 1% of the time, Pallas kernels for 8%

profile of v5, /device:TPU:1, one launch (start us, length us, event | category | flops | bytes accessed | tf_op | source)
XLA Modules:
  0.0 149.9 jit_solution(6394218114357986827)
XLA Ops:
  1.3 2.3 %shard_map.59 = (bf16[640,128]{1,0:T(8,128)(2,1)S(1)}, f32[16,640]{1,0:T(8,128)S(1)}, bf16[256,128]{1,0:T(8,128)(2,1)}) custom-call(s32[32,128]{1,0:T(8,128)S(1)} %bitcast.16), custom_call_target="tpu_custom_call" | custom-call | tf_op jit(solution)/shard_map/pallas_call | solution.py:39
  3.7 10.5 %all-to-all-start = ((bf16[32,8,128]{2,1,0:T(8,128)(2,1)}), bf16[32,8,128]{2,1,0:T(8,128)(2,1)S(1)}, u32[]{:S(2)}, u32[]{:S(2)}) async-start(bf16[32,8,128]{2,1,0:T(8,128)(2,1)} %bitcast.3), calls=%async_computation | async-start | bytes 131072 | tf_op jit(solution)/shard_map/all_to_all | solution.py:315
  14.3 1.9 %copy.6.lat_ref = bf16[1280,576]{1,0:T(8,128)(2,1)S(1)} copy(bf16[1280,576]{0,1:T(8,128)(2,1)} %param.4) | data formatting | bytes 2949120 | tf_op args[0]
  16.2 1.3 shard_map.61.own_ref
  17.4 5.6 %all-to-all-done = bf16[32,8,128]{2,1,0:T(8,128)(2,1)S(1)} async-done(((bf16[32,8,128]{2,1,0:T(8,128)(2,1)}), bf16[32,8,128]{2,1,0:T(8,128)(2,1)S(1)}, u32[]{:S(2)}, u32[]{:S(2)}) %all-to-all-start) | async-done | bytes 65568 | tf_op jit(solution)/shard_map/all_to_all | solution.py:315
  24.2 3.9 %all-to-all-start.1 = ((bf16[32,8,1152]{2,1,0:T(8,128)(2,1)}), bf16[32,8,1152]{2,1,0:T(8,128)(2,1)S(1)}, u32[]{:S(2)}, u32[]{:S(2)}) async-start(bf16[32,8,1152]{2,1,0:T(8,128)(2,1)} %bitcast.5), calls=%async_computation.1 | async-start | bytes 1179648 | tf_op jit(solution)/shard_map/all_to_all | solution.py:315
  30.7 4.0 %collective-permute-start = (bf16[128,2304]{1,0:T(8,128)(2,1)S(1)}, bf16[128,2304]{1,0:T(8,128)(2,1)S(1)}, u32[]{:S(2)}, u32[]{:S(2)}) collective-permute-start(bf16[128,2304]{1,0:T(8,128)(2,1)S(1)} %copy-done.1), channel_id=1, source_target_pairs={{0,1},{1,0},{2,3},{3,2},{4,5},{5,4},{6,7},{7,6},{8,9},{9,8},{10,11... | collective-permute-start | bytes 1769480 | tf_op jit(solution)/shard_map/ppermute | solution.py:343
  34.8 1.9 %collective-permute-start.1 = (bf16[128,2048]{1,0:T(8,128)(2,1)S(1)}, bf16[128,2048]{1,0:T(8,128)(2,1)}, u32[]{:S(2)}, u32[]{:S(2)}) collective-permute-start(bf16[128,2048]{1,0:T(8,128)(2,1)S(1)} %copy-done.2), channel_id=1, source_target_pairs={{0,1},{1,0},{2,3},{3,2},{4,5},{5,4},{6,7},{7,6},{8,9},{9,8},{10,11... | collective-permute-start | bytes 1572872 | tf_op jit(solution)/shard_map/ppermute | solution.py:344
  36.7 7.3 %all-to-all-done.1 = bf16[32,8,1152]{2,1,0:T(8,128)(2,1)S(1)} async-done(((bf16[32,8,1152]{2,1,0:T(8,128)(2,1)}), bf16[32,8,1152]{2,1,0:T(8,128)(2,1)S(1)}, u32[]{:S(2)}, u32[]{:S(2)}) %all-to-all-start.1) | async-done | bytes 589856 | tf_op jit(solution)/shard_map/all_to_all | solution.py:315
  44.3 4.0 %collective-permute-start.2 = (bf16[144,1152]{1,0:T(8,128)(2,1)S(1)}, bf16[144,1152]{1,0:T(8,128)(2,1)S(1)}, u32[]{:S(2)}, u32[]{:S(2)}) collective-permute-start(bf16[144,1152]{1,0:T(8,128)(2,1)S(1)} %shard_map.63.own_ref), channel_id=1, source_target_pairs={{0,2},{1,3},{2,4},{3,5},{4,6},{5,7},{6,8},{7,9},{8,10},{9,11},{10,... | collective-permute-start | bytes 995336 | tf_op jit(solution)/shard_map/ppermute | solution.py:347
  48.3 8.6 %collective-permute-start.3 = (bf16[144,1152]{1,0:T(8,128)(2,1)S(1)}, bf16[144,1152]{1,0:T(8,128)(2,1)S(1)}, u32[]{:S(2)}, u32[]{:S(2)}) collective-permute-start(bf16[144,1152]{1,0:T(8,128)(2,1)S(1)} %shard_map.63.own_ref), channel_id=1, source_target_pairs={{0,14},{1,15},{2,0},{3,1},{4,2},{5,3},{6,4},{7,5},{8,6},{9,7},{10,... | collective-permute-start | bytes 995336 | tf_op jit(solution)/shard_map/ppermute | solution.py:348
  56.9 3.4 %collective-permute-start.4 = (bf16[144,1152]{1,0:T(8,128)(2,1)S(1)}, bf16[144,1152]{1,0:T(8,128)(2,1)S(1)}, u32[]{:S(2)}, u32[]{:S(2)}) collective-permute-start(bf16[144,1152]{1,0:T(8,128)(2,1)S(1)} %shard_map.63.own_ref), channel_id=1, source_target_pairs={{0,4},{1,13},{2,6},{3,15},{4,8},{5,1},{6,10},{7,3},{8,12},{9,5},{1... | collective-permute-start | bytes 995336 | tf_op jit(solution)/shard_map/ppermute | solution.py:349
  61.2 2.2 %shard_map.64 = (f32[288,1024]{1,0:T(8,128)S(1)}, f32[288,1024]{1,0:T(8,128)S(1)}, f32[8,1024]{1,0:T(8,128)S(1)}, bf16[288,576]{1,0:T(8,128)(2,1)S(1)}, bf16[102...) custom-call(bf16[144,1152]{1,0:T(8,128)(2,1)S(1)} %shard_map.63.own_ref, bf16[128,2304]{1,0:T(8,128)(2,1)S(1)} %copy-done.1, ...), custom_call_target="tpu_custom_call" | custom-call | flops 1000000000 | bytes 1000000 | tf_op jit(solution)/shard_map/pallas_call | solution.py:39
  63.4 7.4 %collective-permute-done.4.far_ref = bf16[144,1152]{1,0:T(8,128)(2,1)S(1)} collective-permute-done((bf16[144,1152]{1,0:T(8,128)(2,1)S(1)}, bf16[144,1152]{1,0:T(8,128)(2,1)S(1)}, u32[]{:S(2)}, u32[]{:S(2)}) %collective-permute-start.4) | collective-permute-done | bytes 331808 | tf_op jit(solution)/shard_map/ppermute | solution.py:349
  70.8 3.3 %shard_map.65 = (f32[864,1024]{1,0:T(8,128)S(1)}, f32[864,1024]{1,0:T(8,128)S(1)}, f32[8,1024]{1,0:T(8,128)S(1)}, f32[8,1024]{1,0:T(8,128)S(1)}, bf16[864,576]{1,0:T(8,128)(2,1)S(1)}) custom-call(bf16[144,1152]{1,0:T(8,128)(2,1)S(1)} %collective-permute-done.2.below_ref, bf16[144,1152]{1,0:T(8,128)(2,1)S(1)} %collective-permute-done.3.above_ref, ...), custom_call_target="tpu_custom_call" | custom-call | flops 3000000000 | bytes 1000000 | tf_op jit(solution)/shard_map/pallas_call | solution.py:39
  74.1 7.2 %collective-permute-start.5 = (f32[8,1024]{1,0:T(8,128)S(1)}, f32[8,1024]{1,0:T(8,128)S(1)}, u32[]{:S(2)}, u32[]{:S(2)}) collective-permute-start(f32[8,1024]{1,0:T(8,128)S(1)} %get-tuple-element.47.stat_ref), channel_id=1, source_target_pairs={{0,1},{1,0},{2,3},{3,2},{4,5},{5,4},{6,7},{7,6},{8,9},{9,8},{10,11... | collective-permute-start | bytes 98312 | tf_op jit(solution)/shard_map/ppermute | solution.py:392
  82.2 2.8 %shard_map.67 = (bf16[144,1152]{1,0:T(8,128)(2,1)S(1)}, bf16[144,1152]{1,0:T(8,128)(2,1)S(1)}, bf16[144,1152]{1,0:T(8,128)(2,1)S(1)}, bf16[864,1024]{1,0:T(8,128)(2,1)S(1)}) custom-call(f32[864,1024]{1,0:T(8,128)S(1)} %get-tuple-element.50.e_ref, f32[864,1024]{1,0:T(8,128)S(1)} %get-tuple-element.51.d_ref, f32[8,1024]{1,0:T(8,128)S(1)} %get-tuple-element.47.stat_ref, ...), custom_call_target="tpu_custom_call" | custom-call | flops 3000000000 | bytes 1000000 | tf_op jit(solution)/shard_map/pallas_call | solution.py:39
  85.0 1.9 %collective-permute-start.7 = (bf16[144,1152]{1,0:T(8,128)(2,1)S(1)}, bf16[144,1152]{1,0:T(8,128)(2,1)S(1)}, u32[]{:S(2)}, u32[]{:S(2)}) collective-permute-start(bf16[144,1152]{1,0:T(8,128)(2,1)S(1)} %get-tuple-element.61), channel_id=1, source_target_pairs={{0,2},{1,3},{2,4},{3,5},{4,6},{5,7},{6,8},{7,9},{8,10},{9,11},{10,... | collective-permute-start | bytes 995336 | tf_op jit(solution)/shard_map/ppermute | solution.py:409
  86.9 4.6 %collective-permute-start.8 = (bf16[144,1152]{1,0:T(8,128)(2,1)S(1)}, bf16[144,1152]{1,0:T(8,128)(2,1)S(1)}, u32[]{:S(2)}, u32[]{:S(2)}) collective-permute-start(bf16[144,1152]{1,0:T(8,128)(2,1)S(1)} %get-tuple-element.62), channel_id=1, source_target_pairs={{0,14},{1,15},{2,0},{3,1},{4,2},{5,3},{6,4},{7,5},{8,6},{9,7},{10,... | collective-permute-start | bytes 995336 | tf_op jit(solution)/shard_map/ppermute | solution.py:410
  91.5 2.1 %collective-permute-start.9 = (bf16[144,1152]{1,0:T(8,128)(2,1)S(1)}, bf16[144,1152]{1,0:T(8,128)(2,1)S(1)}, u32[]{:S(2)}, u32[]{:S(2)}) collective-permute-start(bf16[144,1152]{1,0:T(8,128)(2,1)S(1)} %get-tuple-element.63), channel_id=1, source_target_pairs={{0,4},{1,13},{2,6},{3,15},{4,8},{5,1},{6,10},{7,3},{8,12},{9,5},{1... | collective-permute-start | bytes 995336 | tf_op jit(solution)/shard_map/ppermute | solution.py:408
  94.8 2.4 %collective-permute-done.7.up_ref = bf16[144,1152]{1,0:T(8,128)(2,1)S(1)} collective-permute-done((bf16[144,1152]{1,0:T(8,128)(2,1)S(1)}, bf16[144,1152]{1,0:T(8,128)(2,1)S(1)}, u32[]{:S(2)}, u32[]{:S(2)}) %collective-permute-start.7) | collective-permute-done | bytes 331808 | tf_op jit(solution)/shard_map/ppermute | solution.py:409
  97.1 3.1 %collective-permute-done.8.down_ref = bf16[144,1152]{1,0:T(8,128)(2,1)S(1)} collective-permute-done((bf16[144,1152]{1,0:T(8,128)(2,1)S(1)}, bf16[144,1152]{1,0:T(8,128)(2,1)S(1)}, u32[]{:S(2)}, u32[]{:S(2)}) %collective-permute-start.8) | collective-permute-done | bytes 331808 | tf_op jit(solution)/shard_map/ppermute | solution.py:410
  100.2 6.0 %collective-permute-done.9.far_ref = bf16[144,1152]{1,0:T(8,128)(2,1)S(1)} collective-permute-done((bf16[144,1152]{1,0:T(8,128)(2,1)S(1)}, bf16[144,1152]{1,0:T(8,128)(2,1)S(1)}, u32[]{:S(2)}, u32[]{:S(2)}) %collective-permute-start.9) | collective-permute-done | bytes 331808 | tf_op jit(solution)/shard_map/ppermute | solution.py:408
  106.2 1.2 shard_map.70
  107.4 5.0 %all-to-all-start.2 = ((bf16[32,8,1152]{2,1,0:T(8,128)(2,1)}), bf16[32,8,1152]{2,1,0:T(8,128)(2,1)S(1)}, u32[]{:S(2)}, u32[]{:S(2)}) async-start(bf16[32,8,1152]{2,1,0:T(8,128)(2,1)} %bitcast.7), calls=%async_computation.2 | async-start | bytes 1179648 | tf_op jit(solution)/shard_map/all_to_all | solution.py:315
  112.4 1.5 copy-done.4
  113.9 1.2 copy-done.8
  115.1 3.7 %shard_map.68 = (f32[256,1152]{1,0:T(8,128)S(1)}, f32[256,1152]{1,0:T(8,128)}) custom-call(bf16[288,1024]{1,0:T(8,128)(2,1)S(1)} %get-tuple-element.49.ds_ref, bf16[864,1024]{1,0:T(8,128)(2,1)S(1)} %copy-done.4, bf16[288,576]{1,0:T(8,128)(2,1)S(1)} %get-tuple-element.53.k_ref, bf16[864,576]{1,0:T(8,128)(2,1)S(1)} %copy-done.8), custom_call_target="tpu_custom_call" | custom-call | flops 3000000000 | bytes 10000000 | tf_op jit(solution)/shard_map/pallas_call | solution.py:39
  118.8 1.9 %collective-permute-start.6 = (f32[256,1152]{1,0:T(8,128)}, f32[256,1152]{1,0:T(8,128)S(1)}, u32[]{:S(2)}, u32[]{:S(2)}) collective-permute-start(f32[256,1152]{1,0:T(8,128)} %get-tuple-element.56), channel_id=1, source_target_pairs={{0,1},{1,0},{2,3},{3,2},{4,5},{5,4},{6,7},{7,6},{8,9},{9,8},{10,11... | collective-permute-start | bytes 3538952 | tf_op jit(solution)/shard_map/ppermute | solution.py:436
  120.7 10.2 %all-to-all-done.2 = bf16[32,8,1152]{2,1,0:T(8,128)(2,1)S(1)} async-done(((bf16[32,8,1152]{2,1,0:T(8,128)(2,1)}), bf16[32,8,1152]{2,1,0:T(8,128)(2,1)S(1)}, u32[]{:S(2)}, u32[]{:S(2)}) %all-to-all-start.2) | async-done | bytes 589856 | tf_op jit(solution)/shard_map/all_to_all | solution.py:315
  131.9 4.6 %all-to-all-start.3 = ((bf16[16,8,1152]{2,1,0:T(8,128)(2,1)}), bf16[16,8,1152]{2,1,0:T(8,128)(2,1)S(1)}, u32[]{:S(2)}, u32[]{:S(2)}) async-start(bf16[16,8,1152]{2,1,0:T(8,128)(2,1)} %bitcast.9), calls=%async_computation.3 | async-start | bytes 589824 | tf_op jit(solution)/shard_map/all_to_all | solution.py:315
  137.5 11.4 %all-to-all-done.3 = bf16[16,8,1152]{2,1,0:T(8,128)(2,1)S(1)} async-done(((bf16[16,8,1152]{2,1,0:T(8,128)(2,1)}), bf16[16,8,1152]{2,1,0:T(8,128)(2,1)S(1)}, u32[]{:S(2)}, u32[]{:S(2)}) %all-to-all-start.3) | async-done | bytes 294944 | tf_op jit(solution)/shard_map/all_to_all | solution.py:315
  (34 shorter events, 10.7 us)
Async XLA Ops:
  0.6 0.7 copy-start
  3.7 19.3 %all-to-all-start = ((bf16[32,8,128]{2,1,0:T(8,128)(2,1)}), bf16[32,8,128]{2,1,0:T(8,128)(2,1)S(1)}, u32[]{:S(2)}, u32[]{:S(2)}) async-start(bf16[32,8,128]{2,1,0:T(8,128)(2,1)} %bitcast.3), calls=%async_computation | async-start | bytes 131072 | tf_op jit(solution)/shard_map/all_to_all | solution.py:315
  24.2 19.8 %all-to-all-start.1 = ((bf16[32,8,1152]{2,1,0:T(8,128)(2,1)}), bf16[32,8,1152]{2,1,0:T(8,128)(2,1)S(1)}, u32[]{:S(2)}, u32[]{:S(2)}) async-start(bf16[32,8,1152]{2,1,0:T(8,128)(2,1)} %bitcast.5), calls=%async_computation.1 | async-start | bytes 1179648 | tf_op jit(solution)/shard_map/all_to_all | solution.py:315
  28.1 2.6 %copy-start.1 = (bf16[128,2304]{1,0:T(8,128)(2,1)S(1)}, bf16[128,2304]{1,0:T(8,128)(2,1)}, u32[]{:S(2)}) copy-start(bf16[128,2304]{1,0:T(8,128)(2,1)} %q_ref) | copy-start | bytes 1769476
  28.1 6.6 %copy-start.2 = (bf16[128,2048]{1,0:T(8,128)(2,1)S(1)}, bf16[128,2048]{1,0:T(8,128)(2,1)}, u32[]{:S(2)}) copy-start(bf16[128,2048]{1,0:T(8,128)(2,1)} %g_ref) | copy-start | bytes 1572868
  29.3 0.7 copy-start.5
  30.0 0.8 copy-start.9
  30.7 29.5 %collective-permute-start = (bf16[128,2304]{1,0:T(8,128)(2,1)S(1)}, bf16[128,2304]{1,0:T(8,128)(2,1)S(1)}, u32[]{:S(2)}, u32[]{:S(2)}) collective-permute-start(bf16[128,2304]{1,0:T(8,128)(2,1)S(1)} %copy-done.1), channel_id=1, source_target_pairs={{0,1},{1,0},{2,3},{3,2},{4,5},{5,4},{6,7},{7,6},{8,9},{9,8},{10,11... | collective-permute-start | bytes 1769480 | tf_op jit(solution)/shard_map/ppermute | solution.py:343
  34.8 25.5 %collective-permute-start.1 = (bf16[128,2048]{1,0:T(8,128)(2,1)S(1)}, bf16[128,2048]{1,0:T(8,128)(2,1)}, u32[]{:S(2)}, u32[]{:S(2)}) collective-permute-start(bf16[128,2048]{1,0:T(8,128)(2,1)S(1)} %copy-done.2), channel_id=1, source_target_pairs={{0,1},{1,0},{2,3},{3,2},{4,5},{5,4},{6,7},{7,6},{8,9},{9,8},{10,11... | collective-permute-start | bytes 1572872 | tf_op jit(solution)/shard_map/ppermute | solution.py:344
  44.0 26.8 %copy-start.10 = (f32[864,128]{1,0:T(8,128)S(1)}, f32[864,128]{1,0:T(8,128)}, u32[]{:S(2)}) copy-start(f32[864,128]{1,0:T(8,128)} %copy-done.9) | copy-start | bytes 1327108
  44.3 19.1 %collective-permute-start.2 = (bf16[144,1152]{1,0:T(8,128)(2,1)S(1)}, bf16[144,1152]{1,0:T(8,128)(2,1)S(1)}, u32[]{:S(2)}, u32[]{:S(2)}) collective-permute-start(bf16[144,1152]{1,0:T(8,128)(2,1)S(1)} %shard_map.63.own_ref), channel_id=1, source_target_pairs={{0,2},{1,3},{2,4},{3,5},{4,6},{5,7},{6,8},{7,9},{8,10},{9,11},{10,... | collective-permute-start | bytes 995336 | tf_op jit(solution)/shard_map/ppermute | solution.py:347
  48.3 15.1 %collective-permute-start.3 = (bf16[144,1152]{1,0:T(8,128)(2,1)S(1)}, bf16[144,1152]{1,0:T(8,128)(2,1)S(1)}, u32[]{:S(2)}, u32[]{:S(2)}) collective-permute-start(bf16[144,1152]{1,0:T(8,128)(2,1)S(1)} %shard_map.63.own_ref), channel_id=1, source_target_pairs={{0,14},{1,15},{2,0},{3,1},{4,2},{5,3},{6,4},{7,5},{8,6},{9,7},{10,... | collective-permute-start | bytes 995336 | tf_op jit(solution)/shard_map/ppermute | solution.py:348
  56.9 13.9 %collective-permute-start.4 = (bf16[144,1152]{1,0:T(8,128)(2,1)S(1)}, bf16[144,1152]{1,0:T(8,128)(2,1)S(1)}, u32[]{:S(2)}, u32[]{:S(2)}) collective-permute-start(bf16[144,1152]{1,0:T(8,128)(2,1)S(1)} %shard_map.63.own_ref), channel_id=1, source_target_pairs={{0,4},{1,13},{2,6},{3,15},{4,8},{5,1},{6,10},{7,3},{8,12},{9,5},{1... | collective-permute-start | bytes 995336 | tf_op jit(solution)/shard_map/ppermute | solution.py:349
  60.3 0.9 copy-start.6
  74.1 10.9 %copy-start.7 = (bf16[864,576]{1,0:T(8,128)(2,1)}, bf16[864,576]{1,0:T(8,128)(2,1)S(1)}, u32[]{:S(2)}) copy-start(bf16[864,576]{1,0:T(8,128)(2,1)S(1)} %get-tuple-element.54.rest_k_ref) | copy-start | bytes 2985988
  74.1 8.1 %collective-permute-start.5 = (f32[8,1024]{1,0:T(8,128)S(1)}, f32[8,1024]{1,0:T(8,128)S(1)}, u32[]{:S(2)}, u32[]{:S(2)}) collective-permute-start(f32[8,1024]{1,0:T(8,128)S(1)} %get-tuple-element.47.stat_ref), channel_id=1, source_target_pairs={{0,1},{1,0},{2,3},{3,2},{4,5},{5,4},{6,7},{7,6},{8,9},{9,8},{10,11... | collective-permute-start | bytes 98312 | tf_op jit(solution)/shard_map/ppermute | solution.py:392
  85.0 9.8 %copy-start.3 = (bf16[864,1024]{1,0:T(8,128)(2,1)}, bf16[864,1024]{1,0:T(8,128)(2,1)S(1)}, u32[]{:S(2)}) copy-start(bf16[864,1024]{1,0:T(8,128)(2,1)S(1)} %get-tuple-element.52.rest_ref) | copy-start | bytes 5308420
  85.0 12.1 %collective-permute-start.7 = (bf16[144,1152]{1,0:T(8,128)(2,1)S(1)}, bf16[144,1152]{1,0:T(8,128)(2,1)S(1)}, u32[]{:S(2)}, u32[]{:S(2)}) collective-permute-start(bf16[144,1152]{1,0:T(8,128)(2,1)S(1)} %get-tuple-element.61), channel_id=1, source_target_pairs={{0,2},{1,3},{2,4},{3,5},{4,6},{5,7},{6,8},{7,9},{8,10},{9,11},{10,... | collective-permute-start | bytes 995336 | tf_op jit(solution)/shard_map/ppermute | solution.py:409
  86.9 13.3 %collective-permute-start.8 = (bf16[144,1152]{1,0:T(8,128)(2,1)S(1)}, bf16[144,1152]{1,0:T(8,128)(2,1)S(1)}, u32[]{:S(2)}, u32[]{:S(2)}) collective-permute-start(bf16[144,1152]{1,0:T(8,128)(2,1)S(1)} %get-tuple-element.62), channel_id=1, source_target_pairs={{0,14},{1,15},{2,0},{3,1},{4,2},{5,3},{6,4},{7,5},{8,6},{9,7},{10,... | collective-permute-start | bytes 995336 | tf_op jit(solution)/shard_map/ppermute | solution.py:410
  91.5 14.7 %collective-permute-start.9 = (bf16[144,1152]{1,0:T(8,128)(2,1)S(1)}, bf16[144,1152]{1,0:T(8,128)(2,1)S(1)}, u32[]{:S(2)}, u32[]{:S(2)}) collective-permute-start(bf16[144,1152]{1,0:T(8,128)(2,1)S(1)} %get-tuple-element.63), channel_id=1, source_target_pairs={{0,4},{1,13},{2,6},{3,15},{4,8},{5,1},{6,10},{7,3},{8,12},{9,5},{1... | collective-permute-start | bytes 995336 | tf_op jit(solution)/shard_map/ppermute | solution.py:408
  107.4 23.5 %all-to-all-start.2 = ((bf16[32,8,1152]{2,1,0:T(8,128)(2,1)}), bf16[32,8,1152]{2,1,0:T(8,128)(2,1)S(1)}, u32[]{:S(2)}, u32[]{:S(2)}) async-start(bf16[32,8,1152]{2,1,0:T(8,128)(2,1)} %bitcast.7), calls=%async_computation.2 | async-start | bytes 1179648 | tf_op jit(solution)/shard_map/all_to_all | solution.py:315
  112.4 1.5 copy-start.4
  113.9 1.2 copy-start.8
  118.8 17.7 %collective-permute-start.6 = (f32[256,1152]{1,0:T(8,128)}, f32[256,1152]{1,0:T(8,128)S(1)}, u32[]{:S(2)}, u32[]{:S(2)}) collective-permute-start(f32[256,1152]{1,0:T(8,128)} %get-tuple-element.56), channel_id=1, source_target_pairs={{0,1},{1,0},{2,3},{3,2},{4,5},{5,4},{6,7},{7,6},{8,9},{9,8},{10,11... | collective-permute-start | bytes 3538952 | tf_op jit(solution)/shard_map/ppermute | solution.py:436
  131.9 17.0 %all-to-all-start.3 = ((bf16[16,8,1152]{2,1,0:T(8,128)(2,1)}), bf16[16,8,1152]{2,1,0:T(8,128)(2,1)S(1)}, u32[]{:S(2)}, u32[]{:S(2)}) async-start(bf16[16,8,1152]{2,1,0:T(8,128)(2,1)} %bitcast.9), calls=%async_computation.3 | async-start | bytes 589824 | tf_op jit(solution)/shard_map/all_to_all | solution.py:315

commit v6 on v5

--- a/solution.py
+++ b/solution.py
@@ -72,29 +72,36 @@
         out_ref[:, u * width : (u + 1) * width] = lines.astype(bf16)
 
 
-def choose(picks_ref, hit_ref, info_ref, ask_ref, *, per_owner):
+def hits(picks_ref, blocks):
     picks, queries = picks_ref.shape
-    blocks = hit_ref.shape[0]
     block = iota((blocks, queries), 0)
     hit = jnp.zeros((blocks, queries), jnp.bool_)
     for k in range(picks):
         hit = jnp.logical_or(hit, picks_ref[k : k + 1, :] == block)
-    hit = one_hot(hit)
+    return one_hot(hit)
+
+
+def choose(picks_ref, hit_ref, ask_ref, *, per_owner):
+    blocks, queries = hit_ref.shape
+    hit = hits(picks_ref, blocks)
     hit_ref[...] = hit
-    count = dot(jnp.ones((8, queries), bf16), hit, 1, 1)
-    chosen = jnp.where(count > 0.5, 1.0, 0.0)
-    lo, hi = iota((blocks, blocks), 0), iota((blocks, blocks), 1)
-    same = jnp.logical_and(lo < hi, lo >= by20(hi[:1]) * per_owner)
-    rank = dot(chosen.astype(bf16), one_hot(same), 1, 0)
-    info_ref[0:8, :] = chosen
-    info_ref[8:16, :] = rank
-    chosen, rank = chosen[:1], rank[:1]
-    rows = ask_ref.shape[0]
-    row, col = iota((rows, blocks), 0), iota((1, blocks), 1)
-    key = jnp.where(chosen > 0.5, by20(col) * CAP + rank.astype(jnp.int32), -1)
-    local_id = (col - by20(col) * per_owner).astype(f32)
-    ask = jnp.sum(jnp.where((row >> 2) == key, local_id, 0.0), axis=1, keepdims=True)
-    ask_ref[...] = jnp.broadcast_to(ask, ask_ref.shape).astype(bf16)
+    count = dot(hit, jnp.ones((queries, 128), bf16), 1, 0)
+    row, lane = iota((blocks, 128), 0), iota((blocks, 128), 1)
+    owner = by20(row)
+    placed = one_hot(jnp.logical_and(count > 0.5, lane == row - owner * per_owner))
+    owners = ask_ref.shape[0]
+    member = one_hot(by20(iota((owners, blocks), 1)) == iota((owners, blocks), 0))
+    table = dot(member, placed, 1, 0)
+    before = one_hot(iota((128, 128), 0) < iota((128, 128), 1))
+    rank = dot(table.astype(bf16), before, 1, 0)
+    lane = iota((owners, 128), 1).astype(f32)
+    ids = []
+    for k in range(CAP):
+        here = jnp.logical_and(table > 0.5, rank == k)
+        ids.append(jnp.sum(jnp.where(here, lane, 0.0), axis=1, keepdims=True))
+    line = iota(ask_ref.shape, 1)
+    ask = jnp.where(line < LINES, ids[0][:, :, None], ids[1][:, :, None])
+    ask_ref[...] = ask.astype(bf16)
 
 
 def fetch(ask_ref, own_ref, out_ref):
@@ -105,17 +112,19 @@
 
 
 def arrange(
-    pos_ref, hit_ref, info_ref, ask_ref, bias_ref, rest_ref, send_ref, back_ref, sum_ref, place_ref,
-    *, first, per_dest,
+    pos_ref, hit_ref, ask_ref, bias_ref, near_ref, far_ref, send_ref, back_ref, sum_ref, place_ref,
+    *, first, per_dest, per_owner,
 ):
     blocks, queries = hit_ref.shape
     rows, slots = send_ref.shape
     head = pos_ref[1]
-    chosen8 = info_ref[0:8, :]
-    chosen = chosen8[:1]
-    rank = info_ref[8:9, :]
+    count = dot(jnp.ones((8, queries), bf16), hit_ref[...], 1, 1)
+    chosen8 = one_hot(count > 0.5)
+    chosen = count[:1]
     lo, hi = iota((blocks, blocks), 0), iota((blocks, blocks), 1)
-    order = dot(chosen8.astype(bf16), one_hot(lo < hi), 1, 0)[:1]
+    order = dot(chosen8, one_hot(lo < hi), 1, 0)[:1]
+    same = jnp.logical_and(lo < hi, lo >= by20(hi[:1]) * per_owner)
+    rank = dot(chosen8, one_hot(same), 1, 0)[:1]
     row = iota((rows, blocks), 0)
     slot = (row >> 2).astype(f32)
     here = jnp.where(jnp.logical_and(order == slot, chosen > 0.5), 1.0, 0.0)
@@ -127,11 +136,11 @@
     query_pos = first + pos_ref[0] * queries + iota((rows, queries), 1)
     base = block_id * BLOCK + (iota((rows, queries), 0) & 3) - query_pos
     for i, step in enumerate((0, -1, 1, 2)):
-        out_ref = rest_ref if i else bias_ref
+        out_ref = (bias_ref, near_ref, near_ref, far_ref)[i]
         for u in (0, 1):
             offset = near(head, step) * PART + u * LINES
             allowed = jnp.logical_and(picked > 0.5, base + offset <= 0)
-            at = (2 * max(i - 1, 0) + u) * rows
+            at = (2 * (i == 2) + u) * rows
             out_ref[at : at + rows, :] = jnp.where(allowed, 0.0, NEG)
     row = iota(send_ref.shape, 0)
     col = iota(send_ref.shape, 1)
@@ -200,23 +209,35 @@
     stat_ref[3:8, :] = jnp.zeros((5, stat_ref.shape[1]), f32)
 
 
-def score_rest(
-    below_ref, above_ref, far_ref, qs_ref, gs_ref, bias_hbm, first_ref,
+def score_near(
+    below_ref, above_ref, qs_ref, gs_ref, bias_hbm, e_ref, d_ref, stat_ref, k_ref, bias_ref, sem
+):
+    copy = pltpu.make_async_copy(bias_hbm, bias_ref, sem)
+    copy.start()
+    size = 2 * below_ref.shape[0]
+    unpack(below_ref, k_ref, 0)
+    unpack(above_ref, k_ref, size)
+    copy.wait()
+    for i in (0, 1):
+        at = slice(i * size, (i + 1) * size)
+        found = score_piece(k_ref[at, :], bias_ref[at, :], qs_ref, gs_ref, e_ref, d_ref, i * size)
+        for j in range(3):
+            stat_ref[3 * i + j : 3 * i + j + 1, :] = found[j]
+    stat_ref[6:8, :] = jnp.zeros((2, stat_ref.shape[1]), f32)
+
+
+def score_far(
+    far_ref, qs_ref, gs_ref, bias_hbm, own_ref, near_ref,
     e_ref, d_ref, stat_ref, tops_ref, k_ref, bias_ref, sem,
 ):
     copy = pltpu.make_async_copy(bias_hbm, bias_ref, sem)
     copy.start()
-    size = 2 * below_ref.shape[0]
-    pieces = (below_ref, above_ref, far_ref)
-    for i, piece_ref in enumerate(pieces):
-        unpack(piece_ref, k_ref, i * size)
+    unpack(far_ref, k_ref, 0)
     copy.wait()
-    found = [tuple(first_ref[i : i + 1, :] for i in range(3))]
-    for i in range(len(pieces)):
-        at = slice(i * size, (i + 1) * size)
-        found.append(
-            score_piece(k_ref[at, :], bias_ref[at, :], qs_ref, gs_ref, e_ref, d_ref, i * size)
-        )
+    found = [tuple(own_ref[j : j + 1, :] for j in range(3))]
+    for i in (0, 1):
+        found.append(tuple(near_ref[3 * i + j : 3 * i + j + 1, :] for j in range(3)))
+    found.append(score_piece(k_ref[...], bias_ref[...], qs_ref, gs_ref, e_ref, d_ref, 0))
     top = functools.reduce(jnp.maximum, [f[0] for f in found])
     weights = [jnp.exp(f[0] - top) for f in found]
     stat_ref[0:1, :] = top
@@ -255,14 +276,22 @@
             out_ref[:, u * width : (u + 1) * width] = both[u * lines : (u + 1) * lines, :]
 
 
-def query_side(ds_ref, rest_ref, k_ref, rest_k_ref, mine_ref, other_ref):
-    rows, width = mine_ref.shape[0], k_ref.shape[1]
+def query_side(ds0_ref, ds1_ref, ds2_ref, k0_ref, k1_ref, k2_ref, mine_ref, other_ref):
+    rows, width = mine_ref.shape[0], k0_ref.shape[1]
     for i, out_ref in enumerate((mine_ref, other_ref)):
         for u in (0, 1):
             at = slice((2 * i + u) * rows, (2 * i + u + 1) * rows)
-            part = dot(ds_ref[:, at], k_ref[...], 0, 0)
-            part = part + dot(rest_ref[:, at], rest_k_ref[...], 0, 0)
+            part = dot(ds0_ref[:, at], k0_ref[...], 0, 0)
+            part = part + dot(ds1_ref[:, at], k1_ref[...], 0, 0)
+            part = part + dot(ds2_ref[:, at], k2_ref[...], 0, 0)
             out_ref[:, u * width : (u + 1) * width] = part
+
+
+def join(pos_ref, up_ref, down_ref, got_ref, up_out_ref, down_out_ref):
+    core = (pos_ref[1] & 1).astype(f32)
+    got = got_ref[...].astype(f32)
+    up_out_ref[...] = (up_ref[...] + got * (1.0 - core)).astype(bf16)
+    down_out_ref[...] = (down_ref[...] + got * core).astype(bf16)
 
 
 def query_sum(mine_ref, got_ref, dq_ref):
@@ -277,9 +306,8 @@
         dq_ref[:, h2 * width : (h2 + 1) * width] = total[:, width:]
 
 
-def outgoing(back_ref, own_ref, up_ref, down_ref, far_ref, out_ref):
-    total = own_ref[...] + up_ref[...].astype(f32)
-    total = total + down_ref[...].astype(f32) + far_ref[...].astype(f32)
+def outgoing(back_ref, own_ref, up_ref, down_ref, out_ref):
+    total = own_ref[...] + up_ref[...].astype(f32) + down_ref[...].astype(f32)
     out_ref[...] = dot(back_ref[...], total.astype(bf16), 1, 0).astype(bf16)
 
 
@@ -306,7 +334,7 @@
     shape = jax.ShapeDtypeStruct
     up = [(i, (i + 2) % n_head) for i in range(n_head)]
     down = [(i, (i - 2) % n_head) for i in range(n_head)]
-    across = [(i, (i + 4 - 8 * (i & 1)) % n_head) for i in range(n_head)]
+    relay = [(i, (i + 2 - 4 * (i & 1)) % n_head) for i in range(n_head)]
     twin = [(i, i ^ 1) for i in range(n_head)]
 
     def swap(x, axis):
@@ -314,19 +342,21 @@
         x3 = x.reshape(n, -1, x.shape[1])
         return lax.all_to_all(x3, axis, split_axis=0, concat_axis=0, tiled=True).reshape(x.shape)
 
-    hit, info, ask = call(
+    hit, ask = call(
         functools.partial(choose, per_owner=per_owner),
-        (shape((blocks, queries), bf16), shape((16, blocks), f32), shape((slots, 128), bf16)),
+        (shape((blocks, queries), bf16), shape((n_ctx, CAP * LINES, 128), bf16)),
         picks.T,
     )
+    ask = ask.reshape(slots, 128)
     own = call(own_part, shape((per_owner * LINES, line), bf16), pos, latent, flops=10**9, traffic=10**6)
     asked = swap(ask, "ctx")
     lines_out = call(fetch, shape((slots, line), bf16), asked, own)
-    bias, rest_bias, send, back, sums, places = call(
-        functools.partial(arrange, first=first, per_dest=outs // PART),
+    bias, near_bias, far_bias, send, back, sums, places = call(
+        functools.partial(arrange, first=first, per_dest=outs // PART, per_owner=per_owner),
         (
             shape((piece_rows, queries), f32),
-            shape((3 * piece_rows, queries), f32),
+            shape((2 * piece_rows, queries), f32),
+            shape((piece_rows, queries), f32),
             shape((pool_lines, slots), bf16),
             shape((slots, pool_lines), bf16),
             shape((n_head * CAP * LINES, slots), bf16),
@@ -334,7 +364,6 @@
         ),
         pos,
         hit,
-        info,
         asked,
         flops=3 * 10**9,
         traffic=3 * 10**6,
@@ -346,7 +375,8 @@
     mine = call(multiply, shape((pool_lines, line), bf16), send, lines_in)
     from_below = lax.ppermute(mine, "head", up)
     from_above = lax.ppermute(mine, "head", down)
-    from_far = lax.ppermute(mine, "head", across)
+    onward = jnp.where(pos[1] & 1 == 0, from_below, from_above)
+    from_far = lax.ppermute(onward, "head", relay)
     rows = queries * (grad_out.shape[1] // LAT)
     cols = 2 * rows
 
@@ -373,69 +403,77 @@
         traffic=10**6,
         mib=20,
     )
-    rest_scores, rest_prob_grad, stats, tops, rest_keys = call(
-        score_rest,
-        (*arrays(3), row_stats, row_stats, shape((3 * piece_rows, width), bf16)),
+    near_scores, near_prob_grad, near_stats, near_keys = call(
+        score_near,
+        (*arrays(2), row_stats, shape((2 * piece_rows, width), bf16)),
         from_below,
         from_above,
+        query_rows,
+        grad_rows,
+        near_bias,
+        scratch=(pltpu.VMEM((2 * piece_rows, queries), f32), pltpu.SemaphoreType.DMA(())),
+        flops=2 * 10**9,
+        traffic=10**6,
+        mib=20,
+        hbm=(4,),
+    )
+    far_scores, far_prob_grad, stats, tops, far_keys = call(
+        score_far,
+        (*arrays(1), row_stats, row_stats, shape((piece_rows, width), bf16)),
         from_far,
         query_rows,
         grad_rows,
-        rest_bias,
+        far_bias,
         first_stats,
-        scratch=(pltpu.VMEM((3 * piece_rows, queries), f32), pltpu.SemaphoreType.DMA(())),
-        flops=3 * 10**9,
-        traffic=10**6,
-        mib=20,
-        hbm=(5,),
-    )
-    twin_stats = lax.ppermute(stats, "head", twin)
-    piece = shape((pool_lines, line), bf16)
-    to_down, to_up, to_far, rest_score_grad = call(
-        functools.partial(key_side, first=1),
-        (piece, piece, piece, shape((3 * piece_rows, cols), bf16)),
-        rest_scores,
-        rest_prob_grad,
-        stats,
-        twin_stats,
-        tops,
-        query_rows,
-        grad_rows,
-        flops=3 * 10**9,
-        traffic=10**6,
-        mib=20,
-    )
-    sum_far = lax.ppermute(to_far, "head", across)
-    sum_up = lax.ppermute(to_up, "head", up)
-    sum_down = lax.ppermute(to_down, "head", down)
-    to_own, score_grad = call(
-        functools.partial(key_side, first=0),
-        (shape((pool_lines, line), f32), shape((piece_rows, cols), bf16)),
-        scores,
-        prob_grad,
-        stats,
-        twin_stats,
-        tops,
-        query_rows,
-        grad_rows,
+        near_stats,
+        scratch=(pltpu.VMEM((piece_rows, queries), f32), pltpu.SemaphoreType.DMA(())),
         flops=10**9,
         traffic=10**6,
         mib=20,
-    )
+        hbm=(3,),
+    )
+    twin_stats = lax.ppermute(stats, "head", twin)
+
+    def key_grad(first, n, dtype, e, d):
+        return call(
+            functools.partial(key_side, first=first),
+            (shape((pool_lines, line), dtype),) * n + (shape((n * piece_rows, cols), bf16),),
+            e,
+            d,
+            stats,
+            twin_stats,
+            tops,
+            query_rows,
+            grad_rows,
+            flops=n * 10**9,
+            traffic=10**6,
+            mib=20,
+        )
+
+    to_far, far_score_grad = key_grad(3, 1, bf16, far_scores, far_prob_grad)
+    got_far = lax.ppermute(to_far, "head", relay)
+    to_down, to_up, near_score_grad = key_grad(1, 2, f32, near_scores, near_prob_grad)
+    to_own, score_grad = key_grad(0, 1, f32, scores, prob_grad)
+    piece = shape((pool_lines, line), bf16)
+    to_up, to_down = call(join, (piece, piece), pos, to_up, to_down, got_far)
+    sum_up = lax.ppermute(to_up, "head", up)
+    sum_down = lax.ppermute(to_down, "head", down)
     half_grad = shape((rows // 2, line), f32)
     query_mine, query_other = call(
         query_side,
         (half_grad, half_grad),
         score_grad,
-        rest_score_grad,
+        near_score_grad,
+        far_score_grad,
         keys,
-        rest_keys,
+        near_keys,
+        far_keys,
         flops=3 * 10**9,
         traffic=10**7,
     )
     query_got = lax.ppermute(query_other, "head", twin)
     query_grad = call(query_sum, shape(query.shape, bf16), query_mine, query_got)
-    outbox = call(outgoing, shape((slots, line), bf16), back, to_own, sum_up, sum_down, sum_far)
+    outbox = call(outgoing, shape((slots, line), bf16), back, to_own, sum_up, sum_down)
     inbox = swap(outbox, "ctx")
     totals = call(multiply, shape((n_head * CAP * LINES, line), bf16), sums, inbox)
     spread = swap(totals, "head")

time: 151 us -> 151 us (level)
  waiting for transfers between devices: 54.2 us -> 39 us
  starting transfers between devices: 63.6 us -> 77.7 us
    ppermute x2, waiting for transfers between devices: 13.4 us -> 2.63 us  [the longest x1 2.63 us: local(): got_far = lax.ppermute(to_far, 'head', relay)]
    all_to_all x4, starting transfers between devices: 24 us -> 32.3 us  [swap(): lax.all_to_all(x3, axis, split_axis=0, concat_axis=0, tiled=True)]
    ppermute x1, starting transfers between devices: 1.91 us -> 5.79 us  [local(): query_got = lax.ppermute(query_other, 'head', twin)]
    ppermute x1, starting transfers between devices: 7.23 us -> 4.6 us  [local(): twin_stats = lax.ppermute(stats, 'head', twin)]
    ppermute x1, starting transfers between devices: 4 us -> 6.53 us  [local(): twin_query = lax.ppermute(query, 'head', twin)]
    ppermute x1, waiting for transfers between devices: 3.11 us -> 0.9 us  [local(): sum_down = lax.ppermute(to_down, 'head', down)]
    all_to_all x4, waiting for transfers between devices: 34.5 us -> 32.4 us  [swap(): lax.all_to_all(x3, axis, split_axis=0, concat_axis=0, tiled=True)]
    ppermute x2, starting transfers between devices: 5.47 us -> 7.29 us  [the longest x1 3.64 us: local(): got_far = lax.ppermute(to_far, 'head', relay)]
  transfers between devices with their start and end apart: 14 -> 14, of which waited for: 9 -> 8; matrix products, arithmetic and copies ran while one was open for 1% -> 1% of each run, Pallas kernels for 8% -> 10%
where the time goes in v6:
time: 151 us; the launch traced here: 150 us
  starting transfers between devices  77.7 us (51%)
  waiting for transfers between devices  39 us (26%)
  Pallas kernels  23.9 us (16%)
  local copies, waits for them, and re-layouts  7.95 us (5%)
    all_to_all x4, waiting for transfers between devices, swap(): lax.all_to_all(x3, axis, split_axis=0, concat_axis=0, tiled=True)  32.4 us
    all_to_all x4, starting transfers between devices, swap(): lax.all_to_all(x3, axis, split_axis=0, concat_axis=0, tiled=True)  32.3 us
    pallas_call x17, Pallas kernels, call(): pl.pallas_call(body, out_shape=out_shape, in_specs=specs, out_specs=jax.t...  23.9 us
    ppermute x1, starting transfers between devices, local(): from_above = lax.ppermute(mine, 'head', down)  8.59 us
    unnamed x23, local copies, waits for them, and re-layouts  7.95 us
    ppermute x1, starting transfers between devices, local(): twin_query = lax.ppermute(query, 'head', twin)  6.53 us
    ppermute x1, starting transfers between devices, local(): query_got = lax.ppermute(query_other, 'head', twin)  5.79 us
    ppermute x1, starting transfers between devices, local(): sum_down = lax.ppermute(to_down, 'head', down)  4.75 us
  transfers between devices with their start and end apart: 14, of which 8 were waited for; matrix products, arithmetic and copies ran while one was open for 1% of the time, Pallas kernels for 10%

profile of v6, /device:TPU:1, one launch (start us, length us, event | category | flops | bytes accessed | tf_op | source)
XLA Modules:
  0.0 149.6 jit_solution(13193450071186493975)
XLA Ops:
  1.3 2.4 %shard_map.59 = (bf16[640,128]{1,0:T(8,128)(2,1)S(1)}, bf16[32,8,128]{2,1,0:T(8,128)(2,1)}) custom-call(s32[32,128]{1,0:T(8,128)S(1)} %bitcast.15), custom_call_target="tpu_custom_call" | custom-call | tf_op jit(solution)/shard_map/pallas_call | solution.py:39
  3.8 10.5 %all-to-all-start = ((bf16[32,8,128]{2,1,0:T(8,128)(2,1)}), bf16[32,8,128]{2,1,0:T(8,128)(2,1)S(1)}, u32[]{:S(2)}, u32[]{:S(2)}) async-start(bf16[32,8,128]{2,1,0:T(8,128)(2,1)} %get-tuple-element.41), calls=%async_computation | async-start | bytes 131072 | tf_op jit(solution)/shard_map/all_to_all | solution.py:343
  14.3 1.9 %copy.6.lat_ref = bf16[1280,576]{1,0:T(8,128)(2,1)S(1)} copy(bf16[1280,576]{0,1:T(8,128)(2,1)} %param.4) | data formatting | bytes 2949120 | tf_op args[0]
  16.2 1.3 shard_map.61.own_ref
  17.5 5.6 %all-to-all-done = bf16[32,8,128]{2,1,0:T(8,128)(2,1)S(1)} async-done(((bf16[32,8,128]{2,1,0:T(8,128)(2,1)}), bf16[32,8,128]{2,1,0:T(8,128)(2,1)S(1)}, u32[]{:S(2)}, u32[]{:S(2)}) %all-to-all-start) | async-done | bytes 65568 | tf_op jit(solution)/shard_map/all_to_all | solution.py:343
  23.1 1.2 shard_map.62
  24.3 3.9 %all-to-all-start.1 = ((bf16[32,8,1152]{2,1,0:T(8,128)(2,1)}), bf16[32,8,1152]{2,1,0:T(8,128)(2,1)S(1)}, u32[]{:S(2)}, u32[]{:S(2)}) async-start(bf16[32,8,1152]{2,1,0:T(8,128)(2,1)} %bitcast.4), calls=%async_computation.1 | async-start | bytes 1179648 | tf_op jit(solution)/shard_map/all_to_all | solution.py:343
  28.2 1.4 shard_map.60
  29.6 14.5 %all-to-all-done.1 = bf16[32,8,1152]{2,1,0:T(8,128)(2,1)S(1)} async-done(((bf16[32,8,1152]{2,1,0:T(8,128)(2,1)}), bf16[32,8,1152]{2,1,0:T(8,128)(2,1)S(1)}, u32[]{:S(2)}, u32[]{:S(2)}) %all-to-all-start.1) | async-done | bytes 589856 | tf_op jit(solution)/shard_map/all_to_all | solution.py:343
  44.3 4.0 %collective-permute-start.2 = (bf16[144,1152]{1,0:T(8,128)(2,1)S(1)}, bf16[144,1152]{1,0:T(8,128)(2,1)S(1)}, u32[]{:S(2)}, u32[]{:S(2)}) collective-permute-start(bf16[144,1152]{1,0:T(8,128)(2,1)S(1)} %shard_map.63.own_ref), channel_id=1, source_target_pairs={{0,2},{1,3},{2,4},{3,5},{4,6},{5,7},{6,8},{7,9},{8,10},{9,11},{10,... | collective-permute-start | bytes 995336 | tf_op jit(solution)/shard_map/ppermute | solution.py:376
  48.3 8.6 %collective-permute-start.3 = (bf16[144,1152]{1,0:T(8,128)(2,1)S(1)}, bf16[144,1152]{1,0:T(8,128)(2,1)S(1)}, u32[]{:S(2)}, u32[]{:S(2)}) collective-permute-start(bf16[144,1152]{1,0:T(8,128)(2,1)S(1)} %shard_map.63.own_ref), channel_id=1, source_target_pairs={{0,14},{1,15},{2,0},{3,1},{4,2},{5,3},{6,4},{7,5},{8,6},{9,7},{10,... | collective-permute-start | bytes 995336 | tf_op jit(solution)/shard_map/ppermute | solution.py:377
  56.9 6.5 %collective-permute-start = (bf16[128,2304]{1,0:T(8,128)(2,1)S(1)}, bf16[128,2304]{1,0:T(8,128)(2,1)S(1)}, u32[]{:S(2)}, u32[]{:S(2)}) collective-permute-start(bf16[128,2304]{1,0:T(8,128)(2,1)S(1)} %copy-done.1), channel_id=1, source_target_pairs={{0,1},{1,0},{2,3},{3,2},{4,5},{5,4},{6,7},{7,6},{8,9},{9,8},{10,11... | collective-permute-start | bytes 1769480 | tf_op jit(solution)/shard_map/ppermute | solution.py:372
  63.5 1.9 %collective-permute-start.1 = (bf16[128,2048]{1,0:T(8,128)(2,1)}, bf16[128,2048]{1,0:T(8,128)(2,1)S(1)}, u32[]{:S(2)}, u32[]{:S(2)}) collective-permute-start(bf16[128,2048]{1,0:T(8,128)(2,1)} %g_ref), channel_id=1, source_target_pairs={{0,1},{1,0},{2,3},{3,2},{4,5},{5,4},{6,7},{7,6},{8,9},{9,8},{10,11... | collective-permute-start | bytes 1572872 | tf_op jit(solution)/shard_map/ppermute | solution.py:373
  65.5 3.6 %collective-permute-start.4 = (bf16[144,1152]{1,0:T(8,128)(2,1)S(1)}, bf16[144,1152]{1,0:T(8,128)(2,1)S(1)}, u32[]{:S(2)}, u32[]{:S(2)}) collective-permute-start(bf16[144,1152]{1,0:T(8,128)(2,1)S(1)} %broadcast_select_fusion), channel_id=1, source_target_pairs={{0,2},{1,15},{2,4},{3,1},{4,6},{5,3},{6,8},{7,5},{8,10},{9,7},{10,... | collective-permute-start | bytes 995336 | tf_op jit(solution)/shard_map/ppermute | solution.py:379
  71.3 2.0 %shard_map.65 = (f32[576,1024]{1,0:T(8,128)S(1)}, f32[576,1024]{1,0:T(8,128)S(1)}, f32[8,1024]{1,0:T(8,128)S(1)}, bf16[576,576]{1,0:T(8,128)(2,1)S(1)}) custom-call(bf16[144,1152]{1,0:T(8,128)(2,1)S(1)} %collective-permute-done.2.below_ref, bf16[144,1152]{1,0:T(8,128)(2,1)S(1)} %collective-permute-done.3.above_ref, ...), custom_call_target="tpu_custom_call" | custom-call | flops 2000000000 | bytes 1000000 | tf_op jit(solution)/shard_map/pallas_call | solution.py:39
  74.2 1.3 shard_map.66
  75.5 4.6 %collective-permute-start.5 = (f32[8,1024]{1,0:T(8,128)S(1)}, f32[8,1024]{1,0:T(8,128)S(1)}, u32[]{:S(2)}, u32[]{:S(2)}) collective-permute-start(f32[8,1024]{1,0:T(8,128)S(1)} %get-tuple-element.55.stat_ref), channel_id=1, source_target_pairs={{0,1},{1,0},{2,3},{3,2},{4,5},{5,4},{6,7},{7,6},{8,9},{9,8},{10,11... | collective-permute-start | bytes 98312 | tf_op jit(solution)/shard_map/ppermute | solution.py:435
  82.1 3.6 %collective-permute-start.7 = (bf16[144,1152]{1,0:T(8,128)(2,1)S(1)}, bf16[144,1152]{1,0:T(8,128)(2,1)S(1)}, u32[]{:S(2)}, u32[]{:S(2)}) collective-permute-start(bf16[144,1152]{1,0:T(8,128)(2,1)S(1)} %get-tuple-element.75), channel_id=1, source_target_pairs={{0,2},{1,15},{2,4},{3,1},{4,6},{5,3},{6,8},{7,5},{8,10},{9,7},{10,... | collective-permute-start | bytes 995336 | tf_op jit(solution)/shard_map/ppermute | solution.py:454
  85.7 1.9 %shard_map.68 = (f32[144,1152]{1,0:T(8,128)S(1)}, f32[144,1152]{1,0:T(8,128)S(1)}, bf16[576,1024]{1,0:T(8,128)(2,1)S(1)}) custom-call(f32[576,1024]{1,0:T(8,128)S(1)} %get-tuple-element.58.e_ref, f32[576,1024]{1,0:T(8,128)S(1)} %get-tuple-element.59.d_ref, f32[8,1024]{1,0:T(8,128)S(1)} %get-tuple-element.55.stat_ref, ...), custom_call_target="tpu_custom_call" | custom-call | flops 2000000000 | bytes 1000000 | tf_op jit(solution)/shard_map/pallas_call | solution.py:39
  87.6 2.6 %collective-permute-done.7.got_ref = bf16[144,1152]{1,0:T(8,128)(2,1)S(1)} collective-permute-done((bf16[144,1152]{1,0:T(8,128)(2,1)S(1)}, bf16[144,1152]{1,0:T(8,128)(2,1)S(1)}, u32[]{:S(2)}, u32[]{:S(2)}) %collective-permute-start.7) | collective-permute-done | bytes 331808 | tf_op jit(solution)/shard_map/ppermute | solution.py:454
  90.9 1.9 %collective-permute-start.8 = (bf16[144,1152]{1,0:T(8,128)(2,1)S(1)}, bf16[144,1152]{1,0:T(8,128)(2,1)S(1)}, u32[]{:S(2)}, u32[]{:S(2)}) collective-permute-start(bf16[144,1152]{1,0:T(8,128)(2,1)S(1)} %get-tuple-element.76), channel_id=1, source_target_pairs={{0,2},{1,3},{2,4},{3,5},{4,6},{5,7},{6,8},{7,9},{8,10},{9,11},{10,... | collective-permute-start | bytes 995336 | tf_op jit(solution)/shard_map/ppermute | solution.py:459
  92.9 4.8 %collective-permute-start.9 = (bf16[144,1152]{1,0:T(8,128)(2,1)S(1)}, bf16[144,1152]{1,0:T(8,128)(2,1)S(1)}, u32[]{:S(2)}, u32[]{:S(2)}) collective-permute-start(bf16[144,1152]{1,0:T(8,128)(2,1)S(1)} %get-tuple-element.77), channel_id=1, source_target_pairs={{0,14},{1,15},{2,0},{3,1},{4,2},{5,3},{6,4},{7,5},{8,6},{9,7},{10,... | collective-permute-start | bytes 995336 | tf_op jit(solution)/shard_map/ppermute | solution.py:460
  97.6 1.1 shard_map.67
  98.8 2.2 %collective-permute-done.8.up_ref = bf16[144,1152]{1,0:T(8,128)(2,1)S(1)} collective-permute-done((bf16[144,1152]{1,0:T(8,128)(2,1)S(1)}, bf16[144,1152]{1,0:T(8,128)(2,1)S(1)}, u32[]{:S(2)}, u32[]{:S(2)}) %collective-permute-start.8) | collective-permute-done | bytes 331808 | tf_op jit(solution)/shard_map/ppermute | solution.py:459
  101.8 1.2 shard_map.73
  103.0 5.4 %all-to-all-start.2 = ((bf16[32,8,1152]{2,1,0:T(8,128)(2,1)}), bf16[32,8,1152]{2,1,0:T(8,128)(2,1)S(1)}, u32[]{:S(2)}, u32[]{:S(2)}) async-start(bf16[32,8,1152]{2,1,0:T(8,128)(2,1)} %bitcast.6), calls=%async_computation.2 | async-start | bytes 1179648 | tf_op jit(solution)/shard_map/all_to_all | solution.py:343
  109.5 1.3 copy-done.6
  110.7 1.1 copy-done.10
  111.8 4.1 %shard_map.70 = (f32[256,1152]{1,0:T(8,128)S(1)}, f32[256,1152]{1,0:T(8,128)}) custom-call(bf16[288,1024]{1,0:T(8,128)(2,1)S(1)} %copy-done.3, bf16[576,1024]{1,0:T(8,128)(2,1)S(1)} %copy-done.6, bf16[288,1024]{1,0:T(8,128)(2,1)S(1)} %get-tuple-element.63.ds2_ref, bf16[288,576]{1,0:T(8,128)(2,1)S(1)} %copy-done.8, bf16[576,576]{1,0:T(8,128)(2,1)S(1)} %copy-done.10, ...), custom_call_target="tpu_custom_call" | custom-call | flops 3000000000 | bytes 10000000 | tf_op jit(solution)/shard_map/pallas_call | solution.py:39
  115.9 5.8 %collective-permute-start.6 = (f32[256,1152]{1,0:T(8,128)}, f32[256,1152]{1,0:T(8,128)S(1)}, u32[]{:S(2)}, u32[]{:S(2)}) collective-permute-start(f32[256,1152]{1,0:T(8,128)} %get-tuple-element.68), channel_id=1, source_target_pairs={{0,1},{1,0},{2,3},{3,2},{4,5},{5,4},{6,7},{7,6},{8,9},{9,8},{10,11... | collective-permute-start | bytes 3538952 | tf_op jit(solution)/shard_map/ppermute | solution.py:474
  123.7 12.5 %all-to-all-start.3 = ((bf16[16,8,1152]{2,1,0:T(8,128)(2,1)}), bf16[16,8,1152]{2,1,0:T(8,128)(2,1)S(1)}, u32[]{:S(2)}, u32[]{:S(2)}) async-start(bf16[16,8,1152]{2,1,0:T(8,128)(2,1)} %bitcast.8), calls=%async_computation.3 | async-start | bytes 589824 | tf_op jit(solution)/shard_map/all_to_all | solution.py:343
  137.2 11.4 %all-to-all-done.3 = bf16[16,8,1152]{2,1,0:T(8,128)(2,1)S(1)} async-done(((bf16[16,8,1152]{2,1,0:T(8,128)(2,1)}), bf16[16,8,1152]{2,1,0:T(8,128)(2,1)S(1)}, u32[]{:S(2)}, u32[]{:S(2)}) %all-to-all-start.3) | async-done | bytes 294944 | tf_op jit(solution)/shard_map/all_to_all | solution.py:343
  (38 shorter events, 12.7 us)
Async XLA Ops:
  0.6 0.7 copy-start
  3.8 19.3 %all-to-all-start = ((bf16[32,8,128]{2,1,0:T(8,128)(2,1)}), bf16[32,8,128]{2,1,0:T(8,128)(2,1)S(1)}, u32[]{:S(2)}, u32[]{:S(2)}) async-start(bf16[32,8,128]{2,1,0:T(8,128)(2,1)} %get-tuple-element.41), calls=%async_computation | async-start | bytes 131072 | tf_op jit(solution)/shard_map/all_to_all | solution.py:343
  24.3 19.8 %all-to-all-start.1 = ((bf16[32,8,1152]{2,1,0:T(8,128)(2,1)}), bf16[32,8,1152]{2,1,0:T(8,128)(2,1)S(1)}, u32[]{:S(2)}, u32[]{:S(2)}) async-start(bf16[32,8,1152]{2,1,0:T(8,128)(2,1)} %bitcast.4), calls=%async_computation.1 | async-start | bytes 1179648 | tf_op jit(solution)/shard_map/all_to_all | solution.py:343
  28.2 28.8 %copy-start.1 = (bf16[128,2304]{1,0:T(8,128)(2,1)S(1)}, bf16[128,2304]{1,0:T(8,128)(2,1)}, u32[]{:S(2)}) copy-start(bf16[128,2304]{1,0:T(8,128)(2,1)} %q_ref) | copy-start | bytes 1769476
  44.3 21.1 %collective-permute-start.2 = (bf16[144,1152]{1,0:T(8,128)(2,1)S(1)}, bf16[144,1152]{1,0:T(8,128)(2,1)S(1)}, u32[]{:S(2)}, u32[]{:S(2)}) collective-permute-start(bf16[144,1152]{1,0:T(8,128)(2,1)S(1)} %shard_map.63.own_ref), channel_id=1, source_target_pairs={{0,2},{1,3},{2,4},{3,5},{4,6},{5,7},{6,8},{7,9},{8,10},{9,11},{10,... | collective-permute-start | bytes 995336 | tf_op jit(solution)/shard_map/ppermute | solution.py:376
  48.3 17.1 %collective-permute-start.3 = (bf16[144,1152]{1,0:T(8,128)(2,1)S(1)}, bf16[144,1152]{1,0:T(8,128)(2,1)S(1)}, u32[]{:S(2)}, u32[]{:S(2)}) collective-permute-start(bf16[144,1152]{1,0:T(8,128)(2,1)S(1)} %shard_map.63.own_ref), channel_id=1, source_target_pairs={{0,14},{1,15},{2,0},{3,1},{4,2},{5,3},{6,4},{7,5},{8,6},{9,7},{10,... | collective-permute-start | bytes 995336 | tf_op jit(solution)/shard_map/ppermute | solution.py:377
  56.9 12.2 %collective-permute-start = (bf16[128,2304]{1,0:T(8,128)(2,1)S(1)}, bf16[128,2304]{1,0:T(8,128)(2,1)S(1)}, u32[]{:S(2)}, u32[]{:S(2)}) collective-permute-start(bf16[128,2304]{1,0:T(8,128)(2,1)S(1)} %copy-done.1), channel_id=1, source_target_pairs={{0,1},{1,0},{2,3},{3,2},{4,5},{5,4},{6,7},{7,6},{8,9},{9,8},{10,11... | collective-permute-start | bytes 1769480 | tf_op jit(solution)/shard_map/ppermute | solution.py:372
  63.5 5.7 %collective-permute-start.1 = (bf16[128,2048]{1,0:T(8,128)(2,1)}, bf16[128,2048]{1,0:T(8,128)(2,1)S(1)}, u32[]{:S(2)}, u32[]{:S(2)}) collective-permute-start(bf16[128,2048]{1,0:T(8,128)(2,1)} %g_ref), channel_id=1, source_target_pairs={{0,1},{1,0},{2,3},{3,2},{4,5},{5,4},{6,7},{7,6},{8,9},{9,8},{10,11... | collective-permute-start | bytes 1572872 | tf_op jit(solution)/shard_map/ppermute | solution.py:373
  65.5 8.7 %collective-permute-start.4 = (bf16[144,1152]{1,0:T(8,128)(2,1)S(1)}, bf16[144,1152]{1,0:T(8,128)(2,1)S(1)}, u32[]{:S(2)}, u32[]{:S(2)}) collective-permute-start(bf16[144,1152]{1,0:T(8,128)(2,1)S(1)} %broadcast_select_fusion), channel_id=1, source_target_pairs={{0,2},{1,15},{2,4},{3,1},{4,6},{5,3},{6,8},{7,5},{8,10},{9,7},{10,... | collective-permute-start | bytes 995336 | tf_op jit(solution)/shard_map/ppermute | solution.py:379
  69.2 1.0 copy-start.4
  71.3 2.0 %copy-start.7 = (bf16[288,576]{1,0:T(8,128)(2,1)}, bf16[288,576]{1,0:T(8,128)(2,1)S(1)}, u32[]{:S(2)}) copy-start(bf16[288,576]{1,0:T(8,128)(2,1)S(1)} %get-tuple-element.64.k0_ref) | copy-start | bytes 995332
  73.3 0.9 copy-start.9
  75.5 5.4 %collective-permute-start.5 = (f32[8,1024]{1,0:T(8,128)S(1)}, f32[8,1024]{1,0:T(8,128)S(1)}, u32[]{:S(2)}, u32[]{:S(2)}) collective-permute-start(f32[8,1024]{1,0:T(8,128)S(1)} %get-tuple-element.55.stat_ref), channel_id=1, source_target_pairs={{0,1},{1,0},{2,3},{3,2},{4,5},{5,4},{6,7},{7,6},{8,9},{9,8},{10,11... | collective-permute-start | bytes 98312 | tf_op jit(solution)/shard_map/ppermute | solution.py:435
  82.1 8.2 %collective-permute-start.7 = (bf16[144,1152]{1,0:T(8,128)(2,1)S(1)}, bf16[144,1152]{1,0:T(8,128)(2,1)S(1)}, u32[]{:S(2)}, u32[]{:S(2)}) collective-permute-start(bf16[144,1152]{1,0:T(8,128)(2,1)S(1)} %get-tuple-element.75), channel_id=1, source_target_pairs={{0,2},{1,15},{2,4},{3,1},{4,6},{5,3},{6,8},{7,5},{8,10},{9,7},{10,... | collective-permute-start | bytes 995336 | tf_op jit(solution)/shard_map/ppermute | solution.py:454
  87.6 11.2 %copy-start.5 = (bf16[576,1024]{1,0:T(8,128)(2,1)}, bf16[576,1024]{1,0:T(8,128)(2,1)S(1)}, u32[]{:S(2)}) copy-start(bf16[576,1024]{1,0:T(8,128)(2,1)S(1)} %get-tuple-element.60.ds1_ref) | copy-start | bytes 3538948
  90.9 10.0 %collective-permute-start.8 = (bf16[144,1152]{1,0:T(8,128)(2,1)S(1)}, bf16[144,1152]{1,0:T(8,128)(2,1)S(1)}, u32[]{:S(2)}, u32[]{:S(2)}) collective-permute-start(bf16[144,1152]{1,0:T(8,128)(2,1)S(1)} %get-tuple-element.76), channel_id=1, source_target_pairs={{0,2},{1,3},{2,4},{3,5},{4,6},{5,7},{6,8},{7,9},{8,10},{9,11},{10,... | collective-permute-start | bytes 995336 | tf_op jit(solution)/shard_map/ppermute | solution.py:459
  92.9 9.0 %collective-permute-start.9 = (bf16[144,1152]{1,0:T(8,128)(2,1)S(1)}, bf16[144,1152]{1,0:T(8,128)(2,1)S(1)}, u32[]{:S(2)}, u32[]{:S(2)}) collective-permute-start(bf16[144,1152]{1,0:T(8,128)(2,1)S(1)} %get-tuple-element.77), channel_id=1, source_target_pairs={{0,14},{1,15},{2,0},{3,1},{4,2},{5,3},{6,4},{7,5},{8,6},{9,7},{10,... | collective-permute-start | bytes 995336 | tf_op jit(solution)/shard_map/ppermute | solution.py:460
  98.7 4.3 %copy-start.2 = (bf16[288,1024]{1,0:T(8,128)(2,1)}, bf16[288,1024]{1,0:T(8,128)(2,1)S(1)}, u32[]{:S(2)}) copy-start(bf16[288,1024]{1,0:T(8,128)(2,1)S(1)} %get-tuple-element.57.ds0_ref) | copy-start | bytes 1769476
  101.8 6.6 %copy-start.8 = (bf16[288,576]{1,0:T(8,128)(2,1)S(1)}, bf16[288,576]{1,0:T(8,128)(2,1)}, u32[]{:S(2)}) copy-start(bf16[288,576]{1,0:T(8,128)(2,1)} %copy-done.7) | copy-start | bytes 995332
  103.0 19.7 %all-to-all-start.2 = ((bf16[32,8,1152]{2,1,0:T(8,128)(2,1)}), bf16[32,8,1152]{2,1,0:T(8,128)(2,1)S(1)}, u32[]{:S(2)}, u32[]{:S(2)}) async-start(bf16[32,8,1152]{2,1,0:T(8,128)(2,1)} %bitcast.6), calls=%async_computation.2 | async-start | bytes 1179648 | tf_op jit(solution)/shard_map/all_to_all | solution.py:343
  108.4 1.1 copy-start.3
  109.5 1.3 copy-start.6
  110.7 1.1 copy-start.10
  115.9 20.3 %collective-permute-start.6 = (f32[256,1152]{1,0:T(8,128)}, f32[256,1152]{1,0:T(8,128)S(1)}, u32[]{:S(2)}, u32[]{:S(2)}) collective-permute-start(f32[256,1152]{1,0:T(8,128)} %get-tuple-element.68), channel_id=1, source_target_pairs={{0,1},{1,0},{2,3},{3,2},{4,5},{5,4},{6,7},{7,6},{8,9},{9,8},{10,11... | collective-permute-start | bytes 3538952 | tf_op jit(solution)/shard_map/ppermute | solution.py:474
  123.7 24.9 %all-to-all-start.3 = ((bf16[16,8,1152]{2,1,0:T(8,128)(2,1)}), bf16[16,8,1152]{2,1,0:T(8,128)(2,1)S(1)}, u32[]{:S(2)}, u32[]{:S(2)}) async-start(bf16[16,8,1152]{2,1,0:T(8,128)(2,1)} %bitcast.8), calls=%async_computation.3 | async-start | bytes 589824 | tf_op jit(solution)/shard_map/all_to_all | solution.py:343

commit v7 on v6

--- a/solution.py
+++ b/solution.py
@@ -75,10 +75,10 @@
 def hits(picks_ref, blocks):
     picks, queries = picks_ref.shape
     block = iota((blocks, queries), 0)
-    hit = jnp.zeros((blocks, queries), jnp.bool_)
+    least = jnp.full((blocks, queries), blocks, jnp.int32)
     for k in range(picks):
-        hit = jnp.logical_or(hit, picks_ref[k : k + 1, :] == block)
-    return one_hot(hit)
+        least = jnp.minimum(least, picks_ref[k : k + 1, :] ^ block)
+    return one_hot(least == 0)
 
 
 def choose(picks_ref, hit_ref, ask_ref, *, per_owner):
@@ -287,13 +287,6 @@
             out_ref[:, u * width : (u + 1) * width] = part
 
 
-def join(pos_ref, up_ref, down_ref, got_ref, up_out_ref, down_out_ref):
-    core = (pos_ref[1] & 1).astype(f32)
-    got = got_ref[...].astype(f32)
-    up_out_ref[...] = (up_ref[...] + got * (1.0 - core)).astype(bf16)
-    down_out_ref[...] = (down_ref[...] + got * core).astype(bf16)
-
-
 def query_sum(mine_ref, got_ref, dq_ref):
     queries = dq_ref.shape[0]
     heads, line = mine_ref.shape[0] // queries, mine_ref.shape[1]
@@ -306,8 +299,9 @@
         dq_ref[:, h2 * width : (h2 + 1) * width] = total[:, width:]
 
 
-def outgoing(back_ref, own_ref, up_ref, down_ref, out_ref):
-    total = own_ref[...] + up_ref[...].astype(f32) + down_ref[...].astype(f32)
+def outgoing(back_ref, own_ref, up_ref, down_ref, far_ref, out_ref):
+    total = own_ref[...] + up_ref[...].astype(f32)
+    total = total + down_ref[...].astype(f32) + far_ref[...].astype(f32)
     out_ref[...] = dot(back_ref[...], total.astype(bf16), 1, 0).astype(bf16)
 
 
@@ -334,6 +328,7 @@
     shape = jax.ShapeDtypeStruct
     up = [(i, (i + 2) % n_head) for i in range(n_head)]
     down = [(i, (i - 2) % n_head) for i in range(n_head)]
+    across = [(i, (i + 4 - 8 * (i & 1)) % n_head) for i in range(n_head)]
     relay = [(i, (i + 2 - 4 * (i & 1)) % n_head) for i in range(n_head)]
     twin = [(i, i ^ 1) for i in range(n_head)]
 
@@ -373,6 +368,7 @@
     twin_grad = lax.ppermute(grad_out, "head", twin)
     lines_in = swap(lines_out, "ctx")
     mine = call(multiply, shape((pool_lines, line), bf16), send, lines_in)
+    mine, twin_query, twin_grad = lax.optimization_barrier((mine, twin_query, twin_grad))
     from_below = lax.ppermute(mine, "head", up)
     from_above = lax.ppermute(mine, "head", down)
     onward = jnp.where(pos[1] & 1 == 0, from_below, from_above)
@@ -401,7 +397,7 @@
         bias,
         flops=10**9,
         traffic=10**6,
-        mib=20,
+        mib=14,
     )
     near_scores, near_prob_grad, near_stats, near_keys = call(
         score_near,
@@ -414,7 +410,7 @@
         scratch=(pltpu.VMEM((2 * piece_rows, queries), f32), pltpu.SemaphoreType.DMA(())),
         flops=2 * 10**9,
         traffic=10**6,
-        mib=20,
+        mib=14,
         hbm=(4,),
     )
     far_scores, far_prob_grad, stats, tops, far_keys = call(
@@ -429,7 +425,7 @@
         scratch=(pltpu.VMEM((piece_rows, queries), f32), pltpu.SemaphoreType.DMA(())),
         flops=10**9,
         traffic=10**6,
-        mib=20,
+        mib=14,
         hbm=(3,),
     )
     twin_stats = lax.ppermute(stats, "head", twin)
@@ -447,17 +443,15 @@
             grad_rows,
             flops=n * 10**9,
             traffic=10**6,
-            mib=20,
+            mib=14,
         )
 
     to_far, far_score_grad = key_grad(3, 1, bf16, far_scores, far_prob_grad)
-    got_far = lax.ppermute(to_far, "head", relay)
-    to_down, to_up, near_score_grad = key_grad(1, 2, f32, near_scores, near_prob_grad)
-    to_own, score_grad = key_grad(0, 1, f32, scores, prob_grad)
-    piece = shape((pool_lines, line), bf16)
-    to_up, to_down = call(join, (piece, piece), pos, to_up, to_down, got_far)
+    sum_far = lax.ppermute(to_far, "head", across)
+    to_down, to_up, near_score_grad = key_grad(1, 2, bf16, near_scores, near_prob_grad)
     sum_up = lax.ppermute(to_up, "head", up)
     sum_down = lax.ppermute(to_down, "head", down)
+    to_own, score_grad = key_grad(0, 1, f32, scores, prob_grad)
     half_grad = shape((rows // 2, line), f32)
     query_mine, query_other = call(
         query_side,
@@ -473,7 +467,7 @@
     )
     query_got = lax.ppermute(query_other, "head", twin)
     query_grad = call(query_sum, shape(query.shape, bf16), query_mine, query_got)
-    outbox = call(outgoing, shape((slots, line), bf16), back, to_own, sum_up, sum_down)
+    outbox = call(outgoing, shape((slots, line), bf16), back, to_own, sum_up, sum_down, sum_far)
     inbox = swap(outbox, "ctx")
     totals = call(multiply, shape((n_head * CAP * LINES, line), bf16), sums, inbox)
     spread = swap(totals, "head")

time: 151 us -> 148 us (0.980)
  starting transfers between devices: 77.7 us -> 71.2 us
  waiting for transfers between devices: 39 us -> 43.5 us
    all_to_all x4, starting transfers between devices: 32.3 us -> 26.3 us  [swap(): lax.all_to_all(x3, axis, split_axis=0, concat_axis=0, tiled=True)]
    ppermute x1, waiting for transfers between devices: 2.15 us -> 6.35 us  [local(): sum_up = lax.ppermute(to_up, 'head', up)]
    ppermute x1, starting transfers between devices: 4.6 us -> 7.65 us  [local(): twin_stats = lax.ppermute(stats, 'head', twin)]
    ppermute x1, starting transfers between devices: 5.79 us -> 2.75 us  [local(): query_got = lax.ppermute(query_other, 'head', twin)]
    ppermute x1, waiting for transfers between devices: 2.63 us -> 0.01 us  [local(): sum_far = lax.ppermute(to_far, 'head', across)]
    ppermute x1, waiting for transfers between devices: 0.01 us -> 2.56 us  [local(): from_below = lax.ppermute(mine, 'head', up)]
    ppermute x1, starting transfers between devices: 6.53 us -> 4 us  [local(): twin_query = lax.ppermute(query, 'head', twin)]
    unnamed x23 -> x21, local copies, waits for them, and re-layouts: 7.95 us -> 7.38 us
  transfers between devices with their start and end apart: 14 -> 14, of which waited for: 8 -> 8; matrix products, arithmetic and copies ran while one was open for 1% -> 1% of each run, Pallas kernels for 10% -> 11%
where the time goes in v7:
time: 148 us; the launch traced here: 147 us
  starting transfers between devices  71.2 us (48%)
  waiting for transfers between devices  43.5 us (29%)
  Pallas kernels  24.4 us (16%)
  local copies, waits for them, and re-layouts  7.38 us (5%)
    all_to_all x4, waiting for transfers between devices, swap(): lax.all_to_all(x3, axis, split_axis=0, concat_axis=0, tiled=True)  32.2 us
    all_to_all x4, starting transfers between devices, swap(): lax.all_to_all(x3, axis, split_axis=0, concat_axis=0, tiled=True)  26.3 us
    pallas_call x16, Pallas kernels, call(): pl.pallas_call(body, out_shape=out_shape, in_specs=specs, out_specs=jax.t...  24.4 us
    ppermute x1, starting transfers between devices, local(): from_above = lax.ppermute(mine, 'head', down)  8.59 us
    ppermute x1, starting transfers between devices, local(): twin_stats = lax.ppermute(stats, 'head', twin)  7.65 us
    unnamed x21, local copies, waits for them, and re-layouts  7.38 us
    ppermute x1, waiting for transfers between devices, local(): sum_up = lax.ppermute(to_up, 'head', up)  6.35 us
    ppermute x1, starting transfers between devices, local(): from_far = lax.ppermute(onward, 'head', relay)  5.02 us
  transfers between devices with their start and end apart: 14, of which 8 were waited for; matrix products, arithmetic and copies ran while one was open for 1% of the time, Pallas kernels for 11%

profile of v7, /device:TPU:1, one launch (start us, length us, event | category | flops | bytes accessed | tf_op | source)
XLA Modules:
  0.0 147.5 jit_solution(1735733042114472447)
XLA Ops:
  1.3 2.3 %shard_map.59 = (bf16[640,128]{1,0:T(8,128)(2,1)S(1)}, bf16[32,8,128]{2,1,0:T(8,128)(2,1)}) custom-call(s32[32,128]{1,0:T(8,128)S(1)} %bitcast.15), custom_call_target="tpu_custom_call" | custom-call | tf_op jit(solution)/shard_map/pallas_call | solution.py:39
  3.7 10.5 %all-to-all-start = ((bf16[32,8,128]{2,1,0:T(8,128)(2,1)}), bf16[32,8,128]{2,1,0:T(8,128)(2,1)S(1)}, u32[]{:S(2)}, u32[]{:S(2)}) async-start(bf16[32,8,128]{2,1,0:T(8,128)(2,1)} %get-tuple-element.42), calls=%async_computation | async-start | bytes 131072 | tf_op jit(solution)/shard_map/all_to_all | solution.py:338
  14.2 1.9 %copy.6.lat_ref = bf16[1280,576]{1,0:T(8,128)(2,1)S(1)} copy(bf16[1280,576]{0,1:T(8,128)(2,1)} %param.4) | data formatting | bytes 2949120 | tf_op args[0]
  16.1 1.3 shard_map.61.own_ref
  17.4 5.6 %all-to-all-done = bf16[32,8,128]{2,1,0:T(8,128)(2,1)S(1)} async-done(((bf16[32,8,128]{2,1,0:T(8,128)(2,1)}), bf16[32,8,128]{2,1,0:T(8,128)(2,1)S(1)}, u32[]{:S(2)}, u32[]{:S(2)}) %all-to-all-start) | async-done | bytes 65568 | tf_op jit(solution)/shard_map/all_to_all | solution.py:338
  24.2 3.9 %all-to-all-start.1 = ((bf16[32,8,1152]{2,1,0:T(8,128)(2,1)}), bf16[32,8,1152]{2,1,0:T(8,128)(2,1)S(1)}, u32[]{:S(2)}, u32[]{:S(2)}) async-start(bf16[32,8,1152]{2,1,0:T(8,128)(2,1)} %bitcast.4), calls=%async_computation.1 | async-start | bytes 1179648 | tf_op jit(solution)/shard_map/all_to_all | solution.py:338
  28.1 1.4 shard_map.60
  30.1 4.0 %collective-permute-start = (bf16[128,2304]{1,0:T(8,128)(2,1)S(1)}, bf16[128,2304]{1,0:T(8,128)(2,1)S(1)}, u32[]{:S(2)}, u32[]{:S(2)}) collective-permute-start(bf16[128,2304]{1,0:T(8,128)(2,1)S(1)} %copy-done.1), channel_id=1, source_target_pairs={{0,1},{1,0},{2,3},{3,2},{4,5},{5,4},{6,7},{7,6},{8,9},{9,8},{10,11... | collective-permute-start | bytes 1769480 | tf_op jit(solution)/shard_map/ppermute | solution.py:367
  34.1 1.9 %collective-permute-start.1 = (bf16[128,2048]{1,0:T(8,128)(2,1)}, bf16[128,2048]{1,0:T(8,128)(2,1)S(1)}, u32[]{:S(2)}, u32[]{:S(2)}) collective-permute-start(bf16[128,2048]{1,0:T(8,128)(2,1)} %g_ref), channel_id=1, source_target_pairs={{0,1},{1,0},{2,3},{3,2},{4,5},{5,4},{6,7},{7,6},{8,9},{9,8},{10,11... | collective-permute-start | bytes 1572872 | tf_op jit(solution)/shard_map/ppermute | solution.py:368
  36.1 7.9 %all-to-all-done.1 = bf16[32,8,1152]{2,1,0:T(8,128)(2,1)S(1)} async-done(((bf16[32,8,1152]{2,1,0:T(8,128)(2,1)}), bf16[32,8,1152]{2,1,0:T(8,128)(2,1)S(1)}, u32[]{:S(2)}, u32[]{:S(2)}) %all-to-all-start.1) | async-done | bytes 589856 | tf_op jit(solution)/shard_map/all_to_all | solution.py:338
  44.2 4.0 %collective-permute-start.2 = (bf16[144,1152]{1,0:T(8,128)(2,1)S(1)}, bf16[144,1152]{1,0:T(8,128)(2,1)S(1)}, u32[]{:S(2)}, u32[]{:S(2)}) collective-permute-start(bf16[144,1152]{1,0:T(8,128)(2,1)S(1)} %shard_map.63.own_ref), channel_id=1, source_target_pairs={{0,2},{1,3},{2,4},{3,5},{4,6},{5,7},{6,8},{7,9},{8,10},{9,11},{10,... | collective-permute-start | bytes 995336 | tf_op jit(solution)/shard_map/ppermute | solution.py:372
  48.3 8.6 %collective-permute-start.3 = (bf16[144,1152]{1,0:T(8,128)(2,1)S(1)}, bf16[144,1152]{1,0:T(8,128)(2,1)S(1)}, u32[]{:S(2)}, u32[]{:S(2)}) collective-permute-start(bf16[144,1152]{1,0:T(8,128)(2,1)S(1)} %shard_map.63.own_ref), channel_id=1, source_target_pairs={{0,14},{1,15},{2,0},{3,1},{4,2},{5,3},{6,4},{7,5},{8,6},{9,7},{10,... | collective-permute-start | bytes 995336 | tf_op jit(solution)/shard_map/ppermute | solution.py:373
  56.9 2.6 %collective-permute-done.2.below_ref = bf16[144,1152]{1,0:T(8,128)(2,1)S(1)} collective-permute-done((bf16[144,1152]{1,0:T(8,128)(2,1)S(1)}, bf16[144,1152]{1,0:T(8,128)(2,1)S(1)}, u32[]{:S(2)}, u32[]{:S(2)}) %collective-permute-start.2) | collective-permute-done | bytes 331808 | tf_op jit(solution)/shard_map/ppermute | solution.py:372
  59.4 1.5 %collective-permute-done.3.above_ref = bf16[144,1152]{1,0:T(8,128)(2,1)S(1)} collective-permute-done((bf16[144,1152]{1,0:T(8,128)(2,1)S(1)}, bf16[144,1152]{1,0:T(8,128)(2,1)S(1)}, u32[]{:S(2)}, u32[]{:S(2)}) %collective-permute-start.3) | collective-permute-done | bytes 331808 | tf_op jit(solution)/shard_map/ppermute | solution.py:373
  60.9 5.0 %collective-permute-start.4 = (bf16[144,1152]{1,0:T(8,128)(2,1)S(1)}, bf16[144,1152]{1,0:T(8,128)(2,1)S(1)}, u32[]{:S(2)}, u32[]{:S(2)}) collective-permute-start(bf16[144,1152]{1,0:T(8,128)(2,1)S(1)} %broadcast_select_fusion), channel_id=1, source_target_pairs={{0,2},{1,15},{2,4},{3,1},{4,6},{5,3},{6,8},{7,5},{8,10},{9,7},{10,... | collective-permute-start | bytes 995336 | tf_op jit(solution)/shard_map/ppermute | solution.py:375
  66.0 2.2 %shard_map.64 = (f32[288,1024]{1,0:T(8,128)S(1)}, f32[288,1024]{1,0:T(8,128)S(1)}, f32[8,1024]{1,0:T(8,128)S(1)}, bf16[288,576]{1,0:T(8,128)(2,1)S(1)}, bf16[102...) custom-call(bf16[144,1152]{1,0:T(8,128)(2,1)S(1)} %shard_map.63.own_ref, bf16[128,2304]{1,0:T(8,128)(2,1)S(1)} %copy-done.1, ...), custom_call_target="tpu_custom_call" | custom-call | flops 1000000000 | bytes 1000000 | tf_op jit(solution)/shard_map/pallas_call | solution.py:39
  68.9 2.1 %shard_map.65 = (f32[576,1024]{1,0:T(8,128)S(1)}, f32[576,1024]{1,0:T(8,128)S(1)}, f32[8,1024]{1,0:T(8,128)S(1)}, bf16[576,576]{1,0:T(8,128)(2,1)S(1)}) custom-call(bf16[144,1152]{1,0:T(8,128)(2,1)S(1)} %collective-permute-done.2.below_ref, bf16[144,1152]{1,0:T(8,128)(2,1)S(1)} %collective-permute-done.3.above_ref, ...), custom_call_target="tpu_custom_call" | custom-call | flops 2000000000 | bytes 1000000 | tf_op jit(solution)/shard_map/pallas_call | solution.py:39
  71.1 1.3 shard_map.66
  72.4 7.7 %collective-permute-start.5 = (f32[8,1024]{1,0:T(8,128)S(1)}, f32[8,1024]{1,0:T(8,128)S(1)}, u32[]{:S(2)}, u32[]{:S(2)}) collective-permute-start(f32[8,1024]{1,0:T(8,128)S(1)} %get-tuple-element.59.stat_ref), channel_id=1, source_target_pairs={{0,1},{1,0},{2,3},{3,2},{4,5},{5,4},{6,7},{7,6},{8,9},{9,8},{10,11... | collective-permute-start | bytes 98312 | tf_op jit(solution)/shard_map/ppermute | solution.py:431
  82.0 4.2 %collective-permute-start.9 = (bf16[144,1152]{1,0:T(8,128)(2,1)S(1)}, bf16[144,1152]{1,0:T(8,128)(2,1)S(1)}, u32[]{:S(2)}, u32[]{:S(2)}) collective-permute-start(bf16[144,1152]{1,0:T(8,128)(2,1)S(1)} %get-tuple-element.79), channel_id=1, source_target_pairs={{0,4},{1,13},{2,6},{3,15},{4,8},{5,1},{6,10},{7,3},{8,12},{9,5},{1... | collective-permute-start | bytes 995336 | tf_op jit(solution)/shard_map/ppermute | solution.py:450
  86.3 1.9 %shard_map.68 = (bf16[144,1152]{1,0:T(8,128)(2,1)S(1)}, bf16[144,1152]{1,0:T(8,128)(2,1)S(1)}, bf16[576,1024]{1,0:T(8,128)(2,1)S(1)}) custom-call(f32[576,1024]{1,0:T(8,128)S(1)} %get-tuple-element.62.e_ref, f32[576,1024]{1,0:T(8,128)S(1)} %get-tuple-element.63.d_ref, f32[8,1024]{1,0:T(8,128)S(1)} %get-tuple-element.59.stat_ref, ...), custom_call_target="tpu_custom_call" | custom-call | flops 2000000000 | bytes 1000000 | tf_op jit(solution)/shard_map/pallas_call | solution.py:39
  88.2 2.5 %collective-permute-start.7 = (bf16[144,1152]{1,0:T(8,128)(2,1)S(1)}, bf16[144,1152]{1,0:T(8,128)(2,1)S(1)}, u32[]{:S(2)}, u32[]{:S(2)}) collective-permute-start(bf16[144,1152]{1,0:T(8,128)(2,1)S(1)} %get-tuple-element.77), channel_id=1, source_target_pairs={{0,2},{1,3},{2,4},{3,5},{4,6},{5,7},{6,8},{7,9},{8,10},{9,11},{10,... | collective-permute-start | bytes 995336 | tf_op jit(solution)/shard_map/ppermute | solution.py:452
  90.7 4.2 %collective-permute-start.8 = (bf16[144,1152]{1,0:T(8,128)(2,1)S(1)}, bf16[144,1152]{1,0:T(8,128)(2,1)S(1)}, u32[]{:S(2)}, u32[]{:S(2)}) collective-permute-start(bf16[144,1152]{1,0:T(8,128)(2,1)S(1)} %get-tuple-element.78), channel_id=1, source_target_pairs={{0,14},{1,15},{2,0},{3,1},{4,2},{5,3},{6,4},{7,5},{8,6},{9,7},{10,... | collective-permute-start | bytes 995336 | tf_op jit(solution)/shard_map/ppermute | solution.py:453
  96.0 6.3 %collective-permute-done.7.up_ref = bf16[144,1152]{1,0:T(8,128)(2,1)S(1)} collective-permute-done((bf16[144,1152]{1,0:T(8,128)(2,1)S(1)}, bf16[144,1152]{1,0:T(8,128)(2,1)S(1)}, u32[]{:S(2)}, u32[]{:S(2)}) %collective-permute-start.7) | collective-permute-done | bytes 331808 | tf_op jit(solution)/shard_map/ppermute | solution.py:452
  102.4 1.2 shard_map.72
  103.6 5.2 %all-to-all-start.2 = ((bf16[32,8,1152]{2,1,0:T(8,128)(2,1)}), bf16[32,8,1152]{2,1,0:T(8,128)(2,1)S(1)}, u32[]{:S(2)}, u32[]{:S(2)}) async-start(bf16[32,8,1152]{2,1,0:T(8,128)(2,1)} %bitcast.6), calls=%async_computation.2 | async-start | bytes 1179648 | tf_op jit(solution)/shard_map/all_to_all | solution.py:338
  108.8 1.3 copy-done.3
  112.2 4.0 %shard_map.70 = (f32[256,1152]{1,0:T(8,128)S(1)}, f32[256,1152]{1,0:T(8,128)}) custom-call(bf16[288,1024]{1,0:T(8,128)(2,1)S(1)} %get-tuple-element.61.ds0_ref, bf16[576,1024]{1,0:T(8,128)(2,1)S(1)} %copy-done.3, bf16[288,1024]{1,0:T(8,128)(2,1)S(1)} %get-tuple-element.67.ds2_ref, bf16[288,576]{1,0:T(8,128)(2,1)S(1)} %copy-done.5, ...), custom_call_target="tpu_custom_call" | custom-call | flops 3000000000 | bytes 10000000 | tf_op jit(solution)/shard_map/pallas_call | solution.py:39
  116.2 2.8 %collective-permute-start.6 = (f32[256,1152]{1,0:T(8,128)}, f32[256,1152]{1,0:T(8,128)S(1)}, u32[]{:S(2)}, u32[]{:S(2)}) collective-permute-start(f32[256,1152]{1,0:T(8,128)} %get-tuple-element.72), channel_id=1, source_target_pairs={{0,1},{1,0},{2,3},{3,2},{4,5},{5,4},{6,7},{7,6},{8,9},{9,8},{10,11... | collective-permute-start | bytes 3538952 | tf_op jit(solution)/shard_map/ppermute | solution.py:468
  119.0 7.4 %all-to-all-done.2 = bf16[32,8,1152]{2,1,0:T(8,128)(2,1)S(1)} async-done(((bf16[32,8,1152]{2,1,0:T(8,128)(2,1)}), bf16[32,8,1152]{2,1,0:T(8,128)(2,1)S(1)}, u32[]{:S(2)}, u32[]{:S(2)}) %all-to-all-start.2) | async-done | bytes 589856 | tf_op jit(solution)/shard_map/all_to_all | solution.py:338
  127.4 6.7 %all-to-all-start.3 = ((bf16[16,8,1152]{2,1,0:T(8,128)(2,1)}), bf16[16,8,1152]{2,1,0:T(8,128)(2,1)S(1)}, u32[]{:S(2)}, u32[]{:S(2)}) async-start(bf16[16,8,1152]{2,1,0:T(8,128)(2,1)} %bitcast.8), calls=%async_computation.3 | async-start | bytes 589824 | tf_op jit(solution)/shard_map/all_to_all | solution.py:338
  135.1 11.4 %all-to-all-done.3 = bf16[16,8,1152]{2,1,0:T(8,128)(2,1)S(1)} async-done(((bf16[16,8,1152]{2,1,0:T(8,128)(2,1)}), bf16[16,8,1152]{2,1,0:T(8,128)(2,1)S(1)}, u32[]{:S(2)}, u32[]{:S(2)}) %all-to-all-start.3) | async-done | bytes 294944 | tf_op jit(solution)/shard_map/all_to_all | solution.py:338
  (35 shorter events, 11.8 us)
Async XLA Ops:
  0.6 0.7 copy-start
  3.7 19.3 %all-to-all-start = ((bf16[32,8,128]{2,1,0:T(8,128)(2,1)}), bf16[32,8,128]{2,1,0:T(8,128)(2,1)S(1)}, u32[]{:S(2)}, u32[]{:S(2)}) async-start(bf16[32,8,128]{2,1,0:T(8,128)(2,1)} %get-tuple-element.42), calls=%async_computation | async-start | bytes 131072 | tf_op jit(solution)/shard_map/all_to_all | solution.py:338
  24.2 19.8 %all-to-all-start.1 = ((bf16[32,8,1152]{2,1,0:T(8,128)(2,1)}), bf16[32,8,1152]{2,1,0:T(8,128)(2,1)S(1)}, u32[]{:S(2)}, u32[]{:S(2)}) async-start(bf16[32,8,1152]{2,1,0:T(8,128)(2,1)} %bitcast.4), calls=%async_computation.1 | async-start | bytes 1179648 | tf_op jit(solution)/shard_map/all_to_all | solution.py:338
  28.1 2.1 %copy-start.1 = (bf16[128,2304]{1,0:T(8,128)(2,1)S(1)}, bf16[128,2304]{1,0:T(8,128)(2,1)}, u32[]{:S(2)}) copy-start(bf16[128,2304]{1,0:T(8,128)(2,1)} %q_ref) | copy-start | bytes 1769476
  29.5 0.7 copy-start.6
  30.1 14.1 %collective-permute-start = (bf16[128,2304]{1,0:T(8,128)(2,1)S(1)}, bf16[128,2304]{1,0:T(8,128)(2,1)S(1)}, u32[]{:S(2)}, u32[]{:S(2)}) collective-permute-start(bf16[128,2304]{1,0:T(8,128)(2,1)S(1)} %copy-done.1), channel_id=1, source_target_pairs={{0,1},{1,0},{2,3},{3,2},{4,5},{5,4},{6,7},{7,6},{8,9},{9,8},{10,11... | collective-permute-start | bytes 1769480 | tf_op jit(solution)/shard_map/ppermute | solution.py:367
  34.1 10.1 %collective-permute-start.1 = (bf16[128,2048]{1,0:T(8,128)(2,1)}, bf16[128,2048]{1,0:T(8,128)(2,1)S(1)}, u32[]{:S(2)}, u32[]{:S(2)}) collective-permute-start(bf16[128,2048]{1,0:T(8,128)(2,1)} %g_ref), channel_id=1, source_target_pairs={{0,1},{1,0},{2,3},{3,2},{4,5},{5,4},{6,7},{7,6},{8,9},{9,8},{10,11... | collective-permute-start | bytes 1572872 | tf_op jit(solution)/shard_map/ppermute | solution.py:368
  44.2 15.2 %collective-permute-start.2 = (bf16[144,1152]{1,0:T(8,128)(2,1)S(1)}, bf16[144,1152]{1,0:T(8,128)(2,1)S(1)}, u32[]{:S(2)}, u32[]{:S(2)}) collective-permute-start(bf16[144,1152]{1,0:T(8,128)(2,1)S(1)} %shard_map.63.own_ref), channel_id=1, source_target_pairs={{0,2},{1,3},{2,4},{3,5},{4,6},{5,7},{6,8},{7,9},{8,10},{9,11},{10,... | collective-permute-start | bytes 995336 | tf_op jit(solution)/shard_map/ppermute | solution.py:372
  48.3 12.6 %collective-permute-start.3 = (bf16[144,1152]{1,0:T(8,128)(2,1)S(1)}, bf16[144,1152]{1,0:T(8,128)(2,1)S(1)}, u32[]{:S(2)}, u32[]{:S(2)}) collective-permute-start(bf16[144,1152]{1,0:T(8,128)(2,1)S(1)} %shard_map.63.own_ref), channel_id=1, source_target_pairs={{0,14},{1,15},{2,0},{3,1},{4,2},{5,3},{6,4},{7,5},{8,6},{9,7},{10,... | collective-permute-start | bytes 995336 | tf_op jit(solution)/shard_map/ppermute | solution.py:373
  60.9 10.1 %collective-permute-start.4 = (bf16[144,1152]{1,0:T(8,128)(2,1)S(1)}, bf16[144,1152]{1,0:T(8,128)(2,1)S(1)}, u32[]{:S(2)}, u32[]{:S(2)}) collective-permute-start(bf16[144,1152]{1,0:T(8,128)(2,1)S(1)} %broadcast_select_fusion), channel_id=1, source_target_pairs={{0,2},{1,15},{2,4},{3,1},{4,6},{5,3},{6,8},{7,5},{8,10},{9,7},{10,... | collective-permute-start | bytes 995336 | tf_op jit(solution)/shard_map/ppermute | solution.py:375
  68.1 0.7 copy-start.4
  68.9 2.2 %copy-start.7 = (f32[288,128]{1,0:T(8,128)S(1)}, f32[288,128]{1,0:T(8,128)}, u32[]{:S(2)}) copy-start(f32[288,128]{1,0:T(8,128)} %copy-done.6) | copy-start | bytes 442372
  71.0 1.4 copy-start.8
  72.4 8.5 %collective-permute-start.5 = (f32[8,1024]{1,0:T(8,128)S(1)}, f32[8,1024]{1,0:T(8,128)S(1)}, u32[]{:S(2)}, u32[]{:S(2)}) collective-permute-start(f32[8,1024]{1,0:T(8,128)S(1)} %get-tuple-element.59.stat_ref), channel_id=1, source_target_pairs={{0,1},{1,0},{2,3},{3,2},{4,5},{5,4},{6,7},{7,6},{8,9},{9,8},{10,11... | collective-permute-start | bytes 98312 | tf_op jit(solution)/shard_map/ppermute | solution.py:431
  82.0 14.0 %collective-permute-start.9 = (bf16[144,1152]{1,0:T(8,128)(2,1)S(1)}, bf16[144,1152]{1,0:T(8,128)(2,1)S(1)}, u32[]{:S(2)}, u32[]{:S(2)}) collective-permute-start(bf16[144,1152]{1,0:T(8,128)(2,1)S(1)} %get-tuple-element.79), channel_id=1, source_target_pairs={{0,4},{1,13},{2,6},{3,15},{4,8},{5,1},{6,10},{7,3},{8,12},{9,5},{1... | collective-permute-start | bytes 995336 | tf_op jit(solution)/shard_map/ppermute | solution.py:450
  88.2 7.8 %copy-start.2 = (bf16[576,1024]{1,0:T(8,128)(2,1)}, bf16[576,1024]{1,0:T(8,128)(2,1)S(1)}, u32[]{:S(2)}) copy-start(bf16[576,1024]{1,0:T(8,128)(2,1)S(1)} %get-tuple-element.64.ds1_ref) | copy-start | bytes 3538948
  88.2 14.2 %collective-permute-start.7 = (bf16[144,1152]{1,0:T(8,128)(2,1)S(1)}, bf16[144,1152]{1,0:T(8,128)(2,1)S(1)}, u32[]{:S(2)}, u32[]{:S(2)}) collective-permute-start(bf16[144,1152]{1,0:T(8,128)(2,1)S(1)} %get-tuple-element.77), channel_id=1, source_target_pairs={{0,2},{1,3},{2,4},{3,5},{4,6},{5,7},{6,8},{7,9},{8,10},{9,11},{10,... | collective-permute-start | bytes 995336 | tf_op jit(solution)/shard_map/ppermute | solution.py:452
  90.7 11.7 %collective-permute-start.8 = (bf16[144,1152]{1,0:T(8,128)(2,1)S(1)}, bf16[144,1152]{1,0:T(8,128)(2,1)S(1)}, u32[]{:S(2)}, u32[]{:S(2)}) collective-permute-start(bf16[144,1152]{1,0:T(8,128)(2,1)S(1)} %get-tuple-element.78), channel_id=1, source_target_pairs={{0,14},{1,15},{2,0},{3,1},{4,2},{5,3},{6,4},{7,5},{8,6},{9,7},{10,... | collective-permute-start | bytes 995336 | tf_op jit(solution)/shard_map/ppermute | solution.py:453
  103.6 22.8 %all-to-all-start.2 = ((bf16[32,8,1152]{2,1,0:T(8,128)(2,1)}), bf16[32,8,1152]{2,1,0:T(8,128)(2,1)S(1)}, u32[]{:S(2)}, u32[]{:S(2)}) async-start(bf16[32,8,1152]{2,1,0:T(8,128)(2,1)} %bitcast.6), calls=%async_computation.2 | async-start | bytes 1179648 | tf_op jit(solution)/shard_map/all_to_all | solution.py:338
  108.8 1.3 copy-start.3
  110.1 1.0 copy-start.5
  111.1 1.1 copy-start.9
  116.2 17.9 %collective-permute-start.6 = (f32[256,1152]{1,0:T(8,128)}, f32[256,1152]{1,0:T(8,128)S(1)}, u32[]{:S(2)}, u32[]{:S(2)}) collective-permute-start(f32[256,1152]{1,0:T(8,128)} %get-tuple-element.72), channel_id=1, source_target_pairs={{0,1},{1,0},{2,3},{3,2},{4,5},{5,4},{6,7},{7,6},{8,9},{9,8},{10,11... | collective-permute-start | bytes 3538952 | tf_op jit(solution)/shard_map/ppermute | solution.py:468
  127.4 19.1 %all-to-all-start.3 = ((bf16[16,8,1152]{2,1,0:T(8,128)(2,1)}), bf16[16,8,1152]{2,1,0:T(8,128)(2,1)S(1)}, u32[]{:S(2)}, u32[]{:S(2)}) async-start(bf16[16,8,1152]{2,1,0:T(8,128)(2,1)} %bitcast.8), calls=%async_computation.3 | async-start | bytes 589824 | tf_op jit(solution)/shard_map/all_to_all | solution.py:338

commit v8 on v7

--- a/solution.py
+++ b/solution.py
@@ -81,20 +81,20 @@
     return one_hot(least == 0)
 
 
-def choose(picks_ref, hit_ref, ask_ref, *, per_owner):
-    blocks, queries = hit_ref.shape
-    hit = hits(picks_ref, blocks)
-    hit_ref[...] = hit
-    count = dot(hit, jnp.ones((queries, 128), bf16), 1, 0)
-    row, lane = iota((blocks, 128), 0), iota((blocks, 128), 1)
-    owner = by20(row)
-    placed = one_hot(jnp.logical_and(count > 0.5, lane == row - owner * per_owner))
+def choose(picks_ref, ask_ref, *, per_owner):
+    picks, queries = picks_ref.shape
     owners = ask_ref.shape[0]
-    member = one_hot(by20(iota((owners, blocks), 1)) == iota((owners, blocks), 0))
-    table = dot(member, placed, 1, 0)
-    before = one_hot(iota((128, 128), 0) < iota((128, 128), 1))
+    pick = picks_ref[...]
+    owner = by20(pick)
+    place = pick - owner * per_owner
+    row = iota((owners, queries), 0)
+    by_owner = [one_hot(owner[k : k + 1, :] == row) for k in range(picks)]
+    by_place = [one_hot(place[k : k + 1, :] == row) for k in range(picks)]
+    count = dot(jnp.concatenate(by_owner, axis=1), jnp.concatenate(by_place, axis=1), 1, 1)
+    table = jnp.where(count > 0.5, 1.0, 0.0)
+    before = one_hot(iota((owners, owners), 0) < iota((owners, owners), 1))
     rank = dot(table.astype(bf16), before, 1, 0)
-    lane = iota((owners, 128), 1).astype(f32)
+    lane = iota((owners, owners), 1).astype(f32)
     ids = []
     for k in range(CAP):
         here = jnp.logical_and(table > 0.5, rank == k)
@@ -112,13 +112,14 @@
 
 
 def arrange(
-    pos_ref, hit_ref, ask_ref, bias_ref, near_ref, far_ref, send_ref, back_ref, sum_ref, place_ref,
-    *, first, per_dest, per_owner,
+    pos_ref, picks_ref, ask_ref, bias_ref, near_ref, far_ref, send_ref, back_ref, sum_ref, place_ref,
+    *, first, per_dest, per_owner, blocks,
 ):
-    blocks, queries = hit_ref.shape
+    queries = picks_ref.shape[1]
+    hit = hits(picks_ref, blocks)
     rows, slots = send_ref.shape
     head = pos_ref[1]
-    count = dot(jnp.ones((8, queries), bf16), hit_ref[...], 1, 1)
+    count = dot(jnp.ones((8, queries), bf16), hit, 1, 1)
     chosen8 = one_hot(count > 0.5)
     chosen = count[:1]
     lo, hi = iota((blocks, blocks), 0), iota((blocks, blocks), 1)
@@ -132,7 +133,7 @@
     block_rank = jnp.sum(here * rank, axis=1, keepdims=True)
     block_id = block_id.astype(jnp.int32)
     block_rank = block_rank.astype(jnp.int32)
-    picked = dot(here.astype(bf16), hit_ref[...], 1, 0)
+    picked = dot(here.astype(bf16), hit, 1, 0)
     query_pos = first + pos_ref[0] * queries + iota((rows, queries), 1)
     base = block_id * BLOCK + (iota((rows, queries), 0) & 3) - query_pos
     for i, step in enumerate((0, -1, 1, 2)):
@@ -337,17 +338,18 @@
         x3 = x.reshape(n, -1, x.shape[1])
         return lax.all_to_all(x3, axis, split_axis=0, concat_axis=0, tiled=True).reshape(x.shape)
 
-    hit, ask = call(
+    picks = picks.T
+    ask = call(
         functools.partial(choose, per_owner=per_owner),
-        (shape((blocks, queries), bf16), shape((n_ctx, CAP * LINES, 128), bf16)),
-        picks.T,
+        shape((n_ctx, CAP * LINES, 128), bf16),
+        picks,
     )
     ask = ask.reshape(slots, 128)
     own = call(own_part, shape((per_owner * LINES, line), bf16), pos, latent, flops=10**9, traffic=10**6)
     asked = swap(ask, "ctx")
     lines_out = call(fetch, shape((slots, line), bf16), asked, own)
     bias, near_bias, far_bias, send, back, sums, places = call(
-        functools.partial(arrange, first=first, per_dest=outs // PART, per_owner=per_owner),
+        functools.partial(arrange, first=first, per_dest=outs // PART, per_owner=per_owner, blocks=blocks),
         (
             shape((piece_rows, queries), f32),
             shape((2 * piece_rows, queries), f32),
@@ -358,7 +360,7 @@
             shape((2 * outs, n_head * CAP * LINES), bf16),
         ),
         pos,
-        hit,
+        picks,
         asked,
         flops=3 * 10**9,
         traffic=3 * 10**6,

time: 148 us -> 147 us (level)
    unnamed x21 -> x23, local copies, waits for them, and re-layouts: 7.38 us -> 7.38 us
  transfers between devices with their start and end apart: 14 -> 14, of which waited for: 8 -> 8; matrix products, arithmetic and copies ran while one was open for 1% -> 1% of each run, Pallas kernels for 11% -> 12%
where the time goes in v8:
time: 147 us; the launch traced here: 146 us
  starting transfers between devices  71.2 us (48%)
  waiting for transfers between devices  42.3 us (29%)
  Pallas kernels  24.2 us (16%)
  local copies, waits for them, and re-layouts  7.38 us (5%)
    all_to_all x4, waiting for transfers between devices, swap(): lax.all_to_all(x3, axis, split_axis=0, concat_axis=0, tiled=True)  31.1 us
    all_to_all x4, starting transfers between devices, swap(): lax.all_to_all(x3, axis, split_axis=0, concat_axis=0, tiled=True)  26.3 us
    pallas_call x16, Pallas kernels, call(): pl.pallas_call(body, out_shape=out_shape, in_specs=specs, out_specs=jax.t...  24.2 us
    ppermute x1, starting transfers between devices, local(): from_above = lax.ppermute(mine, 'head', down)  8.6 us
    ppermute x1, starting transfers between devices, local(): twin_stats = lax.ppermute(stats, 'head', twin)  7.65 us
    unnamed x23, local copies, waits for them, and re-layouts  7.38 us
    ppermute x1, waiting for transfers between devices, local(): sum_up = lax.ppermute(to_up, 'head', up)  6.33 us
    ppermute x1, starting transfers between devices, local(): from_far = lax.ppermute(onward, 'head', relay)  5.02 us
  transfers between devices with their start and end apart: 14, of which 8 were waited for; matrix products, arithmetic and copies ran while one was open for 1% of the time, Pallas kernels for 12%

profile of v8, /device:TPU:1, one launch (start us, length us, event | category | flops | bytes accessed | tf_op | source)
XLA Modules:
  0.0 146.2 jit_solution(7105781518106678812)
XLA Ops:
  2.4 10.5 %all-to-all-start = ((bf16[32,8,128]{2,1,0:T(8,128)(2,1)}), bf16[32,8,128]{2,1,0:T(8,128)(2,1)S(1)}, u32[]{:S(2)}, u32[]{:S(2)}) async-start(bf16[32,8,128]{2,1,0:T(8,128)(2,1)} %shard_map.59), calls=%async_computation | async-start | bytes 131072 | tf_op jit(solution)/shard_map/all_to_all | solution.py:339
  13.0 1.9 %copy.6.lat_ref = bf16[1280,576]{1,0:T(8,128)(2,1)S(1)} copy(bf16[1280,576]{0,1:T(8,128)(2,1)} %param.4) | data formatting | bytes 2949120 | tf_op args[0]
  14.9 1.3 shard_map.61.own_ref
  16.2 5.6 %all-to-all-done = bf16[32,8,128]{2,1,0:T(8,128)(2,1)S(1)} async-done(((bf16[32,8,128]{2,1,0:T(8,128)(2,1)}), bf16[32,8,128]{2,1,0:T(8,128)(2,1)S(1)}, u32[]{:S(2)}, u32[]{:S(2)}) %all-to-all-start) | async-done | bytes 65568 | tf_op jit(solution)/shard_map/all_to_all | solution.py:339
  21.7 1.2 shard_map.62
  22.9 3.9 %all-to-all-start.1 = ((bf16[32,8,1152]{2,1,0:T(8,128)(2,1)}), bf16[32,8,1152]{2,1,0:T(8,128)(2,1)S(1)}, u32[]{:S(2)}, u32[]{:S(2)}) async-start(bf16[32,8,1152]{2,1,0:T(8,128)(2,1)} %bitcast.4), calls=%async_computation.1 | async-start | bytes 1179648 | tf_op jit(solution)/shard_map/all_to_all | solution.py:339
  26.8 2.5 %shard_map.60 = (f32[288,128]{1,0:T(8,128)S(1)}, f32[576,128]{1,0:T(8,128)S(1)}, f32[288,128]{1,0:T(8,128)S(1)}, bf16[144,256]{1,0:T(8,128)(2,1)S(1)}, bf16[256,...) custom-call(s32[2]{0:T(128)S(1)} %pad_add_fusion.pos_ref, s32[32,128]{1,0:T(8,128)S(1)} %bitcast.16, ...), custom_call_target="tpu_custom_call" | custom-call | flops 3000000000 | bytes 3000000 | tf_op jit(solution)/shard_map/pallas_call | solution.py:39
  30.0 4.0 %collective-permute-start = (bf16[128,2304]{1,0:T(8,128)(2,1)S(1)}, bf16[128,2304]{1,0:T(8,128)(2,1)S(1)}, u32[]{:S(2)}, u32[]{:S(2)}) collective-permute-start(bf16[128,2304]{1,0:T(8,128)(2,1)S(1)} %copy-done.2), channel_id=1, source_target_pairs={{0,1},{1,0},{2,3},{3,2},{4,5},{5,4},{6,7},{7,6},{8,9},{9,8},{10,11... | collective-permute-start | bytes 1769480 | tf_op jit(solution)/shard_map/ppermute | solution.py:369
  34.0 1.9 %collective-permute-start.1 = (bf16[128,2048]{1,0:T(8,128)(2,1)}, bf16[128,2048]{1,0:T(8,128)(2,1)S(1)}, u32[]{:S(2)}, u32[]{:S(2)}) collective-permute-start(bf16[128,2048]{1,0:T(8,128)(2,1)} %g_ref), channel_id=1, source_target_pairs={{0,1},{1,0},{2,3},{3,2},{4,5},{5,4},{6,7},{7,6},{8,9},{9,8},{10,11... | collective-permute-start | bytes 1572872 | tf_op jit(solution)/shard_map/ppermute | solution.py:370
  36.0 6.8 %all-to-all-done.1 = bf16[32,8,1152]{2,1,0:T(8,128)(2,1)S(1)} async-done(((bf16[32,8,1152]{2,1,0:T(8,128)(2,1)}), bf16[32,8,1152]{2,1,0:T(8,128)(2,1)S(1)}, u32[]{:S(2)}, u32[]{:S(2)}) %all-to-all-start.1) | async-done | bytes 589856 | tf_op jit(solution)/shard_map/all_to_all | solution.py:339
  43.0 4.0 %collective-permute-start.2 = (bf16[144,1152]{1,0:T(8,128)(2,1)S(1)}, bf16[144,1152]{1,0:T(8,128)(2,1)S(1)}, u32[]{:S(2)}, u32[]{:S(2)}) collective-permute-start(bf16[144,1152]{1,0:T(8,128)(2,1)S(1)} %shard_map.63.own_ref), channel_id=1, source_target_pairs={{0,2},{1,3},{2,4},{3,5},{4,6},{5,7},{6,8},{7,9},{8,10},{9,11},{10,... | collective-permute-start | bytes 995336 | tf_op jit(solution)/shard_map/ppermute | solution.py:374
  47.0 8.6 %collective-permute-start.3 = (bf16[144,1152]{1,0:T(8,128)(2,1)S(1)}, bf16[144,1152]{1,0:T(8,128)(2,1)S(1)}, u32[]{:S(2)}, u32[]{:S(2)}) collective-permute-start(bf16[144,1152]{1,0:T(8,128)(2,1)S(1)} %shard_map.63.own_ref), channel_id=1, source_target_pairs={{0,14},{1,15},{2,0},{3,1},{4,2},{5,3},{6,4},{7,5},{8,6},{9,7},{10,... | collective-permute-start | bytes 995336 | tf_op jit(solution)/shard_map/ppermute | solution.py:375
  55.6 2.6 %collective-permute-done.2.below_ref = bf16[144,1152]{1,0:T(8,128)(2,1)S(1)} collective-permute-done((bf16[144,1152]{1,0:T(8,128)(2,1)S(1)}, bf16[144,1152]{1,0:T(8,128)(2,1)S(1)}, u32[]{:S(2)}, u32[]{:S(2)}) %collective-permute-start.2) | collective-permute-done | bytes 331808 | tf_op jit(solution)/shard_map/ppermute | solution.py:374
  58.2 1.5 %collective-permute-done.3.above_ref = bf16[144,1152]{1,0:T(8,128)(2,1)S(1)} collective-permute-done((bf16[144,1152]{1,0:T(8,128)(2,1)S(1)}, bf16[144,1152]{1,0:T(8,128)(2,1)S(1)}, u32[]{:S(2)}, u32[]{:S(2)}) %collective-permute-start.3) | collective-permute-done | bytes 331808 | tf_op jit(solution)/shard_map/ppermute | solution.py:375
  59.7 5.0 %collective-permute-start.4 = (bf16[144,1152]{1,0:T(8,128)(2,1)S(1)}, bf16[144,1152]{1,0:T(8,128)(2,1)S(1)}, u32[]{:S(2)}, u32[]{:S(2)}) collective-permute-start(bf16[144,1152]{1,0:T(8,128)(2,1)S(1)} %broadcast_select_fusion), channel_id=1, source_target_pairs={{0,2},{1,15},{2,4},{3,1},{4,6},{5,3},{6,8},{7,5},{8,10},{9,7},{10,... | collective-permute-start | bytes 995336 | tf_op jit(solution)/shard_map/ppermute | solution.py:377
  64.7 2.2 %shard_map.64 = (f32[288,1024]{1,0:T(8,128)S(1)}, f32[288,1024]{1,0:T(8,128)S(1)}, f32[8,1024]{1,0:T(8,128)S(1)}, bf16[288,576]{1,0:T(8,128)(2,1)S(1)}, bf16[102...) custom-call(bf16[144,1152]{1,0:T(8,128)(2,1)S(1)} %shard_map.63.own_ref, bf16[128,2304]{1,0:T(8,128)(2,1)S(1)} %copy-done.2, ...), custom_call_target="tpu_custom_call" | custom-call | flops 1000000000 | bytes 1000000 | tf_op jit(solution)/shard_map/pallas_call | solution.py:39
  67.7 2.1 %shard_map.65 = (f32[576,1024]{1,0:T(8,128)S(1)}, f32[576,1024]{1,0:T(8,128)S(1)}, f32[8,1024]{1,0:T(8,128)S(1)}, bf16[576,576]{1,0:T(8,128)(2,1)S(1)}) custom-call(bf16[144,1152]{1,0:T(8,128)(2,1)S(1)} %collective-permute-done.2.below_ref, bf16[144,1152]{1,0:T(8,128)(2,1)S(1)} %collective-permute-done.3.above_ref, ...), custom_call_target="tpu_custom_call" | custom-call | flops 2000000000 | bytes 1000000 | tf_op jit(solution)/shard_map/pallas_call | solution.py:39
  69.8 1.3 shard_map.66
  71.2 7.7 %collective-permute-start.5 = (f32[8,1024]{1,0:T(8,128)S(1)}, f32[8,1024]{1,0:T(8,128)S(1)}, u32[]{:S(2)}, u32[]{:S(2)}) collective-permute-start(f32[8,1024]{1,0:T(8,128)S(1)} %get-tuple-element.55.stat_ref), channel_id=1, source_target_pairs={{0,1},{1,0},{2,3},{3,2},{4,5},{5,4},{6,7},{7,6},{8,9},{9,8},{10,11... | collective-permute-start | bytes 98312 | tf_op jit(solution)/shard_map/ppermute | solution.py:433
  80.8 4.2 %collective-permute-start.9 = (bf16[144,1152]{1,0:T(8,128)(2,1)S(1)}, bf16[144,1152]{1,0:T(8,128)(2,1)S(1)}, u32[]{:S(2)}, u32[]{:S(2)}) collective-permute-start(bf16[144,1152]{1,0:T(8,128)(2,1)S(1)} %get-tuple-element.75), channel_id=1, source_target_pairs={{0,4},{1,13},{2,6},{3,15},{4,8},{5,1},{6,10},{7,3},{8,12},{9,5},{1... | collective-permute-start | bytes 995336 | tf_op jit(solution)/shard_map/ppermute | solution.py:452
  85.0 1.9 %shard_map.68 = (bf16[144,1152]{1,0:T(8,128)(2,1)S(1)}, bf16[144,1152]{1,0:T(8,128)(2,1)S(1)}, bf16[576,1024]{1,0:T(8,128)(2,1)S(1)}) custom-call(f32[576,1024]{1,0:T(8,128)S(1)} %get-tuple-element.58.e_ref, f32[576,1024]{1,0:T(8,128)S(1)} %get-tuple-element.59.d_ref, f32[8,1024]{1,0:T(8,128)S(1)} %get-tuple-element.55.stat_ref, ...), custom_call_target="tpu_custom_call" | custom-call | flops 2000000000 | bytes 1000000 | tf_op jit(solution)/shard_map/pallas_call | solution.py:39
  87.0 2.5 %collective-permute-start.7 = (bf16[144,1152]{1,0:T(8,128)(2,1)S(1)}, bf16[144,1152]{1,0:T(8,128)(2,1)S(1)}, u32[]{:S(2)}, u32[]{:S(2)}) collective-permute-start(bf16[144,1152]{1,0:T(8,128)(2,1)S(1)} %get-tuple-element.73), channel_id=1, source_target_pairs={{0,2},{1,3},{2,4},{3,5},{4,6},{5,7},{6,8},{7,9},{8,10},{9,11},{10,... | collective-permute-start | bytes 995336 | tf_op jit(solution)/shard_map/ppermute | solution.py:454
  89.5 4.2 %collective-permute-start.8 = (bf16[144,1152]{1,0:T(8,128)(2,1)S(1)}, bf16[144,1152]{1,0:T(8,128)(2,1)S(1)}, u32[]{:S(2)}, u32[]{:S(2)}) collective-permute-start(bf16[144,1152]{1,0:T(8,128)(2,1)S(1)} %get-tuple-element.74), channel_id=1, source_target_pairs={{0,14},{1,15},{2,0},{3,1},{4,2},{5,3},{6,4},{7,5},{8,6},{9,7},{10,... | collective-permute-start | bytes 995336 | tf_op jit(solution)/shard_map/ppermute | solution.py:455
  94.8 6.3 %collective-permute-done.7.up_ref = bf16[144,1152]{1,0:T(8,128)(2,1)S(1)} collective-permute-done((bf16[144,1152]{1,0:T(8,128)(2,1)S(1)}, bf16[144,1152]{1,0:T(8,128)(2,1)S(1)}, u32[]{:S(2)}, u32[]{:S(2)}) %collective-permute-start.7) | collective-permute-done | bytes 331808 | tf_op jit(solution)/shard_map/ppermute | solution.py:454
  101.1 1.2 shard_map.72
  102.4 5.2 %all-to-all-start.2 = ((bf16[32,8,1152]{2,1,0:T(8,128)(2,1)}), bf16[32,8,1152]{2,1,0:T(8,128)(2,1)S(1)}, u32[]{:S(2)}, u32[]{:S(2)}) async-start(bf16[32,8,1152]{2,1,0:T(8,128)(2,1)} %bitcast.6), calls=%async_computation.2 | async-start | bytes 1179648 | tf_op jit(solution)/shard_map/all_to_all | solution.py:339
  107.6 1.3 copy-done.4
  110.9 4.0 %shard_map.70 = (f32[256,1152]{1,0:T(8,128)S(1)}, f32[256,1152]{1,0:T(8,128)}) custom-call(bf16[288,1024]{1,0:T(8,128)(2,1)S(1)} %get-tuple-element.57.ds0_ref, bf16[576,1024]{1,0:T(8,128)(2,1)S(1)} %copy-done.4, bf16[288,1024]{1,0:T(8,128)(2,1)S(1)} %get-tuple-element.63.ds2_ref, bf16[288,576]{1,0:T(8,128)(2,1)S(1)} %copy-done.6, ...), custom_call_target="tpu_custom_call" | custom-call | flops 3000000000 | bytes 10000000 | tf_op jit(solution)/shard_map/pallas_call | solution.py:39
  115.0 2.8 %collective-permute-start.6 = (f32[256,1152]{1,0:T(8,128)}, f32[256,1152]{1,0:T(8,128)S(1)}, u32[]{:S(2)}, u32[]{:S(2)}) collective-permute-start(f32[256,1152]{1,0:T(8,128)} %get-tuple-element.68), channel_id=1, source_target_pairs={{0,1},{1,0},{2,3},{3,2},{4,5},{5,4},{6,7},{7,6},{8,9},{9,8},{10,11... | collective-permute-start | bytes 3538952 | tf_op jit(solution)/shard_map/ppermute | solution.py:470
  117.7 7.4 %all-to-all-done.2 = bf16[32,8,1152]{2,1,0:T(8,128)(2,1)S(1)} async-done(((bf16[32,8,1152]{2,1,0:T(8,128)(2,1)}), bf16[32,8,1152]{2,1,0:T(8,128)(2,1)S(1)}, u32[]{:S(2)}, u32[]{:S(2)}) %all-to-all-start.2) | async-done | bytes 589856 | tf_op jit(solution)/shard_map/all_to_all | solution.py:339
  126.1 6.8 %all-to-all-start.3 = ((bf16[16,8,1152]{2,1,0:T(8,128)(2,1)}), bf16[16,8,1152]{2,1,0:T(8,128)(2,1)S(1)}, u32[]{:S(2)}, u32[]{:S(2)}) async-start(bf16[16,8,1152]{2,1,0:T(8,128)(2,1)} %bitcast.8), calls=%async_computation.3 | async-start | bytes 589824 | tf_op jit(solution)/shard_map/all_to_all | solution.py:339
  133.9 11.4 %all-to-all-done.3 = bf16[16,8,1152]{2,1,0:T(8,128)(2,1)S(1)} async-done(((bf16[16,8,1152]{2,1,0:T(8,128)(2,1)}), bf16[16,8,1152]{2,1,0:T(8,128)(2,1)S(1)}, u32[]{:S(2)}, u32[]{:S(2)}) %all-to-all-start.3) | async-done | bytes 294944 | tf_op jit(solution)/shard_map/all_to_all | solution.py:339
  (37 shorter events, 11.7 us)
Async XLA Ops:
  0.6 0.7 copy-start
  2.4 19.3 %all-to-all-start = ((bf16[32,8,128]{2,1,0:T(8,128)(2,1)}), bf16[32,8,128]{2,1,0:T(8,128)(2,1)S(1)}, u32[]{:S(2)}, u32[]{:S(2)}) async-start(bf16[32,8,128]{2,1,0:T(8,128)(2,1)} %shard_map.59), calls=%async_computation | async-start | bytes 131072 | tf_op jit(solution)/shard_map/all_to_all | solution.py:339
  16.2 10.7 %copy-start.1 = (s32[128,32]{0,1:T(8,128)S(1)}, s32[128,32]{0,1:T(8,128)}, u32[]{:S(2)}) copy-start(s32[128,32]{0,1:T(8,128)} %param.7) | copy-start | bytes 49156
  22.9 19.8 %all-to-all-start.1 = ((bf16[32,8,1152]{2,1,0:T(8,128)(2,1)}), bf16[32,8,1152]{2,1,0:T(8,128)(2,1)S(1)}, u32[]{:S(2)}, u32[]{:S(2)}) async-start(bf16[32,8,1152]{2,1,0:T(8,128)(2,1)} %bitcast.4), calls=%async_computation.1 | async-start | bytes 1179648 | tf_op jit(solution)/shard_map/all_to_all | solution.py:339
  26.8 3.2 %copy-start.2 = (bf16[128,2304]{1,0:T(8,128)(2,1)S(1)}, bf16[128,2304]{1,0:T(8,128)(2,1)}, u32[]{:S(2)}) copy-start(bf16[128,2304]{1,0:T(8,128)(2,1)} %q_ref) | copy-start | bytes 1769476
  29.3 0.7 copy-start.7
  30.0 13.0 %collective-permute-start = (bf16[128,2304]{1,0:T(8,128)(2,1)S(1)}, bf16[128,2304]{1,0:T(8,128)(2,1)S(1)}, u32[]{:S(2)}, u32[]{:S(2)}) collective-permute-start(bf16[128,2304]{1,0:T(8,128)(2,1)S(1)} %copy-done.2), channel_id=1, source_target_pairs={{0,1},{1,0},{2,3},{3,2},{4,5},{5,4},{6,7},{7,6},{8,9},{9,8},{10,11... | collective-permute-start | bytes 1769480 | tf_op jit(solution)/shard_map/ppermute | solution.py:369
  34.0 9.0 %collective-permute-start.1 = (bf16[128,2048]{1,0:T(8,128)(2,1)}, bf16[128,2048]{1,0:T(8,128)(2,1)S(1)}, u32[]{:S(2)}, u32[]{:S(2)}) collective-permute-start(bf16[128,2048]{1,0:T(8,128)(2,1)} %g_ref), channel_id=1, source_target_pairs={{0,1},{1,0},{2,3},{3,2},{4,5},{5,4},{6,7},{7,6},{8,9},{9,8},{10,11... | collective-permute-start | bytes 1572872 | tf_op jit(solution)/shard_map/ppermute | solution.py:370
  43.0 15.2 %collective-permute-start.2 = (bf16[144,1152]{1,0:T(8,128)(2,1)S(1)}, bf16[144,1152]{1,0:T(8,128)(2,1)S(1)}, u32[]{:S(2)}, u32[]{:S(2)}) collective-permute-start(bf16[144,1152]{1,0:T(8,128)(2,1)S(1)} %shard_map.63.own_ref), channel_id=1, source_target_pairs={{0,2},{1,3},{2,4},{3,5},{4,6},{5,7},{6,8},{7,9},{8,10},{9,11},{10,... | collective-permute-start | bytes 995336 | tf_op jit(solution)/shard_map/ppermute | solution.py:374
  47.0 12.6 %collective-permute-start.3 = (bf16[144,1152]{1,0:T(8,128)(2,1)S(1)}, bf16[144,1152]{1,0:T(8,128)(2,1)S(1)}, u32[]{:S(2)}, u32[]{:S(2)}) collective-permute-start(bf16[144,1152]{1,0:T(8,128)(2,1)S(1)} %shard_map.63.own_ref), channel_id=1, source_target_pairs={{0,14},{1,15},{2,0},{3,1},{4,2},{5,3},{6,4},{7,5},{8,6},{9,7},{10,... | collective-permute-start | bytes 995336 | tf_op jit(solution)/shard_map/ppermute | solution.py:375
  59.7 10.1 %collective-permute-start.4 = (bf16[144,1152]{1,0:T(8,128)(2,1)S(1)}, bf16[144,1152]{1,0:T(8,128)(2,1)S(1)}, u32[]{:S(2)}, u32[]{:S(2)}) collective-permute-start(bf16[144,1152]{1,0:T(8,128)(2,1)S(1)} %broadcast_select_fusion), channel_id=1, source_target_pairs={{0,2},{1,15},{2,4},{3,1},{4,6},{5,3},{6,8},{7,5},{8,10},{9,7},{10,... | collective-permute-start | bytes 995336 | tf_op jit(solution)/shard_map/ppermute | solution.py:377
  66.9 0.7 copy-start.5
  67.6 2.2 %copy-start.8 = (f32[288,128]{1,0:T(8,128)S(1)}, f32[288,128]{1,0:T(8,128)}, u32[]{:S(2)}) copy-start(f32[288,128]{1,0:T(8,128)} %copy-done.7) | copy-start | bytes 442372
  69.8 1.4 copy-start.9
  71.2 8.5 %collective-permute-start.5 = (f32[8,1024]{1,0:T(8,128)S(1)}, f32[8,1024]{1,0:T(8,128)S(1)}, u32[]{:S(2)}, u32[]{:S(2)}) collective-permute-start(f32[8,1024]{1,0:T(8,128)S(1)} %get-tuple-element.55.stat_ref), channel_id=1, source_target_pairs={{0,1},{1,0},{2,3},{3,2},{4,5},{5,4},{6,7},{7,6},{8,9},{9,8},{10,11... | collective-permute-start | bytes 98312 | tf_op jit(solution)/shard_map/ppermute | solution.py:433
  80.8 14.0 %collective-permute-start.9 = (bf16[144,1152]{1,0:T(8,128)(2,1)S(1)}, bf16[144,1152]{1,0:T(8,128)(2,1)S(1)}, u32[]{:S(2)}, u32[]{:S(2)}) collective-permute-start(bf16[144,1152]{1,0:T(8,128)(2,1)S(1)} %get-tuple-element.75), channel_id=1, source_target_pairs={{0,4},{1,13},{2,6},{3,15},{4,8},{5,1},{6,10},{7,3},{8,12},{9,5},{1... | collective-permute-start | bytes 995336 | tf_op jit(solution)/shard_map/ppermute | solution.py:452
  86.9 7.8 %copy-start.3 = (bf16[576,1024]{1,0:T(8,128)(2,1)}, bf16[576,1024]{1,0:T(8,128)(2,1)S(1)}, u32[]{:S(2)}) copy-start(bf16[576,1024]{1,0:T(8,128)(2,1)S(1)} %get-tuple-element.60.ds1_ref) | copy-start | bytes 3538948
  87.0 14.2 %collective-permute-start.7 = (bf16[144,1152]{1,0:T(8,128)(2,1)S(1)}, bf16[144,1152]{1,0:T(8,128)(2,1)S(1)}, u32[]{:S(2)}, u32[]{:S(2)}) collective-permute-start(bf16[144,1152]{1,0:T(8,128)(2,1)S(1)} %get-tuple-element.73), channel_id=1, source_target_pairs={{0,2},{1,3},{2,4},{3,5},{4,6},{5,7},{6,8},{7,9},{8,10},{9,11},{10,... | collective-permute-start | bytes 995336 | tf_op jit(solution)/shard_map/ppermute | solution.py:454
  89.5 11.7 %collective-permute-start.8 = (bf16[144,1152]{1,0:T(8,128)(2,1)S(1)}, bf16[144,1152]{1,0:T(8,128)(2,1)S(1)}, u32[]{:S(2)}, u32[]{:S(2)}) collective-permute-start(bf16[144,1152]{1,0:T(8,128)(2,1)S(1)} %get-tuple-element.74), channel_id=1, source_target_pairs={{0,14},{1,15},{2,0},{3,1},{4,2},{5,3},{6,4},{7,5},{8,6},{9,7},{10,... | collective-permute-start | bytes 995336 | tf_op jit(solution)/shard_map/ppermute | solution.py:455
  102.4 22.8 %all-to-all-start.2 = ((bf16[32,8,1152]{2,1,0:T(8,128)(2,1)}), bf16[32,8,1152]{2,1,0:T(8,128)(2,1)S(1)}, u32[]{:S(2)}, u32[]{:S(2)}) async-start(bf16[32,8,1152]{2,1,0:T(8,128)(2,1)} %bitcast.6), calls=%async_computation.2 | async-start | bytes 1179648 | tf_op jit(solution)/shard_map/all_to_all | solution.py:339
  107.5 1.3 copy-start.4
  108.8 1.0 copy-start.6
  109.8 1.1 copy-start.10
  115.0 17.9 %collective-permute-start.6 = (f32[256,1152]{1,0:T(8,128)}, f32[256,1152]{1,0:T(8,128)S(1)}, u32[]{:S(2)}, u32[]{:S(2)}) collective-permute-start(f32[256,1152]{1,0:T(8,128)} %get-tuple-element.68), channel_id=1, source_target_pairs={{0,1},{1,0},{2,3},{3,2},{4,5},{5,4},{6,7},{7,6},{8,9},{9,8},{10,11... | collective-permute-start | bytes 3538952 | tf_op jit(solution)/shard_map/ppermute | solution.py:470
  126.1 19.1 %all-to-all-start.3 = ((bf16[16,8,1152]{2,1,0:T(8,128)(2,1)}), bf16[16,8,1152]{2,1,0:T(8,128)(2,1)S(1)}, u32[]{:S(2)}, u32[]{:S(2)}) async-start(bf16[16,8,1152]{2,1,0:T(8,128)(2,1)} %bitcast.8), calls=%async_computation.3 | async-start | bytes 589824 | tf_op jit(solution)/shard_map/all_to_all | solution.py:339
